TPU v7x, 32 devices: a whole 2x2x4 slice. The times are simulated.
32 devices in a mesh: circ: 8 (over z, core), span: 4 (over y, x).
Axes of the slice: x: 2, y: 2, z: 4, core: 2. Of those that a mesh axis runs over, the one named last changes fastest.
Arguments:
- adjoint_rotor: float32 [6, 8, 4, 2048], P(None, 'span', None, 'circ'), may hold values from -6 to 6
- adjoint_stator: float32 [6, 8, 4, 2048], P(None, 'span', None, 'circ'), may hold values from -6 to 6
- jac_diag_rotor: float32 [6, 8, 4, 2048], P(None, 'span', None, 'circ'), may hold values from 2 to 4
- jac_diag_stator: float32 [6, 8, 4, 2048], P(None, 'span', None, 'circ'), may hold values from 2 to 4
- jac_off_rotor: bfloat16 [6, 6, 8, 4, 2048], P(None, None, 'span', None, 'circ'), may hold values from -1 to 1
- jac_off_stator: bfloat16 [6, 6, 8, 4, 2048], P(None, None, 'span', None, 'circ'), may hold values from -1 to 1
- source_rotor: float32 [6, 8, 4, 2048], P(None, 'span', None, 'circ'), may hold values from -6 to 6
- source_stator: float32 [6, 8, 4, 2048], P(None, 'span', None, 'circ'), may hold values from -6 to 6
- rotor_state: bfloat16 [6, 8, 2048], P(None, 'span', 'circ'), may hold values from -6 to 6
- margin_block: int32 [8, 16, 4], P('span'), may hold values from 0 to 15, as said below
- face_count: int32 [8, 16], P('span'), may hold values from 1 to 4
- margin_weight: float32 [8, 16, 4, 128], P('span'), may hold values from 0.2 to 1
Outputs:
- rotor_adjoint: float32 [6, 8, 4, 2048], P(None, 'span', None, 'circ')
- stator_adjoint: float32 [6, 8, 4, 2048], P(None, 'span', None, 'circ')
Inputs may be any that keep to these rules, and one draw needn't show every extreme that they name: `margin_block`: entry k of the list of stator block b in spanwise row s is rotor block (b + o + 2 * 2 * s + 1 + j + k) mod 16, with one o for the whole array and j from 0 to 2 for each block of each row.
All inputs are finite; a program needn't handle non-finite values.
Results may differ from a plain program's by a relative error of at most 0.00055.
Values may be sent and summed in bfloat16 or wider, within the bound.
No kernel may reach another device: no remote copies, remote signals or barrier semaphores. Data moves between devices by JAX's collectives and lax.ppermute only.
A program may use at most 64 MiB of HBM per device.

v0:
```python
import functools

import jax
import jax.numpy as jnp
from jax import lax
from jax.experimental import pallas as pl
from jax.experimental.pallas import tpu as pltpu
from jax.sharding import PartitionSpec as P

step_size = 0.1
coupling = 0.2
carry = step_size * coupling
REACH = 8
TILE = 128
f32 = jnp.float32
params = pltpu.CompilerParams(vmem_limit_bytes=24 * 1024 * 1024)


def iota(shape, dim):
    return lax.broadcasted_iota(jnp.int32, shape, dim)


def wrapped(x, count):
    if count & (count - 1) == 0:
        return jnp.bitwise_and(x, count - 1)
    return lax.rem(x + 4 * count, count)


def lanes_apart(x):
    cells = x.shape[1]
    lane = iota(x.shape, 1)
    before = jnp.where(lane == 0, 0.0, pltpu.roll(x, 1, 1))
    after = jnp.where(lane == cells - 1, 0.0, pltpu.roll(x, cells - 1, 1))
    return before + after


def layers_apart(x):
    return pltpu.roll(x, 1, 0) + pltpu.roll(x, 7, 0)


def edge_pick(row, cells):
    at = iota((8, cells), 0)
    lane = iota((8, cells), 1)
    first = jnp.logical_and(at == row, lane == 0)
    last = jnp.logical_and(at == 4 + row, lane == cells - 1)
    return jnp.where(jnp.logical_or(first, last), 1.0, 0.0).astype(f32)


def split(x):
    high = x.astype(jnp.bfloat16).astype(f32)
    return high, x - high


def flux_of(primal, adjoint):
    speeds = jnp.sqrt(1.0 + primal * primal)
    over = jnp.sum(primal * adjoint, axis=0, keepdims=True)
    under = 6.0 + jnp.sum(primal * primal, axis=0, keepdims=True)
    return speeds * adjoint + 0.5 * primal * (over / under)


def jacobian_row(diag, off, state, v, s, var_count):
    total = diag[v, s] * state[v]
    for w in range(var_count):
        total = total + off[w, v, s].astype(f32) * state[w]
    return total


def pull_row(flux, weights, margin, count, s, slot, first_block, base, total):
    target = wrapped(first_block + slot + total, total)
    acc = jnp.zeros((8, TILE), f32)
    for e in range(REACH):
        b = wrapped(base + slot + e, total)
        k = wrapped(target - margin[s, 0, b] + total, total)
        live = jnp.where(k < count[s, b], 1.0, 0.0).astype(f32)
        kept = jnp.minimum(k, weights.shape[2] - 1)
        acc = acc + (weights[s, b, pl.ds(kept, 1), :] * live) * flux(slot + e)
    return acc


def first_kernel(*refs):
    outer, refs = refs[:12], refs[12:]
    v_r, v_s, out, a_r, a_s, weights, margin, count = refs[:8]
    jd_r, jd_s, jo_r, jo_s, src_r, src_s, state = refs[8:15]
    xs, sems, wide_out = refs[15:19], refs[19], refs[20]
    var_count, rows, layers, cells = a_r.shape
    own_blocks = cells // TILE
    inner = (a_r, a_s, jd_r, jd_s, jo_r, jo_s, src_r, src_s, state, margin, count, weights)
    copies = [pltpu.make_async_copy(x, y, sems.at[n]) for n, (x, y) in enumerate(zip(outer, inner))]
    for copy in copies:
        copy.start()
    wide_out[...] = jnp.zeros(wide_out.shape, f32)
    for x in xs:
        x[...] = jnp.zeros(x.shape, f32)
    for copy in copies:
        copy.wait()
    fields = ((a_r, jd_r, jo_r, src_r, v_r, xs[0], xs[2]), (a_s, jd_s, jo_s, src_s, v_s, xs[1], xs[3]))
    for a, jd, jo, src, partial, x_a, x_p in fields:
        for v in range(var_count):
            for s in range(rows):
                x_a[v * rows + s, 0:layers, :] = a[v, s]
        for s in range(rows):
            state_row = [a[v, s] for v in range(var_count)]
            for v in range(var_count):
                wide = x_a[v * rows + s]
                beside = (lanes_apart(wide) + layers_apart(wide))[0:layers]
                if s > 0:
                    beside = beside + a[v, s - 1]
                if s < rows - 1:
                    beside = beside + a[v, s + 1]
                res = jacobian_row(jd, jo, state_row, v, s, var_count) - coupling * beside - src[v, s]
                new = state_row[v] - step_size * res
                partial[v, s] = new
                x_p[v * rows + s, 0:layers, :] = new
    edges = jnp.zeros((8, TILE), f32)
    for q in range(4):
        flat = xs[q][...].reshape(TILE, cells)
        edges = edges + lax.dot_general(
            edge_pick(q, cells), flat, (((1,), (1,)), ((), ())), preferred_element_type=f32
        )
    for v in range(var_count):
        rotor = state[v].astype(f32)
        for s in range(rows):
            for i in range(own_blocks):
                cut = slice(i * TILE, (i + 1) * TILE)
                wide_out[i, s, v : v + 1, :] = rotor[s : s + 1, cut]
                wide_out[i, rows + s, v : v + 1, :] = a_s[v, s, 0:1, cut]
                wide_out[i, 2 * rows + s, v : v + 1, :] = v_s[v, s, 0:1, cut]
    row8 = iota((8, TILE), 0)
    filled = row8 < var_count
    for i in range(own_blocks):
        if i in (0, own_blocks - 1):
            side = 4 if i else 0
            for s in range(rows):
                wide_out[i, 2 * rows + s, 6:8, :] = edges[side + 2 * s : side + 2 * s + 2]
        groups = []
        for s in range(rows):
            p_high, p_rest = split(wide_out[i, rows + s])
            u_high, u_rest = split(wide_out[i, 2 * rows + s])
            groups.append((
                jnp.where(filled, wide_out[i, s], pltpu.roll(u_rest, 6, 0)),
                jnp.where(filled, p_high, pltpu.roll(u_rest, 4, 0)),
                jnp.where(filled, p_rest, pltpu.roll(u_rest, 2, 0)),
                u_high,
            ))
        for n in range(4):
            out[i, n * 16 : n * 16 + 16, :] = jnp.concatenate([x[n] for x in groups], axis=0).astype(jnp.bfloat16)


def second_kernel(
    masks, mine, other, v_r, v_s, a_r, a_s, weights, margin, count,
    o_r, o_s, h_r, h_s, q_out, p_out, outer, inner, flux, held, spot, g,
):
    var_count, rows, layers, cells = a_r.shape
    total = 2 * mine.shape[0]
    own_blocks = cells // TILE
    entries = weights.shape[2]
    spread = REACH + own_blocks + 1
    first_block = lax.axis_index("circ") * own_blocks
    row8 = iota((8, TILE), 0)
    lane = iota((8, TILE), 1)
    lane_all = iota((layers, cells), 1)
    layer_all = iota((layers, cells), 0)
    edge = jnp.logical_or(lane_all == 0, lane_all == cells - 1)
    left = wrapped(first_block - 1 + total, total)
    right = wrapped(first_block + own_blocks, total)

    filled = row8 < var_count
    here = lax.axis_index("circ")
    for at in range(total):
        half, part = divmod(at, total // 2)
        place, i = divmod(part, own_blocks)
        mask = half + sum(m for n, m in enumerate(masks) if place >> n & 1)
        b = jnp.bitwise_xor(here, mask) * own_blocks + i
        whole = other if half else mine
        tiles = [whole[part, n * 16 : n * 16 + 16, :].astype(f32) for n in range(4)]
        for s in range(rows):
            rotor, p_high, p_rest, u_high = [x[s * 8 : s * 8 + 8] for x in tiles]
            u_rest = jnp.where(
                row8 < 2, pltpu.roll(rotor, 2, 0), jnp.where(row8 < 4, pltpu.roll(p_high, 4, 0), pltpu.roll(p_rest, 6, 0))
            )
            g[b, s] = rotor
            g[b, rows + s] = p_high + p_rest
            g[b, 2 * rows + s] = u_high + jnp.where(filled, u_rest, 0.0)
    spot[0:2, :] = g[left, 2 * rows, 6:8, :]
    spot[2:4, :] = g[left, 2 * rows + 1, 6:8, :]
    spot[4:6, :] = g[right, 2 * rows, 6:8, :]
    spot[6:8, :] = g[right, 2 * rows + 1, 6:8, :]
    spots = spot[...]
    columns = [
        lax.dot_general(spots, edge_pick(q, cells), (((0,), (0,)), ((), ())), preferred_element_type=f32)
        for q in range(4)
    ]

    def block(s, b):
        primal = jnp.zeros((8, TILE), f32)
        for k in range(entries):
            live = jnp.where(k < count[s, b], 1.0, 0.0).astype(f32)
            primal = primal + (weights[s, b, k : k + 1, :] * live) * g[margin[s, k, b], s]
        primal = jnp.where(filled, primal, 0.0)
        adjoint = g[b, rows + s]
        return primal, flux_of(primal, adjoint)

    def advanced(s, b, moved):
        place = lax.rem(b, own_blocks)
        before = jnp.where(place == 0, carry, 0.0).astype(f32)
        after = jnp.where(place == own_blocks - 1, carry, 0.0).astype(f32)
        low = pltpu.roll(g[wrapped(b - 1 + total, total), rows + s], 1, 1)
        high = pltpu.roll(g[wrapped(b + 1, total), rows + s], TILE - 1, 1)
        base = g[b, 2 * rows + s]
        base = base + jnp.where(lane == 0, low * before, 0.0) + jnp.where(lane == TILE - 1, high * after, 0.0)
        return base - step_size * moved

    for s in range(rows):
        base = first_block - margin[s, 0, 0] - 5 + 4 * total
        for t in range(spread):
            b = wrapped(base - 1 + t, total)
            primal, moved = block(s, b)
            flux[s, t] = moved.astype(jnp.bfloat16).astype(f32)
            if 0 < t < spread - 1:
                q_out[s, t - 1] = primal
                p_out[s, t - 1] = advanced(s, b, moved)
        own = []
        for i in range(own_blocks):
            primal, moved = block(s, first_block + i)
            own.append(moved)
            q_out[s, spread - 2 + i] = primal
            p_out[s, spread - 2 + i] = advanced(s, first_block + i, moved)
        blank = [jnp.zeros((8, TILE), f32)] * (own_blocks - 2)
        side_flux = [block(s, left)[1], block(s, right)[1]]
        pulls = [
            pull_row(lambda t: flux[s, t + 1], weights, margin, count, s, slot, first_block, base, total)
            for slot in range(-1, own_blocks + 1)
        ]

        def at_sides(low, high):
            return jnp.concatenate([pltpu.roll(low, 1, 1), *blank, pltpu.roll(high, TILE - 1, 1)], axis=1)

        pulled = step_size * jnp.concatenate(pulls[1:-1], axis=1)
        pulled_side = step_size * at_sides(pulls[0], pulls[-1])
        pushed = step_size * jnp.concatenate(own, axis=1)
        pushed_side = step_size * at_sides(*side_flux)
        for v in range(var_count):
            at = (v * rows + s) * 8
            cut = slice(at, at + layers)
            o_r[v, s] = (
                v_r[v, s] + carry * columns[0][cut] + jnp.where(layer_all == layers - 1, pulled[v : v + 1], 0.0)
            )
            o_s[v, s] = v_s[v, s] + carry * columns[1][cut] - jnp.where(layer_all == 0, pushed[v : v + 1], 0.0)
            h_r[v, s] = columns[2][cut] + jnp.where(
                edge, carry * a_r[v, s] + jnp.where(layer_all == layers - 1, pulled_side[v : v + 1], 0.0), 0.0
            )
            h_s[v, s] = columns[3][cut] + jnp.where(
                edge, carry * a_s[v, s] - jnp.where(layer_all == 0, pushed_side[v : v + 1], 0.0), 0.0
            )

    last = jnp.concatenate([spots, jnp.ones((8, TILE), f32)], axis=0).astype(jnp.bfloat16)
    odd = jnp.bitwise_and(lax.axis_index("span"), 1)
    for to, s in ((inner, (1 - odd) * (rows - 1)), (outer, odd * (rows - 1))):
        for j in range(total // 2):
            to[j] = jnp.concatenate([g[2 * j, rows + s], g[2 * j + 1, rows + s]], axis=0).astype(jnp.bfloat16)
        for v in range(var_count):
            for n, ref in enumerate((a_r, a_s, o_r, o_s)):
                held[v, n * layers : (n + 1) * layers, :] = ref[v, s]
            for i in range(own_blocks):
                to[total // 2 + v * own_blocks + i] = held[v, :, i * TILE : (i + 1) * TILE].astype(jnp.bfloat16)
        to[total // 2 + var_count * own_blocks] = last


def third_kernel(
    outer, inner, o_r, o_s, h_r, h_s, q, p, a_r, a_s, jd_r, jd_s, jo_r, jo_s, src_r, src_s, weights, margin, count,
    out_r, out_s, flux, x_r, x_s, rows_low, rows_high,
):
    var_count, rows, layers, cells = a_r.shape
    total = weights.shape[1]
    own_blocks = cells // TILE
    spread = REACH + own_blocks + 1
    first_block = lax.axis_index("circ") * own_blocks
    lane = iota((8, TILE), 1)
    layer_all = iota((layers, cells), 0)
    end = total // 2 + var_count * own_blocks
    for x in (x_r, x_s):
        x[...] = jnp.zeros(x.shape, f32)
    odd = jnp.bitwise_and(lax.axis_index("span"), 1) == 1

    def low(n):
        return jnp.where(odd, inner[n].astype(f32), outer[n].astype(f32))

    def high(n):
        return jnp.where(odd, outer[n].astype(f32), inner[n].astype(f32))

    for side, to in ((low, rows_low), (high, rows_high)):
        for v in range(var_count):
            for i in range(own_blocks):
                to[v, :, i * TILE : (i + 1) * TILE] = side(total // 2 + v * own_blocks + i)
    ends = [low(end), high(end)]
    inside = [jnp.concatenate([x[8:9]] * own_blocks, axis=1) for x in ends]
    group = lax.rem(lax.shift_right_logical(lane, 3), rows)
    corner = jnp.where(group == 0, pltpu.roll(ends[0][0:8], (TILE - 8 * (rows - 1)) % TILE, 1), 0.0)
    corner = corner + jnp.where(group == rows - 1, pltpu.roll(ends[1][0:8], 8 * (rows - 1), 1), 0.0)
    columns = [
        lax.dot_general(corner, edge_pick(n, cells), (((0,), (0,)), ((), ())), preferred_element_type=f32)
        for n in range(2)
    ]

    def halo(side, b):
        both = side(lax.shift_right_logical(b, 1))
        return jnp.where(jnp.bitwise_and(b, 1) == 1, both[8:16], both[0:8])

    extra = []
    for s in range(rows):
        base = first_block - margin[s, 0, 0] - 5 + 4 * total
        own = []
        for t in range(spread - 2 + own_blocks):
            b = wrapped(base + t, total) if t < spread - 2 else first_block + t - (spread - 2)
            adjoint = p[s, t]
            if s == 0:
                adjoint = adjoint + carry * halo(low, b)
            if s == rows - 1:
                adjoint = adjoint + carry * halo(high, b)
            moved = flux_of(q[s, t], adjoint)
            if t < spread - 2:
                flux[s, t] = moved.astype(jnp.bfloat16).astype(f32)
            else:
                own.append(moved)
        pulls = [
            pull_row(lambda t: flux[s, t], weights, margin, count, s, slot, first_block, base, total)
            for slot in range(own_blocks)
        ]
        extra.append((step_size * jnp.concatenate(pulls, axis=1), -step_size * jnp.concatenate(own, axis=1)))

    fields = (
        (o_r, h_r, a_r, jd_r, jo_r, src_r, x_r, out_r, layers - 1),
        (o_s, h_s, a_s, jd_s, jo_s, src_s, x_s, out_s, 0),
    )
    for n, (o, h, a, jd, jo, src, x, out, layer) in enumerate(fields):
        old = slice(n * layers, (n + 1) * layers)
        new = slice((2 + n) * layers, (3 + n) * layers)
        for v in range(var_count):
            for s in range(rows):
                value = o[v, s]
                if s == 0:
                    value = value + carry * rows_low[v, old, :]
                if s == rows - 1:
                    value = value + carry * rows_high[v, old, :]
                x[v * rows + s, 0:layers, :] = value
        for s in range(rows):
            state_row = [x[v * rows + s, 0:layers, :] for v in range(var_count)]
            for v in range(var_count):
                wide = x[v * rows + s]
                beside = (lanes_apart(wide) + layers_apart(wide))[0:layers]
                at = (v * rows + s) * 8
                beside = beside + h[v, s] + carry * columns[n][at : at + layers]
                if s > 0:
                    beside = beside + x[v * rows + s - 1, 0:layers, :]
                else:
                    beside = beside + inside[0] * (rows_low[v, new, :] + carry * a[v, 0])
                if s < rows - 1:
                    beside = beside + x[v * rows + s + 1, 0:layers, :]
                else:
                    beside = beside + inside[1] * (rows_high[v, new, :] + carry * a[v, rows - 1])
                res = jacobian_row(jd, jo, state_row, v, s, var_count) - coupling * beside - src[v, s]
                out[v, s] = (
                    state_row[v] - step_size * res + jnp.where(layer_all == layer, extra[s][n][v : v + 1], 0.0)
                )


def per_device(
    adjoint_rotor,
    adjoint_stator,
    jac_diag_rotor,
    jac_diag_stator,
    jac_off_rotor,
    jac_off_stator,
    source_rotor,
    source_stator,
    rotor_state,
    margin_block,
    face_count,
    margin_weight,
):
    var_count, rows, layers, cells = adjoint_rotor.shape
    own_blocks = cells // TILE
    total = margin_block.shape[1]
    spread = REACH + own_blocks + 1
    field = jax.ShapeDtypeStruct(adjoint_rotor.shape, f32)
    vmem = pl.BlockSpec(memory_space=pltpu.VMEM)
    smem = pl.BlockSpec(memory_space=pltpu.SMEM)
    padded = pltpu.VMEM((TILE // 8, 8, cells), f32)

    margin = jnp.swapaxes(margin_block, 1, 2)
    arguments = (
        adjoint_rotor, adjoint_stator, jac_diag_rotor, jac_diag_stator, jac_off_rotor, jac_off_stator,
        source_rotor, source_stator, rotor_state, margin, face_count, margin_weight,
    )
    shapes = [jax.ShapeDtypeStruct(x.shape, x.dtype) for x in arguments]
    v_r, v_s, share, a_r, a_s, weights, margin, count = pl.pallas_call(
        first_kernel,
        out_shape=(
            field, field, jax.ShapeDtypeStruct((own_blocks, 64, TILE), jnp.bfloat16),
            shapes[0], shapes[1], shapes[11], shapes[9], shapes[10],
        ),
        in_specs=[pl.BlockSpec(memory_space=pltpu.HBM)] * 12,
        out_specs=(vmem,) * 8,
        scratch_shapes=[pltpu.VMEM(x.shape, x.dtype) for x in shapes[2:9]]
        + [padded] * 4
        + [pltpu.SemaphoreType.DMA((12,)), pltpu.VMEM((own_blocks, 3 * rows, 8, TILE), f32)],
        compiler_params=params,
        name="local_part",
    )(*[pltpu.with_memory_space_constraint(x, pltpu.HBM) for x in arguments])
    members = lax.axis_size("circ")
    mine, masks = share, []
    mask = members // 2
    while mask > 0:
        other = lax.ppermute(mine, "circ", [(i, i ^ mask) for i in range(members)])
        if mask > 1:
            mine = jnp.concatenate([mine, other], axis=0)
            masks.append(mask)
        mask //= 2
    tiles = jax.ShapeDtypeStruct((total // 2 + var_count * own_blocks + 1, 16, TILE), jnp.bfloat16)
    listed = jax.ShapeDtypeStruct((rows, spread - 2 + own_blocks, 8, TILE), f32)
    o_r, o_s, h_r, h_s, q, p, outer, inner = pl.pallas_call(
        functools.partial(second_kernel, masks),
        out_shape=(field, field, field, field, listed, listed, tiles, tiles),
        in_specs=[vmem] * 7 + [smem] * 2,
        out_specs=(vmem,) * 8,
        scratch_shapes=[
            pltpu.VMEM((rows, spread, 8, TILE), f32),
            pltpu.VMEM((var_count, 4 * layers, cells), f32),
            pltpu.VMEM((8, TILE), f32),
            pltpu.VMEM((total, 3 * rows, 8, TILE), f32),
        ],
        compiler_params=params,
        name="interface_part",
    )(mine, other, v_r, v_s, a_r, a_s, weights, margin, count)
    bands = lax.axis_size("span")
    near = [(i, i ^ 1) for i in range(bands)]
    far = [pair for i in range(1, bands - 1, 2) for pair in ((i, i + 1), (i + 1, i))]
    outer = lax.ppermute(outer, "span", far)
    inner = lax.ppermute(inner, "span", near)
    out_r, out_s = pl.pallas_call(
        third_kernel,
        out_shape=(field, field),
        in_specs=[vmem] * 17 + [smem] * 2,
        out_specs=(vmem,) * 2,
        scratch_shapes=[
            pltpu.VMEM((rows, spread - 2, 8, TILE), f32),
            padded,
            padded,
            pltpu.VMEM((var_count, 4 * layers, cells), f32),
            pltpu.VMEM((var_count, 4 * layers, cells), f32),
        ],
        compiler_params=params,
        name="final_part",
    )(
        outer, inner, o_r, o_s, h_r, h_s, q, p, a_r, a_s, jac_diag_rotor, jac_diag_stator,
        jac_off_rotor, jac_off_stator, source_rotor, source_stator, weights, margin, count,
    )
    return (out_r, out_s)


def solution(mesh):
    field = P(None, "span", None, "circ")
    placed = (
        (field,) * 4
        + (P(None, None, "span", None, "circ"),) * 2
        + (field,) * 2
        + (P(None, "span", "circ"), P("span", None, None), P("span", None), P("span", None, None, None))
    )
    return jax.shard_map(
        per_device, mesh=mesh, in_specs=placed, out_specs=(field, field), check_vma=False
    )
```

profile of v0, /device:TPU:0, one launch (start us, length us, event | category | flops | bytes accessed | tf_op | source)
XLA Modules:
  0.0 27.4 jit_solution(13297661798181577654)
XLA Ops:
  0.6 1.6 %local_part.1 = (f32[6,2,4,256]{3,2,1,0:T(4,128)S(1)}, f32[6,2,4,256]{3,2,1,0:T(4,128)S(1)}, bf16[2,64,128]{2,1,0:T(8,128)(2,1)S(1)}, f32[6,2,4,256]{3,2,1,0:T(4...) custom-call(f32[6,2,4,256]{3,2,1,0:T(4,128)} %refs_0_.1, ...), custom_call_target="tpu_custom_call" | custom-call | tf_op jit(solution)/shard_map/local_part/pallas_call | solution.py:396
  2.3 4.1 %collective-permute-start = (bf16[2,64,128]{2,1,0:T(8,128)(2,1)S(1)}, bf16[2,64,128]{2,1,0:T(8,128)(2,1)S(1)}, u32[]{:S(2)}, u32[]{:S(2)}) collective-permute-start(bf16[2,64,128]{2,1,0:T(8,128)(2,1)S(1)} %get-tuple-element.18), channel_id=1, source_target_pairs={{0,16},{4,20},{8,24},{12,28},{16,0},{20,4},{24,8},{28,12},{1,17},{... | collective-permute-start | bytes 98312 | tf_op jit(solution)/shard_map/ppermute | solution.py:414
  6.4 2.2 %collective-permute-done = bf16[2,64,128]{2,1,0:T(8,128)(2,1)S(1)} collective-permute-done((bf16[2,64,128]{2,1,0:T(8,128)(2,1)S(1)}, bf16[2,64,128]{2,1,0:T(8,128)(2,1)S(1)}, u32[]{:S(2)}, u32[]{:S(2)}) %collective-permute-start) | collective-permute-done | bytes 32800 | tf_op jit(solution)/shard_map/ppermute | solution.py:414
  8.6 1.6 %collective-permute-start.1 = (bf16[4,64,128]{2,1,0:T(8,128)(2,1)S(1)}, bf16[4,64,128]{2,1,0:T(8,128)(2,1)S(1)}, u32[]{:S(2)}, u32[]{:S(2)}) collective-permute-start(bf16[4,64,128]{2,1,0:T(8,128)(2,1)S(1)} %pad_maximum_fusion), channel_id=1, source_target_pairs={{0,8},{4,12},{8,0},{12,4},{16,24},{20,28},{24,16},{28,20},{1,9},{5... | collective-permute-start | bytes 196616 | tf_op jit(solution)/shard_map/ppermute | solution.py:414
  10.3 2.7 %collective-permute-done.1 = bf16[4,64,128]{2,1,0:T(8,128)(2,1)S(1)} collective-permute-done((bf16[4,64,128]{2,1,0:T(8,128)(2,1)S(1)}, bf16[4,64,128]{2,1,0:T(8,128)(2,1)S(1)}, u32[]{:S(2)}, u32[]{:S(2)}) %collective-permute-start.1) | collective-permute-done | bytes 65568 | tf_op jit(solution)/shard_map/ppermute | solution.py:414
  13.0 0.1 collective-permute-start.2
  13.1 1.3 %collective-permute-done.2.other = bf16[8,64,128]{2,1,0:T(8,128)(2,1)S(1)} collective-permute-done((bf16[8,64,128]{2,1,0:T(8,128)(2,1)S(1)}, bf16[8,64,128]{2,1,0:T(8,128)(2,1)S(1)}, u32[]{:S(2)}, u32[]{:S(2)}) %collective-permute-start.2) | collective-permute-done | bytes 131104 | tf_op jit(solution)/shard_map/ppermute | solution.py:414
  14.4 0.0 copy-start
  14.4 0.0 copy-start.1
  14.4 0.0 copy-start.2
  14.4 0.0 copy-start.3
  14.4 0.0 copy-start.4
  14.4 0.0 copy-start.5
  14.4 1.5 %interface_part.1 = (f32[6,2,4,256]{3,2,1,0:T(4,128)S(1)}, f32[6,2,4,256]{3,2,1,0:T(4,128)S(1)}, f32[6,2,4,256]{3,2,1,0:T(4,128)S(1)}, f32[6,2,4,256]{3,2,1,0:T(...) custom-call(bf16[8,64,128]{2,1,0:T(8,128)(2,1)S(1)} %constant_dynami, ...), custom_call_target="tpu_custom_call" | custom-call | tf_op jit(solution)/shard_map/interface_part/pallas_call | solution.py:421
  16.0 0.7 %collective-permute-start.3 = (bf16[21,16,128]{2,1,0:T(8,128)(2,1)S(1)}, bf16[21,16,128]{2,1,0:T(8,128)(2,1)S(1)}, u32[]{:S(2)}, u32[]{:S(2)}) collective-permute-start(bf16[21,16,128]{2,1,0:T(8,128)(2,1)S(1)} %get-tuple-element.26), channel_id=1, source_target_pairs={{1,2},{2,1},{5,6},{6,5},{9,10},{10,9},{13,14},{14,13},{17,18},{18,... | collective-permute-start | bytes 258056 | tf_op jit(solution)/shard_map/ppermute | solution.py:438
  16.6 4.5 %collective-permute-start.4 = (bf16[21,16,128]{2,1,0:T(8,128)(2,1)S(1)}, bf16[21,16,128]{2,1,0:T(8,128)(2,1)S(1)}, u32[]{:S(2)}, u32[]{:S(2)}) collective-permute-start(bf16[21,16,128]{2,1,0:T(8,128)(2,1)S(1)} %get-tuple-element.27), channel_id=1, source_target_pairs={{0,1},{1,0},{2,3},{3,2},{4,5},{5,4},{6,7},{7,6},{8,9},{9,8},{10,11... | collective-permute-start | bytes 258056 | tf_op jit(solution)/shard_map/ppermute | solution.py:439
  21.1 0.0 collective-permute-done.3.outer
  21.1 4.3 %collective-permute-done.4.inner = bf16[21,16,128]{2,1,0:T(8,128)(2,1)S(1)} collective-permute-done((bf16[21,16,128]{2,1,0:T(8,128)(2,1)S(1)}, bf16[21,16,128]{2,1,0:T(8,128)(2,1)S(1)}, u32[]{:S(2)}, u32[]{:S(2)}) %collective-permute-start.4) | collective-permute-done | bytes 86048 | tf_op jit(solution)/shard_map/ppermute | solution.py:439
  25.4 0.0 copy-done
  25.4 0.0 copy-done.1
  25.4 0.0 copy-done.2
  25.5 0.0 copy-done.3
  25.5 0.0 copy-done.4
  25.5 0.0 copy-done.5
  25.5 1.9 %final_part.1 = (f32[6,2,4,256]{3,2,1,0:T(4,128)}, f32[6,2,4,256]{3,2,1,0:T(4,128)}) custom-call(bf16[21,16,128]{2,1,0:T(8,128)(2,1)S(1)} %collective-permute-done.3.outer, bf16[21,16,128]{2,1,0:T(8,128)(2,1)S(1)} %collective-permute-done.4.inner, f32[6,2,4,256]{3,2,1,0:T(4,128)S(1)} %get-tuple-element.28.o_r, f32[6,2,4,256]{3,2,1,0:T(4,128)S(1)} %get-tuple-element.29.o_s, ...), custom_call_target="tpu_custom_call" | custom-call | tf_op jit(solution)/shard_map/final_part/pallas_call | solution.py:440
  (4 shorter events, 0.0 us)
Async XLA Ops:
  2.3 6.3 %collective-permute-start = (bf16[2,64,128]{2,1,0:T(8,128)(2,1)S(1)}, bf16[2,64,128]{2,1,0:T(8,128)(2,1)S(1)}, u32[]{:S(2)}, u32[]{:S(2)}) collective-permute-start(bf16[2,64,128]{2,1,0:T(8,128)(2,1)S(1)} %get-tuple-element.18), channel_id=1, source_target_pairs={{0,16},{4,20},{8,24},{12,28},{16,0},{20,4},{24,8},{28,12},{1,17},{... | collective-permute-start | bytes 98312 | tf_op jit(solution)/shard_map/ppermute | solution.py:414
  8.6 4.3 %collective-permute-start.1 = (bf16[4,64,128]{2,1,0:T(8,128)(2,1)S(1)}, bf16[4,64,128]{2,1,0:T(8,128)(2,1)S(1)}, u32[]{:S(2)}, u32[]{:S(2)}) collective-permute-start(bf16[4,64,128]{2,1,0:T(8,128)(2,1)S(1)} %pad_maximum_fusion), channel_id=1, source_target_pairs={{0,8},{4,12},{8,0},{12,4},{16,24},{20,28},{24,16},{28,20},{1,9},{5... | collective-permute-start | bytes 196616 | tf_op jit(solution)/shard_map/ppermute | solution.py:414
  13.0 1.4 %collective-permute-start.2 = (bf16[8,64,128]{2,1,0:T(8,128)(2,1)S(1)}, bf16[8,64,128]{2,1,0:T(8,128)(2,1)S(1)}, u32[]{:S(2)}, u32[]{:S(2)}) collective-permute-start(bf16[8,64,128]{2,1,0:T(8,128)(2,1)S(1)} %constant_dynamic-update-slice_fusion.mine), channel_id=1, source_target_pairs={{0,4},{4,0},{8,12},{12,8},{16,20},{20,16},{24,28},{28,24},{1,5},{5... | collective-permute-start | bytes 393224 | tf_op jit(solution)/shard_map/ppermute | solution.py:414
  14.4 11.1 %copy-start = (bf16[6,6,2,4,256]{4,3,2,1,0:T(4,128)(2,1)S(1)}, bf16[6,6,2,4,256]{4,3,2,1,0:T(4,128)(2,1)}, u32[]{:S(2)}) copy-start(bf16[6,6,2,4,256]{4,3,2,1,0:T(4,128)(2,1)} %jo_r.1) | copy-start | bytes 442372
  14.4 11.1 %copy-start.1 = (bf16[6,6,2,4,256]{4,3,2,1,0:T(4,128)(2,1)S(1)}, bf16[6,6,2,4,256]{4,3,2,1,0:T(4,128)(2,1)}, u32[]{:S(2)}) copy-start(bf16[6,6,2,4,256]{4,3,2,1,0:T(4,128)(2,1)} %jo_s.1) | copy-start | bytes 442372
  14.4 11.1 %copy-start.2 = (f32[6,2,4,256]{3,2,1,0:T(4,128)S(1)}, f32[6,2,4,256]{3,2,1,0:T(4,128)}, u32[]{:S(2)}) copy-start(f32[6,2,4,256]{3,2,1,0:T(4,128)} %jd_r.1) | copy-start | bytes 147460
  14.4 11.1 %copy-start.3 = (f32[6,2,4,256]{3,2,1,0:T(4,128)S(1)}, f32[6,2,4,256]{3,2,1,0:T(4,128)}, u32[]{:S(2)}) copy-start(f32[6,2,4,256]{3,2,1,0:T(4,128)} %jd_s.1) | copy-start | bytes 147460
  14.4 11.1 %copy-start.4 = (f32[6,2,4,256]{3,2,1,0:T(4,128)S(1)}, f32[6,2,4,256]{3,2,1,0:T(4,128)}, u32[]{:S(2)}) copy-start(f32[6,2,4,256]{3,2,1,0:T(4,128)} %src_r.1) | copy-start | bytes 147460
  14.4 11.1 %copy-start.5 = (f32[6,2,4,256]{3,2,1,0:T(4,128)S(1)}, f32[6,2,4,256]{3,2,1,0:T(4,128)}, u32[]{:S(2)}) copy-start(f32[6,2,4,256]{3,2,1,0:T(4,128)} %src_s.1) | copy-start | bytes 147460
  16.0 5.2 %collective-permute-start.3 = (bf16[21,16,128]{2,1,0:T(8,128)(2,1)S(1)}, bf16[21,16,128]{2,1,0:T(8,128)(2,1)S(1)}, u32[]{:S(2)}, u32[]{:S(2)}) collective-permute-start(bf16[21,16,128]{2,1,0:T(8,128)(2,1)S(1)} %get-tuple-element.26), channel_id=1, source_target_pairs={{1,2},{2,1},{5,6},{6,5},{9,10},{10,9},{13,14},{14,13},{17,18},{18,... | collective-permute-start | bytes 258056 | tf_op jit(solution)/shard_map/ppermute | solution.py:438
  16.6 8.8 %collective-permute-start.4 = (bf16[21,16,128]{2,1,0:T(8,128)(2,1)S(1)}, bf16[21,16,128]{2,1,0:T(8,128)(2,1)S(1)}, u32[]{:S(2)}, u32[]{:S(2)}) collective-permute-start(bf16[21,16,128]{2,1,0:T(8,128)(2,1)S(1)} %get-tuple-element.27), channel_id=1, source_target_pairs={{0,1},{1,0},{2,3},{3,2},{4,5},{5,4},{6,7},{7,6},{8,9},{9,8},{10,11... | collective-permute-start | bytes 258056 | tf_op jit(solution)/shard_map/ppermute | solution.py:439
where the time goes:
time: 27.5 us; the launch traced here: 27.4 us
  starting transfers between devices  11 us (40%)
  waiting for transfers between devices  10.6 us (39%)
  Pallas kernels  5.07 us (18%)
  between operations  0.72 us (3%)
    ppermute x3, waiting for transfers between devices, per_device(): other = lax.ppermute(mine, 'circ', [(i, i ^ mask) for i in range(members)])  6.28 us
    ppermute x3, starting transfers between devices, per_device(): other = lax.ppermute(mine, 'circ', [(i, i ^ mask) for i in range(members)])  5.79 us
    ppermute x1, starting transfers between devices, per_device(): inner = lax.ppermute(inner, 'span', near)  4.5 us
    ppermute x1, waiting for transfers between devices, per_device(): inner = lax.ppermute(inner, 'span', near)  4.3 us
    pallas_call x1, Pallas kernels, per_device(): pl.pallas_call(third_kernel, out_shape=(field, field), in_specs=[vmem] *...  1.91 us
    pallas_call x1, Pallas kernels, per_device(): pl.pallas_call(first_kernel, out_shape=(field, field, jax.ShapeDtypeStruc...  1.63 us
    pallas_call x1, Pallas kernels, per_device(): pl.pallas_call(functools.partial(second_kernel, masks), out_shape=(field,...  1.54 us
    ppermute x1, starting transfers between devices, per_device(): outer = lax.ppermute(outer, 'span', far)  0.67 us
  transfers between devices with their start and end apart: 5, of which 4 were waited for; matrix products, arithmetic and copies ran while one was open for 0% of the time, Pallas kernels for 0%

commit v1 on v0

--- a/solution.py
+++ b/solution.py
@@ -146,26 +146,33 @@
             out[i, n * 16 : n * 16 + 16, :] = jnp.concatenate([x[n] for x in groups], axis=0).astype(jnp.bfloat16)
 
 
+def early_kernel(a_r, a_s, v_r, v_s, outer, inner, held):
+    var_count, rows, layers, cells = a_r.shape
+    own_blocks = cells // TILE
+    odd = jnp.bitwise_and(lax.axis_index("span"), 1)
+    for to, s in ((outer, odd * (rows - 1)), (inner, (1 - odd) * (rows - 1))):
+        for v in range(var_count):
+            for n, ref in enumerate((a_r, a_s, v_r, v_s)):
+                held[v, n * layers : (n + 1) * layers, :] = ref[v, s]
+            for i in range(own_blocks):
+                to[v * own_blocks + i] = held[v, :, i * TILE : (i + 1) * TILE].astype(jnp.bfloat16)
+
+
 def second_kernel(
-    masks, mine, other, v_r, v_s, a_r, a_s, weights, margin, count,
-    o_r, o_s, h_r, h_s, q_out, p_out, outer, inner, flux, held, spot, g,
+    var_count, masks, mine, other, weights, margin, count,
+    q_out, p_out, pulls_out, moved_out, spot, outer, inner, flux, g,
 ):
-    var_count, rows, layers, cells = a_r.shape
-    total = 2 * mine.shape[0]
-    own_blocks = cells // TILE
-    entries = weights.shape[2]
+    rows, total, entries, _ = weights.shape
+    own_blocks = pulls_out.shape[1] - 2
     spread = REACH + own_blocks + 1
-    first_block = lax.axis_index("circ") * own_blocks
+    here = lax.axis_index("circ")
+    first_block = here * own_blocks
     row8 = iota((8, TILE), 0)
     lane = iota((8, TILE), 1)
-    lane_all = iota((layers, cells), 1)
-    layer_all = iota((layers, cells), 0)
-    edge = jnp.logical_or(lane_all == 0, lane_all == cells - 1)
     left = wrapped(first_block - 1 + total, total)
     right = wrapped(first_block + own_blocks, total)
 
     filled = row8 < var_count
-    here = lax.axis_index("circ")
     for at in range(total):
         half, part = divmod(at, total // 2)
         place, i = divmod(part, own_blocks)
@@ -185,11 +192,6 @@
     spot[2:4, :] = g[left, 2 * rows + 1, 6:8, :]
     spot[4:6, :] = g[right, 2 * rows, 6:8, :]
     spot[6:8, :] = g[right, 2 * rows + 1, 6:8, :]
-    spots = spot[...]
-    columns = [
-        lax.dot_general(spots, edge_pick(q, cells), (((0,), (0,)), ((), ())), preferred_element_type=f32)
-        for q in range(4)
-    ]
 
     def block(s, b):
         primal = jnp.zeros((8, TILE), f32)
@@ -219,67 +221,113 @@
             if 0 < t < spread - 1:
                 q_out[s, t - 1] = primal
                 p_out[s, t - 1] = advanced(s, b, moved)
-        own = []
         for i in range(own_blocks):
             primal, moved = block(s, first_block + i)
-            own.append(moved)
+            moved_out[s, 1 + i] = moved
             q_out[s, spread - 2 + i] = primal
             p_out[s, spread - 2 + i] = advanced(s, first_block + i, moved)
-        blank = [jnp.zeros((8, TILE), f32)] * (own_blocks - 2)
-        side_flux = [block(s, left)[1], block(s, right)[1]]
-        pulls = [
-            pull_row(lambda t: flux[s, t + 1], weights, margin, count, s, slot, first_block, base, total)
-            for slot in range(-1, own_blocks + 1)
-        ]
-
-        def at_sides(low, high):
-            return jnp.concatenate([pltpu.roll(low, 1, 1), *blank, pltpu.roll(high, TILE - 1, 1)], axis=1)
-
-        pulled = step_size * jnp.concatenate(pulls[1:-1], axis=1)
-        pulled_side = step_size * at_sides(pulls[0], pulls[-1])
-        pushed = step_size * jnp.concatenate(own, axis=1)
-        pushed_side = step_size * at_sides(*side_flux)
-        for v in range(var_count):
-            at = (v * rows + s) * 8
-            cut = slice(at, at + layers)
-            o_r[v, s] = (
-                v_r[v, s] + carry * columns[0][cut] + jnp.where(layer_all == layers - 1, pulled[v : v + 1], 0.0)
+        moved_out[s, 0] = block(s, left)[1]
+        moved_out[s, own_blocks + 1] = block(s, right)[1]
+        for slot in range(-1, own_blocks + 1):
+            pulls_out[s, slot + 1] = pull_row(
+                lambda t: flux[s, t + 1], weights, margin, count, s, slot, first_block, base, total
             )
-            o_s[v, s] = v_s[v, s] + carry * columns[1][cut] - jnp.where(layer_all == 0, pushed[v : v + 1], 0.0)
-            h_r[v, s] = columns[2][cut] + jnp.where(
-                edge, carry * a_r[v, s] + jnp.where(layer_all == layers - 1, pulled_side[v : v + 1], 0.0), 0.0
-            )
-            h_s[v, s] = columns[3][cut] + jnp.where(
-                edge, carry * a_s[v, s] - jnp.where(layer_all == 0, pushed_side[v : v + 1], 0.0), 0.0
-            )
-
-    last = jnp.concatenate([spots, jnp.ones((8, TILE), f32)], axis=0).astype(jnp.bfloat16)
+
     odd = jnp.bitwise_and(lax.axis_index("span"), 1)
-    for to, s in ((inner, (1 - odd) * (rows - 1)), (outer, odd * (rows - 1))):
+    last = jnp.concatenate([spot[...], jnp.zeros((8, TILE), f32)], axis=0).astype(jnp.bfloat16)
+    for to, s in ((outer, odd * (rows - 1)), (inner, (1 - odd) * (rows - 1))):
         for j in range(total // 2):
             to[j] = jnp.concatenate([g[2 * j, rows + s], g[2 * j + 1, rows + s]], axis=0).astype(jnp.bfloat16)
-        for v in range(var_count):
-            for n, ref in enumerate((a_r, a_s, o_r, o_s)):
-                held[v, n * layers : (n + 1) * layers, :] = ref[v, s]
-            for i in range(own_blocks):
-                to[total // 2 + v * own_blocks + i] = held[v, :, i * TILE : (i + 1) * TILE].astype(jnp.bfloat16)
-        to[total // 2 + var_count * own_blocks] = last
+        for i in range(own_blocks):
+            pair = jnp.concatenate([pulls_out[s, 1 + i], moved_out[s, 1 + i]], axis=0)
+            to[total // 2 + i] = pair.astype(jnp.bfloat16)
+        to[total // 2 + own_blocks] = last
 
 
 def third_kernel(
-    outer, inner, o_r, o_s, h_r, h_s, q, p, a_r, a_s, jd_r, jd_s, jo_r, jo_s, src_r, src_s, weights, margin, count,
-    out_r, out_s, flux, x_r, x_s, rows_low, rows_high,
+    bands, outer, inner, v_r, v_s, a_r, a_s, pulls, moved, spot, jd_r, jd_s, jo_r, jo_s, src_r, src_s,
+    part_r, part_s, x_r, x_s, rows_low, rows_high,
 ):
     var_count, rows, layers, cells = a_r.shape
+    own_blocks = cells // TILE
+    band = lax.axis_index("span")
+    odd = jnp.bitwise_and(band, 1) == 1
+    lane_all = iota((layers, cells), 1)
+    layer_all = iota((layers, cells), 0)
+    edge = jnp.logical_or(lane_all == 0, lane_all == cells - 1)
+    for x in (x_r, x_s):
+        x[...] = jnp.zeros(x.shape, f32)
+    for v in range(var_count):
+        for i in range(own_blocks):
+            one = outer[v * own_blocks + i].astype(f32)
+            two = inner[v * own_blocks + i].astype(f32)
+            rows_low[v, :, i * TILE : (i + 1) * TILE] = jnp.where(odd, two, one)
+            rows_high[v, :, i * TILE : (i + 1) * TILE] = jnp.where(odd, one, two)
+    inside = (jnp.where(band > 0, 1.0, 0.0).astype(f32), jnp.where(band < bands - 1, 1.0, 0.0).astype(f32))
+    spots = spot[...]
+    columns = [
+        lax.dot_general(spots, edge_pick(q, cells), (((0,), (0,)), ((), ())), preferred_element_type=f32)
+        for q in range(4)
+    ]
+    blank = [jnp.zeros((8, TILE), f32)] * (own_blocks - 2)
+
+    def middle(ref, s):
+        return jnp.concatenate([ref[s, 1 + i] for i in range(own_blocks)], axis=1)
+
+    def sides(ref, s):
+        low = pltpu.roll(ref[s, 0], 1, 1)
+        high = pltpu.roll(ref[s, own_blocks + 1], TILE - 1, 1)
+        return jnp.concatenate([low, *blank, high], axis=1)
+
+    fields = (
+        (0, v_r, a_r, jd_r, jo_r, src_r, x_r, part_r, layers - 1, pulls, step_size),
+        (1, v_s, a_s, jd_s, jo_s, src_s, x_s, part_s, 0, moved, -step_size),
+    )
+    for n, local, a, jd, jo, src, x, part, layer, source, factor in fields:
+        old = slice(n * layers, (n + 1) * layers)
+        new = slice((2 + n) * layers, (3 + n) * layers)
+        centre = [factor * middle(source, s) for s in range(rows)]
+        beyond = [factor * sides(source, s) for s in range(rows)]
+        for v in range(var_count):
+            for s in range(rows):
+                at = (v * rows + s) * 8
+                value = local[v, s] + carry * columns[n][at : at + layers]
+                value = value + jnp.where(layer_all == layer, centre[s][v : v + 1], 0.0)
+                if s == 0:
+                    value = value + carry * rows_low[v, old, :]
+                if s == rows - 1:
+                    value = value + carry * rows_high[v, old, :]
+                x[v * rows + s, 0:layers, :] = value
+        for s in range(rows):
+            state_row = [x[v * rows + s, 0:layers, :] for v in range(var_count)]
+            for v in range(var_count):
+                wide = x[v * rows + s]
+                at = (v * rows + s) * 8
+                beside = (lanes_apart(wide) + layers_apart(wide))[0:layers]
+                beside = beside + columns[2 + n][at : at + layers] + jnp.where(
+                    edge, carry * a[v, s] + jnp.where(layer_all == layer, beyond[s][v : v + 1], 0.0), 0.0
+                )
+                if s > 0:
+                    beside = beside + x[v * rows + s - 1, 0:layers, :]
+                else:
+                    beside = beside + inside[0] * (rows_low[v, new, :] + carry * a[v, 0])
+                if s < rows - 1:
+                    beside = beside + x[v * rows + s + 1, 0:layers, :]
+                else:
+                    beside = beside + inside[1] * (rows_high[v, new, :] + carry * a[v, rows - 1])
+                res = jacobian_row(jd, jo, state_row, v, s, var_count) - coupling * beside - src[v, s]
+                part[v, s] = state_row[v] - step_size * res
+
+
+def fourth_kernel(outer, inner, q, p, part_r, part_s, weights, margin, count, out_r, out_s, flux):
+    var_count, rows, layers, cells = part_r.shape
     total = weights.shape[1]
     own_blocks = cells // TILE
     spread = REACH + own_blocks + 1
     first_block = lax.axis_index("circ") * own_blocks
     lane = iota((8, TILE), 1)
     layer_all = iota((layers, cells), 0)
-    end = total // 2 + var_count * own_blocks
-    for x in (x_r, x_s):
-        x[...] = jnp.zeros(x.shape, f32)
+    end = total // 2 + own_blocks
     odd = jnp.bitwise_and(lax.axis_index("span"), 1) == 1
 
     def low(n):
@@ -288,25 +336,25 @@
     def high(n):
         return jnp.where(odd, outer[n].astype(f32), inner[n].astype(f32))
 
-    for side, to in ((low, rows_low), (high, rows_high)):
-        for v in range(var_count):
-            for i in range(own_blocks):
-                to[v, :, i * TILE : (i + 1) * TILE] = side(total // 2 + v * own_blocks + i)
-    ends = [low(end), high(end)]
-    inside = [jnp.concatenate([x[8:9]] * own_blocks, axis=1) for x in ends]
     group = lax.rem(lax.shift_right_logical(lane, 3), rows)
-    corner = jnp.where(group == 0, pltpu.roll(ends[0][0:8], (TILE - 8 * (rows - 1)) % TILE, 1), 0.0)
-    corner = corner + jnp.where(group == rows - 1, pltpu.roll(ends[1][0:8], 8 * (rows - 1), 1), 0.0)
+    corner = jnp.where(group == 0, pltpu.roll(low(end)[0:8], (TILE - 8 * (rows - 1)) % TILE, 1), 0.0)
+    corner = corner + jnp.where(group == rows - 1, pltpu.roll(high(end)[0:8], 8 * (rows - 1), 1), 0.0)
     columns = [
         lax.dot_general(corner, edge_pick(n, cells), (((0,), (0,)), ((), ())), preferred_element_type=f32)
         for n in range(2)
     ]
+    beside = []
+    for side in (low, high):
+        pairs = [side(total // 2 + i) for i in range(own_blocks)]
+        beside.append([
+            (carry * step_size) * jnp.concatenate([x[0:8] for x in pairs], axis=1),
+            -(carry * step_size) * jnp.concatenate([x[8:16] for x in pairs], axis=1),
+        ])
 
     def halo(side, b):
         both = side(lax.shift_right_logical(b, 1))
         return jnp.where(jnp.bitwise_and(b, 1) == 1, both[8:16], both[0:8])
 
-    extra = []
     for s in range(rows):
         base = first_block - margin[s, 0, 0] - 5 + 4 * total
         own = []
@@ -326,42 +374,22 @@
             pull_row(lambda t: flux[s, t], weights, margin, count, s, slot, first_block, base, total)
             for slot in range(own_blocks)
         ]
-        extra.append((step_size * jnp.concatenate(pulls, axis=1), -step_size * jnp.concatenate(own, axis=1)))
-
-    fields = (
-        (o_r, h_r, a_r, jd_r, jo_r, src_r, x_r, out_r, layers - 1),
-        (o_s, h_s, a_s, jd_s, jo_s, src_s, x_s, out_s, 0),
-    )
-    for n, (o, h, a, jd, jo, src, x, out, layer) in enumerate(fields):
-        old = slice(n * layers, (n + 1) * layers)
-        new = slice((2 + n) * layers, (3 + n) * layers)
-        for v in range(var_count):
-            for s in range(rows):
-                value = o[v, s]
-                if s == 0:
-                    value = value + carry * rows_low[v, old, :]
-                if s == rows - 1:
-                    value = value + carry * rows_high[v, old, :]
-                x[v * rows + s, 0:layers, :] = value
-        for s in range(rows):
-            state_row = [x[v * rows + s, 0:layers, :] for v in range(var_count)]
+        extra = [step_size * jnp.concatenate(pulls, axis=1), -step_size * jnp.concatenate(own, axis=1)]
+        for n, (part, out, layer) in enumerate(((part_r, out_r, layers - 1), (part_s, out_s, 0))):
+            more = extra[n]
+            edges = 0
+            if s == 0:
+                more = more + beside[0][n]
+                edges = edges + 1
+            if s == rows - 1:
+                more = more + beside[1][n]
+                edges = edges + 1
             for v in range(var_count):
-                wide = x[v * rows + s]
-                beside = (lanes_apart(wide) + layers_apart(wide))[0:layers]
                 at = (v * rows + s) * 8
-                beside = beside + h[v, s] + carry * columns[n][at : at + layers]
-                if s > 0:
-                    beside = beside + x[v * rows + s - 1, 0:layers, :]
-                else:
-                    beside = beside + inside[0] * (rows_low[v, new, :] + carry * a[v, 0])
-                if s < rows - 1:
-                    beside = beside + x[v * rows + s + 1, 0:layers, :]
-                else:
-                    beside = beside + inside[1] * (rows_high[v, new, :] + carry * a[v, rows - 1])
-                res = jacobian_row(jd, jo, state_row, v, s, var_count) - coupling * beside - src[v, s]
-                out[v, s] = (
-                    state_row[v] - step_size * res + jnp.where(layer_all == layer, extra[s][n][v : v + 1], 0.0)
-                )
+                value = part[v, s] + jnp.where(layer_all == layer, more[v : v + 1], 0.0)
+                if edges:
+                    value = value + (2.0 * carry * carry) * columns[n][at : at + layers]
+                out[v, s] = value
 
 
 def per_device(
@@ -407,54 +435,70 @@
         compiler_params=params,
         name="local_part",
     )(*[pltpu.with_memory_space_constraint(x, pltpu.HBM) for x in arguments])
+    held = pltpu.VMEM((var_count, 4 * layers, cells), f32)
+    bands = lax.axis_size("span")
+    near = [(i, i ^ 1) for i in range(bands)]
+    far = [pair for i in range(1, bands - 1, 2) for pair in ((i, i + 1), (i + 1, i))]
     members = lax.axis_size("circ")
     mine, masks = share, []
     mask = members // 2
     while mask > 0:
         other = lax.ppermute(mine, "circ", [(i, i ^ mask) for i in range(members)])
+        if mask == members // 2:
+            early = jax.ShapeDtypeStruct((var_count * own_blocks, 16, TILE), jnp.bfloat16)
+            early_outer, early_inner = pl.pallas_call(
+                early_kernel,
+                out_shape=(early, early),
+                in_specs=[vmem] * 4,
+                out_specs=(vmem,) * 2,
+                scratch_shapes=[held],
+                compiler_params=params,
+                name="early_rows",
+            )(a_r, a_s, v_r, v_s)
+            early_outer = lax.ppermute(early_outer, "span", far)
+            early_inner = lax.ppermute(early_inner, "span", near)
         if mask > 1:
             mine = jnp.concatenate([mine, other], axis=0)
             masks.append(mask)
         mask //= 2
-    tiles = jax.ShapeDtypeStruct((total // 2 + var_count * own_blocks + 1, 16, TILE), jnp.bfloat16)
+    tiles = jax.ShapeDtypeStruct((total // 2 + own_blocks + 1, 16, TILE), jnp.bfloat16)
     listed = jax.ShapeDtypeStruct((rows, spread - 2 + own_blocks, 8, TILE), f32)
-    o_r, o_s, h_r, h_s, q, p, outer, inner = pl.pallas_call(
-        functools.partial(second_kernel, masks),
-        out_shape=(field, field, field, field, listed, listed, tiles, tiles),
-        in_specs=[vmem] * 7 + [smem] * 2,
-        out_specs=(vmem,) * 8,
+    around = jax.ShapeDtypeStruct((rows, own_blocks + 2, 8, TILE), f32)
+    q, p, pulls, moved, spot, outer, inner = pl.pallas_call(
+        functools.partial(second_kernel, var_count, masks),
+        out_shape=(listed, listed, around, around, jax.ShapeDtypeStruct((8, TILE), f32), tiles, tiles),
+        in_specs=[vmem] * 3 + [smem] * 2,
+        out_specs=(vmem,) * 7,
         scratch_shapes=[
             pltpu.VMEM((rows, spread, 8, TILE), f32),
-            pltpu.VMEM((var_count, 4 * layers, cells), f32),
-            pltpu.VMEM((8, TILE), f32),
             pltpu.VMEM((total, 3 * rows, 8, TILE), f32),
         ],
         compiler_params=params,
         name="interface_part",
-    )(mine, other, v_r, v_s, a_r, a_s, weights, margin, count)
-    bands = lax.axis_size("span")
-    near = [(i, i ^ 1) for i in range(bands)]
-    far = [pair for i in range(1, bands - 1, 2) for pair in ((i, i + 1), (i + 1, i))]
+    )(mine, other, weights, margin, count)
     outer = lax.ppermute(outer, "span", far)
     inner = lax.ppermute(inner, "span", near)
+    part_r, part_s = pl.pallas_call(
+        functools.partial(third_kernel, bands),
+        out_shape=(field, field),
+        in_specs=[vmem] * 15,
+        out_specs=(vmem,) * 2,
+        scratch_shapes=[padded, padded, held, held],
+        compiler_params=params,
+        name="own_part",
+    )(
+        early_outer, early_inner, v_r, v_s, a_r, a_s, pulls, moved, spot, jac_diag_rotor, jac_diag_stator,
+        jac_off_rotor, jac_off_stator, source_rotor, source_stator,
+    )
     out_r, out_s = pl.pallas_call(
-        third_kernel,
+        fourth_kernel,
         out_shape=(field, field),
-        in_specs=[vmem] * 17 + [smem] * 2,
+        in_specs=[vmem] * 7 + [smem] * 2,
         out_specs=(vmem,) * 2,
-        scratch_shapes=[
-            pltpu.VMEM((rows, spread - 2, 8, TILE), f32),
-            padded,
-            padded,
-            pltpu.VMEM((var_count, 4 * layers, cells), f32),
-            pltpu.VMEM((var_count, 4 * layers, cells), f32),
-        ],
+        scratch_shapes=[pltpu.VMEM((rows, spread - 2, 8, TILE), f32)],
         compiler_params=params,
         name="final_part",
-    )(
-        outer, inner, o_r, o_s, h_r, h_s, q, p, a_r, a_s, jac_diag_rotor, jac_diag_stator,
-        jac_off_rotor, jac_off_stator, source_rotor, source_stator, weights, margin, count,
-    )
+    )(outer, inner, q, p, part_r, part_s, weights, margin, count)
     return (out_r, out_s)
 
 

time: 27.5 us -> 27.7 us (level)
  waiting for transfers between devices: 10.6 us -> 7.06 us
  starting transfers between devices: 11 us -> 14.4 us
    ppermute x0 -> x2, starting transfers between devices: none -> 5.16 us  [the longest x1 4.5 us: per_device(): early_inner = lax.ppermute(early_inner, 'span', near)]
    ppermute x1, waiting for transfers between devices: 4.3 us -> 2.11 us  [per_device(): inner = lax.ppermute(inner, 'span', near)]
    ppermute x1, starting transfers between devices: 4.5 us -> 2.79 us  [per_device(): inner = lax.ppermute(inner, 'span', near)]
    ppermute x3, waiting for transfers between devices: 6.28 us -> 4.94 us  [per_device(): other = lax.ppermute(mine, 'circ', [(i, i ^ mask) for i in range(members)])]
    pallas_call x2 -> x4, Pallas kernels: 3.45 us -> 3.6 us  [the longest x1 1.63 us: per_device(): pl.pallas_call(fourth_kernel, out_shape=(field, field), in_specs=[vmem] *...]
  transfers between devices with their start and end apart: 5 -> 7, of which waited for: 4 -> 3; matrix products, arithmetic and copies ran while one was open for 0% -> 0% of each run, Pallas kernels for 0% -> 7%
where the time goes in v1:
time: 27.7 us; the launch traced here: 27.5 us
  starting transfers between devices  14.4 us (52%)
  waiting for transfers between devices  7.06 us (25%)
  Pallas kernels  5.23 us (19%)
  between operations  0.76 us (3%)
    ppermute x3, starting transfers between devices, per_device(): other = lax.ppermute(mine, 'circ', [(i, i ^ mask) for i in range(members)])  5.79 us
    ppermute x3, waiting for transfers between devices, per_device(): other = lax.ppermute(mine, 'circ', [(i, i ^ mask) for i in range(members)])  4.94 us
    ppermute x1, starting transfers between devices, per_device(): early_inner = lax.ppermute(early_inner, 'span', near)  4.5 us
    ppermute x1, starting transfers between devices, per_device(): inner = lax.ppermute(inner, 'span', near)  2.79 us
    ppermute x1, waiting for transfers between devices, per_device(): inner = lax.ppermute(inner, 'span', near)  2.11 us
    pallas_call x1, Pallas kernels, per_device(): pl.pallas_call(first_kernel, out_shape=(field, field, jax.ShapeDtypeStruc...  1.63 us
    pallas_call x1, Pallas kernels, per_device(): pl.pallas_call(fourth_kernel, out_shape=(field, field), in_specs=[vmem] *...  1.63 us
    pallas_call x1, Pallas kernels, per_device(): pl.pallas_call(functools.partial(second_kernel, var_count, masks), out_sh...  1.38 us
  transfers between devices with their start and end apart: 7, of which 3 were waited for; matrix products, arithmetic and copies ran while one was open for 0% of the time, Pallas kernels for 7%

profile of v1, /device:TPU:0, one launch (start us, length us, event | category | flops | bytes accessed | tf_op | source)
XLA Modules:
  0.0 27.5 jit_solution(13947960828120690459)
XLA Ops:
  0.6 1.6 %local_part.1 = (f32[6,2,4,256]{3,2,1,0:T(4,128)S(1)}, f32[6,2,4,256]{3,2,1,0:T(4,128)S(1)}, bf16[2,64,128]{2,1,0:T(8,128)(2,1)S(1)}, f32[6,2,4,256]{3,2,1,0:T(4...) custom-call(f32[6,2,4,256]{3,2,1,0:T(4,128)} %refs_0_.1, ...), custom_call_target="tpu_custom_call" | custom-call | tf_op jit(solution)/shard_map/local_part/pallas_call | solution.py:424
  2.3 4.1 %collective-permute-start = (bf16[2,64,128]{2,1,0:T(8,128)(2,1)S(1)}, bf16[2,64,128]{2,1,0:T(8,128)(2,1)S(1)}, u32[]{:S(2)}, u32[]{:S(2)}) collective-permute-start(bf16[2,64,128]{2,1,0:T(8,128)(2,1)S(1)} %get-tuple-element.21), channel_id=1, source_target_pairs={{0,16},{4,20},{8,24},{12,28},{16,0},{20,4},{24,8},{28,12},{1,17},{... | collective-permute-start | bytes 98312 | tf_op jit(solution)/shard_map/ppermute | solution.py:446
  6.4 2.2 %collective-permute-done = bf16[2,64,128]{2,1,0:T(8,128)(2,1)S(1)} collective-permute-done((bf16[2,64,128]{2,1,0:T(8,128)(2,1)S(1)}, bf16[2,64,128]{2,1,0:T(8,128)(2,1)S(1)}, u32[]{:S(2)}, u32[]{:S(2)}) %collective-permute-start) | collective-permute-done | bytes 32800 | tf_op jit(solution)/shard_map/ppermute | solution.py:446
  8.6 1.6 %collective-permute-start.1 = (bf16[4,64,128]{2,1,0:T(8,128)(2,1)S(1)}, bf16[4,64,128]{2,1,0:T(8,128)(2,1)S(1)}, u32[]{:S(2)}, u32[]{:S(2)}) collective-permute-start(bf16[4,64,128]{2,1,0:T(8,128)(2,1)S(1)} %pad_maximum_fusion), channel_id=1, source_target_pairs={{0,8},{4,12},{8,0},{12,4},{16,24},{20,28},{24,16},{28,20},{1,9},{5... | collective-permute-start | bytes 196616 | tf_op jit(solution)/shard_map/ppermute | solution.py:446
  10.3 2.7 %collective-permute-done.1 = bf16[4,64,128]{2,1,0:T(8,128)(2,1)S(1)} collective-permute-done((bf16[4,64,128]{2,1,0:T(8,128)(2,1)S(1)}, bf16[4,64,128]{2,1,0:T(8,128)(2,1)S(1)}, u32[]{:S(2)}, u32[]{:S(2)}) %collective-permute-start.1) | collective-permute-done | bytes 65568 | tf_op jit(solution)/shard_map/ppermute | solution.py:446
  13.0 0.1 collective-permute-start.2
  13.1 0.0 copy-start.2
  13.1 0.0 copy-start.3
  13.1 0.0 copy-start.4
  13.1 0.0 copy-start.5
  13.1 0.1 early_rows.1
  13.2 0.7 %collective-permute-start.5 = (bf16[12,16,128]{2,1,0:T(8,128)(2,1)S(1)}, bf16[12,16,128]{2,1,0:T(8,128)(2,1)S(1)}, u32[]{:S(2)}, u32[]{:S(2)}) collective-permute-start(bf16[12,16,128]{2,1,0:T(8,128)(2,1)S(1)} %get-tuple-element.33), channel_id=1, source_target_pairs={{1,2},{2,1},{5,6},{6,5},{9,10},{10,9},{13,14},{14,13},{17,18},{18,... | collective-permute-start | bytes 147464 | tf_op jit(solution)/shard_map/ppermute | solution.py:458
  13.8 4.5 %collective-permute-start.6 = (bf16[12,16,128]{2,1,0:T(8,128)(2,1)S(1)}, bf16[12,16,128]{2,1,0:T(8,128)(2,1)S(1)}, u32[]{:S(2)}, u32[]{:S(2)}) collective-permute-start(bf16[12,16,128]{2,1,0:T(8,128)(2,1)S(1)} %get-tuple-element.34), channel_id=1, source_target_pairs={{0,1},{1,0},{2,3},{3,2},{4,5},{5,4},{6,7},{7,6},{8,9},{9,8},{10,11... | collective-permute-start | bytes 147464 | tf_op jit(solution)/shard_map/ppermute | solution.py:459
  18.3 0.0 collective-permute-done.2.other
  18.3 0.0 copy-start
  18.3 0.0 copy-start.1
  18.3 1.4 %interface_part.1 = (f32[2,11,8,128]{3,2,1,0:T(8,128)S(1)}, f32[2,11,8,128]{3,2,1,0:T(8,128)S(1)}, f32[2,4,8,128]{3,2,1,0:T(8,128)S(1)}, f32[2,4,8,128]{3,2,1,0:...) custom-call(bf16[8,64,128]{2,1,0:T(8,128)(2,1)S(1)} %constant_dynamic-update-, ...), custom_call_target="tpu_custom_call" | custom-call | tf_op jit(solution)/shard_map/interface_part/pallas_call | solution.py:467
  19.7 0.7 %collective-permute-start.3 = (bf16[11,16,128]{2,1,0:T(8,128)(2,1)S(1)}, bf16[11,16,128]{2,1,0:T(8,128)(2,1)S(1)}, u32[]{:S(2)}, u32[]{:S(2)}) collective-permute-start(bf16[11,16,128]{2,1,0:T(8,128)(2,1)S(1)} %get-tuple-element.25), channel_id=1, source_target_pairs={{1,2},{2,1},{5,6},{6,5},{9,10},{10,9},{13,14},{14,13},{17,18},{18,... | collective-permute-start | bytes 135176 | tf_op jit(solution)/shard_map/ppermute | solution.py:479
  20.4 2.8 %collective-permute-start.4 = (bf16[11,16,128]{2,1,0:T(8,128)(2,1)S(1)}, bf16[11,16,128]{2,1,0:T(8,128)(2,1)S(1)}, u32[]{:S(2)}, u32[]{:S(2)}) collective-permute-start(bf16[11,16,128]{2,1,0:T(8,128)(2,1)S(1)} %get-tuple-element.26), channel_id=1, source_target_pairs={{0,1},{1,0},{2,3},{3,2},{4,5},{5,4},{6,7},{7,6},{8,9},{9,8},{10,11... | collective-permute-start | bytes 135176 | tf_op jit(solution)/shard_map/ppermute | solution.py:480
  23.2 0.0 collective-permute-done.5.outer
  23.2 0.0 collective-permute-done.6.inner
  23.2 0.0 copy-done.2
  23.2 0.0 copy-done.3
  23.2 0.0 copy-done.4
  23.2 0.0 copy-done.5
  23.2 0.0 copy-done
  23.2 0.0 copy-done.1
  23.2 0.5 %own_part.1 = (f32[6,2,4,256]{3,2,1,0:T(4,128)S(1)}, f32[6,2,4,256]{3,2,1,0:T(4,128)S(1)}) custom-call(bf16[12,16,128]{2,1,0:T(8,128)(2,1)S(1)} %collective-permute-done.5.outer, bf16[12,16,128]{2,1,0:T(8,128)(2,1)S(1)} %collective-permute-done.6.inner, f32[6,2,4,256]{3,2,1,0:T(4,128)S(1)} %get-tuple-element.31.v_r, ...), custom_call_target="tpu_custom_call" | custom-call | tf_op jit(solution)/shard_map/own_part/pallas_call | solution.py:481
  23.8 0.0 collective-permute-done.3.outer
  23.8 2.1 %collective-permute-done.4.inner = bf16[11,16,128]{2,1,0:T(8,128)(2,1)S(1)} collective-permute-done((bf16[11,16,128]{2,1,0:T(8,128)(2,1)S(1)}, bf16[11,16,128]{2,1,0:T(8,128)(2,1)S(1)}, u32[]{:S(2)}, u32[]{:S(2)}) %collective-permute-start.4) | collective-permute-done | bytes 45088 | tf_op jit(solution)/shard_map/ppermute | solution.py:480
  25.9 1.6 %final_part.1 = (f32[6,2,4,256]{3,2,1,0:T(4,128)}, f32[6,2,4,256]{3,2,1,0:T(4,128)}) custom-call(bf16[11,16,128]{2,1,0:T(8,128)(2,1)S(1)} %collective-permute-done.3.outer, bf16[11,16,128]{2,1,0:T(8,128)(2,1)S(1)} %collective-permute-done.4.inner, f32[2,11,8,128]{3,2,1,0:T(8,128)S(1)} %get-tuple-element.27.q, f32[2,11,8,128]{3,2,1,0:T(8,128)S(1)} %get-tuple-element.28.p, ...), custom_call_target="tpu_custom_call" | custom-call | tf_op jit(solution)/shard_map/final_part/pallas_call | solution.py:493
  (4 shorter events, 0.0 us)
Async XLA Ops:
  2.3 6.3 %collective-permute-start = (bf16[2,64,128]{2,1,0:T(8,128)(2,1)S(1)}, bf16[2,64,128]{2,1,0:T(8,128)(2,1)S(1)}, u32[]{:S(2)}, u32[]{:S(2)}) collective-permute-start(bf16[2,64,128]{2,1,0:T(8,128)(2,1)S(1)} %get-tuple-element.21), channel_id=1, source_target_pairs={{0,16},{4,20},{8,24},{12,28},{16,0},{20,4},{24,8},{28,12},{1,17},{... | collective-permute-start | bytes 98312 | tf_op jit(solution)/shard_map/ppermute | solution.py:446
  8.6 4.3 %collective-permute-start.1 = (bf16[4,64,128]{2,1,0:T(8,128)(2,1)S(1)}, bf16[4,64,128]{2,1,0:T(8,128)(2,1)S(1)}, u32[]{:S(2)}, u32[]{:S(2)}) collective-permute-start(bf16[4,64,128]{2,1,0:T(8,128)(2,1)S(1)} %pad_maximum_fusion), channel_id=1, source_target_pairs={{0,8},{4,12},{8,0},{12,4},{16,24},{20,28},{24,16},{28,20},{1,9},{5... | collective-permute-start | bytes 196616 | tf_op jit(solution)/shard_map/ppermute | solution.py:446
  13.0 5.4 %collective-permute-start.2 = (bf16[8,64,128]{2,1,0:T(8,128)(2,1)S(1)}, bf16[8,64,128]{2,1,0:T(8,128)(2,1)S(1)}, u32[]{:S(2)}, u32[]{:S(2)}) collective-permute-start(bf16[8,64,128]{2,1,0:T(8,128)(2,1)S(1)} %constant_dynamic-update-slice_fusion.mine), channel_id=1, source_target_pairs={{0,4},{4,0},{8,12},{12,8},{16,20},{20,16},{24,28},{28,24},{1,5},{5... | collective-permute-start | bytes 393224 | tf_op jit(solution)/shard_map/ppermute | solution.py:446
  13.1 10.1 %copy-start.2 = (f32[6,2,4,256]{3,2,1,0:T(4,128)S(1)}, f32[6,2,4,256]{3,2,1,0:T(4,128)}, u32[]{:S(2)}) copy-start(f32[6,2,4,256]{3,2,1,0:T(4,128)} %jd_r.1) | copy-start | bytes 147460
  13.1 10.1 %copy-start.3 = (f32[6,2,4,256]{3,2,1,0:T(4,128)S(1)}, f32[6,2,4,256]{3,2,1,0:T(4,128)}, u32[]{:S(2)}) copy-start(f32[6,2,4,256]{3,2,1,0:T(4,128)} %jd_s.1) | copy-start | bytes 147460
  13.1 10.1 %copy-start.4 = (f32[6,2,4,256]{3,2,1,0:T(4,128)S(1)}, f32[6,2,4,256]{3,2,1,0:T(4,128)}, u32[]{:S(2)}) copy-start(f32[6,2,4,256]{3,2,1,0:T(4,128)} %src_r.1) | copy-start | bytes 147460
  13.1 10.1 %copy-start.5 = (f32[6,2,4,256]{3,2,1,0:T(4,128)S(1)}, f32[6,2,4,256]{3,2,1,0:T(4,128)}, u32[]{:S(2)}) copy-start(f32[6,2,4,256]{3,2,1,0:T(4,128)} %src_s.1) | copy-start | bytes 147460
  13.2 10.0 %collective-permute-start.5 = (bf16[12,16,128]{2,1,0:T(8,128)(2,1)S(1)}, bf16[12,16,128]{2,1,0:T(8,128)(2,1)S(1)}, u32[]{:S(2)}, u32[]{:S(2)}) collective-permute-start(bf16[12,16,128]{2,1,0:T(8,128)(2,1)S(1)} %get-tuple-element.33), channel_id=1, source_target_pairs={{1,2},{2,1},{5,6},{6,5},{9,10},{10,9},{13,14},{14,13},{17,18},{18,... | collective-permute-start | bytes 147464 | tf_op jit(solution)/shard_map/ppermute | solution.py:458
  13.8 9.4 %collective-permute-start.6 = (bf16[12,16,128]{2,1,0:T(8,128)(2,1)S(1)}, bf16[12,16,128]{2,1,0:T(8,128)(2,1)S(1)}, u32[]{:S(2)}, u32[]{:S(2)}) collective-permute-start(bf16[12,16,128]{2,1,0:T(8,128)(2,1)S(1)} %get-tuple-element.34), channel_id=1, source_target_pairs={{0,1},{1,0},{2,3},{3,2},{4,5},{5,4},{6,7},{7,6},{8,9},{9,8},{10,11... | collective-permute-start | bytes 147464 | tf_op jit(solution)/shard_map/ppermute | solution.py:459
  18.3 4.9 %copy-start = (bf16[6,6,2,4,256]{4,3,2,1,0:T(4,128)(2,1)S(1)}, bf16[6,6,2,4,256]{4,3,2,1,0:T(4,128)(2,1)}, u32[]{:S(2)}) copy-start(bf16[6,6,2,4,256]{4,3,2,1,0:T(4,128)(2,1)} %jo_r.1) | copy-start | bytes 442372
  18.3 4.9 %copy-start.1 = (bf16[6,6,2,4,256]{4,3,2,1,0:T(4,128)(2,1)S(1)}, bf16[6,6,2,4,256]{4,3,2,1,0:T(4,128)(2,1)}, u32[]{:S(2)}) copy-start(bf16[6,6,2,4,256]{4,3,2,1,0:T(4,128)(2,1)} %jo_s.1) | copy-start | bytes 442372
  19.7 4.1 %collective-permute-start.3 = (bf16[11,16,128]{2,1,0:T(8,128)(2,1)S(1)}, bf16[11,16,128]{2,1,0:T(8,128)(2,1)S(1)}, u32[]{:S(2)}, u32[]{:S(2)}) collective-permute-start(bf16[11,16,128]{2,1,0:T(8,128)(2,1)S(1)} %get-tuple-element.25), channel_id=1, source_target_pairs={{1,2},{2,1},{5,6},{6,5},{9,10},{10,9},{13,14},{14,13},{17,18},{18,... | collective-permute-start | bytes 135176 | tf_op jit(solution)/shard_map/ppermute | solution.py:479
  20.4 5.5 %collective-permute-start.4 = (bf16[11,16,128]{2,1,0:T(8,128)(2,1)S(1)}, bf16[11,16,128]{2,1,0:T(8,128)(2,1)S(1)}, u32[]{:S(2)}, u32[]{:S(2)}) collective-permute-start(bf16[11,16,128]{2,1,0:T(8,128)(2,1)S(1)} %get-tuple-element.26), channel_id=1, source_target_pairs={{0,1},{1,0},{2,3},{3,2},{4,5},{5,4},{6,7},{7,6},{8,9},{9,8},{10,11... | collective-permute-start | bytes 135176 | tf_op jit(solution)/shard_map/ppermute | solution.py:480

commit v2 on v0

--- a/solution.py
+++ b/solution.py
@@ -146,12 +146,12 @@
             out[i, n * 16 : n * 16 + 16, :] = jnp.concatenate([x[n] for x in groups], axis=0).astype(jnp.bfloat16)
 
 
-def second_kernel(
-    masks, mine, other, v_r, v_s, a_r, a_s, weights, margin, count,
-    o_r, o_s, h_r, h_s, q_out, p_out, outer, inner, flux, held, spot, g,
-):
+def second_kernel(masks, *refs):
+    pieces, refs = refs[: len(masks)], refs[len(masks) :]
+    v_r, v_s, a_r, a_s, weights, margin, count = refs[:7]
+    o_r, o_s, h_r, h_s, q_out, p_out, outer, inner, flux, held, spot, g = refs[7:]
     var_count, rows, layers, cells = a_r.shape
-    total = 2 * mine.shape[0]
+    total = weights.shape[1]
     own_blocks = cells // TILE
     entries = weights.shape[2]
     spread = REACH + own_blocks + 1
@@ -166,13 +166,15 @@
 
     filled = row8 < var_count
     here = lax.axis_index("circ")
-    for at in range(total):
-        half, part = divmod(at, total // 2)
-        place, i = divmod(part, own_blocks)
-        mask = half + sum(m for n, m in enumerate(masks) if place >> n & 1)
+    shares = [
+        (piece, n * own_blocks + i, mask, i)
+        for piece, listed in zip(pieces, masks)
+        for n, mask in enumerate(listed)
+        for i in range(own_blocks)
+    ]
+    for piece, at, mask, i in shares:
         b = jnp.bitwise_xor(here, mask) * own_blocks + i
-        whole = other if half else mine
-        tiles = [whole[part, n * 16 : n * 16 + 16, :].astype(f32) for n in range(4)]
+        tiles = [piece[at, n * 16 : n * 16 + 16, :].astype(f32) for n in range(4)]
         for s in range(rows):
             rotor, p_high, p_rest, u_high = [x[s * 8 : s * 8 + 8] for x in tiles]
             u_rest = jnp.where(
@@ -408,20 +410,29 @@
         name="local_part",
     )(*[pltpu.with_memory_space_constraint(x, pltpu.HBM) for x in arguments])
     members = lax.axis_size("circ")
-    mine, masks = share, []
+    pieces = [(share, [0])]
     mask = members // 2
     while mask > 0:
-        other = lax.ppermute(mine, "circ", [(i, i ^ mask) for i in range(members)])
-        if mask > 1:
-            mine = jnp.concatenate([mine, other], axis=0)
-            masks.append(mask)
+        if mask == 1 and len(pieces) > 1:
+            pieces = pieces[::-1]
+            pieces = [(jnp.concatenate([x for x, _ in pieces], axis=0), sum((m for _, m in pieces), []))]
+        pairs = [(i, i ^ mask) for i in range(members)]
+        moved = [(lax.ppermute(x, "circ", pairs), [m ^ mask for m in masks]) for x, masks in pieces]
+        pieces = pieces + moved
+        if mask > 2 and len(pieces) > 2:
+            half = len(pieces) // 2
+            pieces = [
+                (jnp.concatenate([x for x, _ in part], axis=0), sum((m for _, m in part), []))
+                for part in (pieces[:half], pieces[half:])
+            ]
         mask //= 2
+    masks = [m for _, m in pieces]
     tiles = jax.ShapeDtypeStruct((total // 2 + var_count * own_blocks + 1, 16, TILE), jnp.bfloat16)
     listed = jax.ShapeDtypeStruct((rows, spread - 2 + own_blocks, 8, TILE), f32)
     o_r, o_s, h_r, h_s, q, p, outer, inner = pl.pallas_call(
         functools.partial(second_kernel, masks),
         out_shape=(field, field, field, field, listed, listed, tiles, tiles),
-        in_specs=[vmem] * 7 + [smem] * 2,
+        in_specs=[vmem] * (len(pieces) + 5) + [smem] * 2,
         out_specs=(vmem,) * 8,
         scratch_shapes=[
             pltpu.VMEM((rows, spread, 8, TILE), f32),
@@ -431,7 +442,7 @@
         ],
         compiler_params=params,
         name="interface_part",
-    )(mine, other, v_r, v_s, a_r, a_s, weights, margin, count)
+    )(*[x for x, _ in pieces], v_r, v_s, a_r, a_s, weights, margin, count)
     bands = lax.axis_size("span")
     near = [(i, i ^ 1) for i in range(bands)]
     far = [pair for i in range(1, bands - 1, 2) for pair in ((i, i + 1), (i + 1, i))]

time: 27.5 us -> 28.5 us (1.036)
  waiting for transfers between devices: 10.6 us -> 11.3 us
    ppermute x3 -> x4, waiting for transfers between devices: 6.28 us -> 7.02 us  [per_device(): lax.ppermute(x, 'circ', pairs)]
    ppermute x3 -> x4, starting transfers between devices: 5.79 us -> 6.2 us  [per_device(): lax.ppermute(x, 'circ', pairs)]
  transfers between devices with their start and end apart: 5 -> 6, of which waited for: 4 -> 5; matrix products, arithmetic and copies ran while one was open for 0% -> 0% of each run, Pallas kernels for 0% -> 0%
where the time goes in v2:
time: 28.5 us; the launch traced here: 28.3 us
  waiting for transfers between devices  11.3 us (40%)
  starting transfers between devices  11.2 us (39%)
  Pallas kernels  5.07 us (18%)
  between operations  0.72 us (3%)
    ppermute x4, waiting for transfers between devices, per_device(): lax.ppermute(x, 'circ', pairs)  7.02 us
    ppermute x4, starting transfers between devices, per_device(): lax.ppermute(x, 'circ', pairs)  6.2 us
    ppermute x1, waiting for transfers between devices, per_device(): inner = lax.ppermute(inner, 'span', near)  4.31 us
    ppermute x1, starting transfers between devices, per_device(): inner = lax.ppermute(inner, 'span', near)  4.29 us
    pallas_call x1, Pallas kernels, per_device(): pl.pallas_call(third_kernel, out_shape=(field, field), in_specs=[vmem] *...  1.91 us
    pallas_call x1, Pallas kernels, per_device(): pl.pallas_call(first_kernel, out_shape=(field, field, jax.ShapeDtypeStruc...  1.63 us
    pallas_call x1, Pallas kernels, per_device(): pl.pallas_call(functools.partial(second_kernel, masks), out_shape=(field,...  1.54 us
    ppermute x1, starting transfers between devices, per_device(): outer = lax.ppermute(outer, 'span', far)  0.67 us
  transfers between devices with their start and end apart: 6, of which 5 were waited for; matrix products, arithmetic and copies ran while one was open for 0% of the time, Pallas kernels for 0%

profile of v2, /device:TPU:0, one launch (start us, length us, event | category | flops | bytes accessed | tf_op | source)
XLA Modules:
  0.0 28.3 jit_solution(15586959629819551662)
XLA Ops:
  0.6 1.6 %local_part.1 = (f32[6,2,4,256]{3,2,1,0:T(4,128)S(1)}, f32[6,2,4,256]{3,2,1,0:T(4,128)S(1)}, bf16[2,64,128]{2,1,0:T(8,128)(2,1)S(1)}, f32[6,2,4,256]{3,2,1,0:T(4...) custom-call(f32[6,2,4,256]{3,2,1,0:T(4,128)} %refs_0_.1, ...), custom_call_target="tpu_custom_call" | custom-call | tf_op jit(solution)/shard_map/local_part/pallas_call | solution.py:398
  2.3 4.1 %collective-permute-start = (bf16[2,64,128]{2,1,0:T(8,128)(2,1)S(1)}, bf16[2,64,128]{2,1,0:T(8,128)(2,1)S(1)}, u32[]{:S(2)}, u32[]{:S(2)}) collective-permute-start(bf16[2,64,128]{2,1,0:T(8,128)(2,1)S(1)} %get-tuple-element.18), channel_id=1, source_target_pairs={{0,16},{4,20},{8,24},{12,28},{16,0},{20,4},{24,8},{28,12},{1,17},{... | collective-permute-start | bytes 98312 | tf_op jit(solution)/shard_map/ppermute | solution.py:420
  6.4 2.2 %collective-permute-done = bf16[2,64,128]{2,1,0:T(8,128)(2,1)S(1)} collective-permute-done((bf16[2,64,128]{2,1,0:T(8,128)(2,1)S(1)}, bf16[2,64,128]{2,1,0:T(8,128)(2,1)S(1)}, u32[]{:S(2)}, u32[]{:S(2)}) %collective-permute-start) | collective-permute-done | bytes 32800 | tf_op jit(solution)/shard_map/ppermute | solution.py:420
  8.6 1.6 %collective-permute-start.1 = (bf16[2,64,128]{2,1,0:T(8,128)(2,1)S(1)}, bf16[2,64,128]{2,1,0:T(8,128)(2,1)S(1)}, u32[]{:S(2)}, u32[]{:S(2)}) collective-permute-start(bf16[2,64,128]{2,1,0:T(8,128)(2,1)S(1)} %collective-permute-done), channel_id=1, source_target_pairs={{0,8},{4,12},{8,0},{12,4},{16,24},{20,28},{24,16},{28,20},{1,9},{5... | collective-permute-start | bytes 98312 | tf_op jit(solution)/shard_map/ppermute | solution.py:420
  10.2 0.5 %collective-permute-start.2 = (bf16[2,64,128]{2,1,0:T(8,128)(2,1)S(1)}, bf16[2,64,128]{2,1,0:T(8,128)(2,1)S(1)}, u32[]{:S(2)}, u32[]{:S(2)}) collective-permute-start(bf16[2,64,128]{2,1,0:T(8,128)(2,1)S(1)} %get-tuple-element.18), channel_id=1, source_target_pairs={{0,8},{4,12},{8,0},{12,4},{16,24},{20,28},{24,16},{28,20},{1,9},{5... | collective-permute-start | bytes 98312 | tf_op jit(solution)/shard_map/ppermute | solution.py:420
  10.6 1.9 %collective-permute-done.1 = bf16[2,64,128]{2,1,0:T(8,128)(2,1)S(1)} collective-permute-done((bf16[2,64,128]{2,1,0:T(8,128)(2,1)S(1)}, bf16[2,64,128]{2,1,0:T(8,128)(2,1)S(1)}, u32[]{:S(2)}, u32[]{:S(2)}) %collective-permute-start.1) | collective-permute-done | bytes 32800 | tf_op jit(solution)/shard_map/ppermute | solution.py:420
  12.5 1.6 %collective-permute-done.2 = bf16[2,64,128]{2,1,0:T(8,128)(2,1)S(1)} collective-permute-done((bf16[2,64,128]{2,1,0:T(8,128)(2,1)S(1)}, bf16[2,64,128]{2,1,0:T(8,128)(2,1)S(1)}, u32[]{:S(2)}, u32[]{:S(2)}) %collective-permute-start.2) | collective-permute-done | bytes 32800 | tf_op jit(solution)/shard_map/ppermute | solution.py:420
  14.1 0.1 collective-permute-start.3
  14.2 1.3 %collective-permute-done.3.refs_1_ = bf16[8,64,128]{2,1,0:T(8,128)(2,1)S(1)} collective-permute-done((bf16[8,64,128]{2,1,0:T(8,128)(2,1)S(1)}, bf16[8,64,128]{2,1,0:T(8,128)(2,1)S(1)}, u32[]{:S(2)}, u32[]{:S(2)}) %collective-permute-start.3) | collective-permute-done | bytes 131104 | tf_op jit(solution)/shard_map/ppermute | solution.py:420
  15.5 0.0 copy-start
  15.5 0.0 copy-start.1
  15.5 0.0 copy-start.2
  15.5 0.0 copy-start.3
  15.5 0.0 copy-start.4
  15.6 0.0 copy-start.5
  15.6 1.5 %interface_part.1 = (f32[6,2,4,256]{3,2,1,0:T(4,128)S(1)}, f32[6,2,4,256]{3,2,1,0:T(4,128)S(1)}, f32[6,2,4,256]{3,2,1,0:T(4,128)S(1)}, f32[6,2,4,256]{3,2,1,0:T(...) custom-call(bf16[8,64,128]{2,1,0:T(8,128)(2,1)S(1)} %constant_dynami, ...), custom_call_target="tpu_custom_call" | custom-call | tf_op jit(solution)/shard_map/interface_part/pallas_call | solution.py:432
  17.1 0.7 %collective-permute-start.4 = (bf16[21,16,128]{2,1,0:T(8,128)(2,1)S(1)}, bf16[21,16,128]{2,1,0:T(8,128)(2,1)S(1)}, u32[]{:S(2)}, u32[]{:S(2)}) collective-permute-start(bf16[21,16,128]{2,1,0:T(8,128)(2,1)S(1)} %get-tuple-element.26), channel_id=1, source_target_pairs={{1,2},{2,1},{5,6},{6,5},{9,10},{10,9},{13,14},{14,13},{17,18},{18,... | collective-permute-start | bytes 258056 | tf_op jit(solution)/shard_map/ppermute | solution.py:449
  17.8 4.3 %collective-permute-start.5 = (bf16[21,16,128]{2,1,0:T(8,128)(2,1)S(1)}, bf16[21,16,128]{2,1,0:T(8,128)(2,1)S(1)}, u32[]{:S(2)}, u32[]{:S(2)}) collective-permute-start(bf16[21,16,128]{2,1,0:T(8,128)(2,1)S(1)} %get-tuple-element.27), channel_id=1, source_target_pairs={{0,1},{1,0},{2,3},{3,2},{4,5},{5,4},{6,7},{7,6},{8,9},{9,8},{10,11... | collective-permute-start | bytes 258056 | tf_op jit(solution)/shard_map/ppermute | solution.py:450
  22.1 0.0 collective-permute-done.4.outer
  22.1 4.3 %collective-permute-done.5.inner = bf16[21,16,128]{2,1,0:T(8,128)(2,1)S(1)} collective-permute-done((bf16[21,16,128]{2,1,0:T(8,128)(2,1)S(1)}, bf16[21,16,128]{2,1,0:T(8,128)(2,1)S(1)}, u32[]{:S(2)}, u32[]{:S(2)}) %collective-permute-start.5) | collective-permute-done | bytes 86048 | tf_op jit(solution)/shard_map/ppermute | solution.py:450
  26.4 0.0 copy-done
  26.4 0.0 copy-done.1
  26.4 0.0 copy-done.2
  26.4 0.0 copy-done.3
  26.4 0.0 copy-done.4
  26.4 0.0 copy-done.5
  26.4 1.9 %final_part.1 = (f32[6,2,4,256]{3,2,1,0:T(4,128)}, f32[6,2,4,256]{3,2,1,0:T(4,128)}) custom-call(bf16[21,16,128]{2,1,0:T(8,128)(2,1)S(1)} %collective-permute-done.4.outer, bf16[21,16,128]{2,1,0:T(8,128)(2,1)S(1)} %collective-permute-done.5.inner, f32[6,2,4,256]{3,2,1,0:T(4,128)S(1)} %get-tuple-element.28.o_r, f32[6,2,4,256]{3,2,1,0:T(4,128)S(1)} %get-tuple-element.29.o_s, ...), custom_call_target="tpu_custom_call" | custom-call | tf_op jit(solution)/shard_map/final_part/pallas_call | solution.py:451
  (4 shorter events, 0.0 us)
Async XLA Ops:
  2.3 6.3 %collective-permute-start = (bf16[2,64,128]{2,1,0:T(8,128)(2,1)S(1)}, bf16[2,64,128]{2,1,0:T(8,128)(2,1)S(1)}, u32[]{:S(2)}, u32[]{:S(2)}) collective-permute-start(bf16[2,64,128]{2,1,0:T(8,128)(2,1)S(1)} %get-tuple-element.18), channel_id=1, source_target_pairs={{0,16},{4,20},{8,24},{12,28},{16,0},{20,4},{24,8},{28,12},{1,17},{... | collective-permute-start | bytes 98312 | tf_op jit(solution)/shard_map/ppermute | solution.py:420
  8.6 3.9 %collective-permute-start.1 = (bf16[2,64,128]{2,1,0:T(8,128)(2,1)S(1)}, bf16[2,64,128]{2,1,0:T(8,128)(2,1)S(1)}, u32[]{:S(2)}, u32[]{:S(2)}) collective-permute-start(bf16[2,64,128]{2,1,0:T(8,128)(2,1)S(1)} %collective-permute-done), channel_id=1, source_target_pairs={{0,8},{4,12},{8,0},{12,4},{16,24},{20,28},{24,16},{28,20},{1,9},{5... | collective-permute-start | bytes 98312 | tf_op jit(solution)/shard_map/ppermute | solution.py:420
  10.2 3.9 %collective-permute-start.2 = (bf16[2,64,128]{2,1,0:T(8,128)(2,1)S(1)}, bf16[2,64,128]{2,1,0:T(8,128)(2,1)S(1)}, u32[]{:S(2)}, u32[]{:S(2)}) collective-permute-start(bf16[2,64,128]{2,1,0:T(8,128)(2,1)S(1)} %get-tuple-element.18), channel_id=1, source_target_pairs={{0,8},{4,12},{8,0},{12,4},{16,24},{20,28},{24,16},{28,20},{1,9},{5... | collective-permute-start | bytes 98312 | tf_op jit(solution)/shard_map/ppermute | solution.py:420
  14.1 1.4 %collective-permute-start.3 = (bf16[8,64,128]{2,1,0:T(8,128)(2,1)S(1)}, bf16[8,64,128]{2,1,0:T(8,128)(2,1)S(1)}, u32[]{:S(2)}, u32[]{:S(2)}) collective-permute-start(bf16[8,64,128]{2,1,0:T(8,128)(2,1)S(1)} %constant_dynamic-update-slice_fusion.refs_0_), channel_id=1, source_target_pairs={{0,4},{4,0},{8,12},{12,8},{16,20},{20,16},{24,28},{28,24},{1,5},{5... | collective-permute-start | bytes 393224 | tf_op jit(solution)/shard_map/ppermute | solution.py:420
  15.5 10.9 %copy-start = (bf16[6,6,2,4,256]{4,3,2,1,0:T(4,128)(2,1)S(1)}, bf16[6,6,2,4,256]{4,3,2,1,0:T(4,128)(2,1)}, u32[]{:S(2)}) copy-start(bf16[6,6,2,4,256]{4,3,2,1,0:T(4,128)(2,1)} %jo_r.1) | copy-start | bytes 442372
  15.5 10.9 %copy-start.1 = (bf16[6,6,2,4,256]{4,3,2,1,0:T(4,128)(2,1)S(1)}, bf16[6,6,2,4,256]{4,3,2,1,0:T(4,128)(2,1)}, u32[]{:S(2)}) copy-start(bf16[6,6,2,4,256]{4,3,2,1,0:T(4,128)(2,1)} %jo_s.1) | copy-start | bytes 442372
  15.5 10.9 %copy-start.2 = (f32[6,2,4,256]{3,2,1,0:T(4,128)S(1)}, f32[6,2,4,256]{3,2,1,0:T(4,128)}, u32[]{:S(2)}) copy-start(f32[6,2,4,256]{3,2,1,0:T(4,128)} %jd_r.1) | copy-start | bytes 147460
  15.5 10.9 %copy-start.3 = (f32[6,2,4,256]{3,2,1,0:T(4,128)S(1)}, f32[6,2,4,256]{3,2,1,0:T(4,128)}, u32[]{:S(2)}) copy-start(f32[6,2,4,256]{3,2,1,0:T(4,128)} %jd_s.1) | copy-start | bytes 147460
  15.5 10.9 %copy-start.4 = (f32[6,2,4,256]{3,2,1,0:T(4,128)S(1)}, f32[6,2,4,256]{3,2,1,0:T(4,128)}, u32[]{:S(2)}) copy-start(f32[6,2,4,256]{3,2,1,0:T(4,128)} %src_r.1) | copy-start | bytes 147460
  15.6 10.9 %copy-start.5 = (f32[6,2,4,256]{3,2,1,0:T(4,128)S(1)}, f32[6,2,4,256]{3,2,1,0:T(4,128)}, u32[]{:S(2)}) copy-start(f32[6,2,4,256]{3,2,1,0:T(4,128)} %src_s.1) | copy-start | bytes 147460
  17.1 5.0 %collective-permute-start.4 = (bf16[21,16,128]{2,1,0:T(8,128)(2,1)S(1)}, bf16[21,16,128]{2,1,0:T(8,128)(2,1)S(1)}, u32[]{:S(2)}, u32[]{:S(2)}) collective-permute-start(bf16[21,16,128]{2,1,0:T(8,128)(2,1)S(1)} %get-tuple-element.26), channel_id=1, source_target_pairs={{1,2},{2,1},{5,6},{6,5},{9,10},{10,9},{13,14},{14,13},{17,18},{18,... | collective-permute-start | bytes 258056 | tf_op jit(solution)/shard_map/ppermute | solution.py:449
  17.8 8.6 %collective-permute-start.5 = (bf16[21,16,128]{2,1,0:T(8,128)(2,1)S(1)}, bf16[21,16,128]{2,1,0:T(8,128)(2,1)S(1)}, u32[]{:S(2)}, u32[]{:S(2)}) collective-permute-start(bf16[21,16,128]{2,1,0:T(8,128)(2,1)S(1)} %get-tuple-element.27), channel_id=1, source_target_pairs={{0,1},{1,0},{2,3},{3,2},{4,5},{5,4},{6,7},{7,6},{8,9},{9,8},{10,11... | collective-permute-start | bytes 258056 | tf_op jit(solution)/shard_map/ppermute | solution.py:450

commit v3 on v0

--- a/solution.py
+++ b/solution.py
@@ -148,7 +148,7 @@
 
 def second_kernel(
     masks, mine, other, v_r, v_s, a_r, a_s, weights, margin, count,
-    o_r, o_s, h_r, h_s, q_out, p_out, outer, inner, flux, held, spot, g,
+    o_r, o_s, h_r, h_s, q_out, p_out, inner, outer, flux, held, spot, g,
 ):
     var_count, rows, layers, cells = a_r.shape
     total = 2 * mine.shape[0]
@@ -267,7 +267,7 @@
 
 
 def third_kernel(
-    outer, inner, o_r, o_s, h_r, h_s, q, p, a_r, a_s, jd_r, jd_s, jo_r, jo_s, src_r, src_s, weights, margin, count,
+    inner, outer, o_r, o_s, h_r, h_s, q, p, a_r, a_s, jd_r, jd_s, jo_r, jo_s, src_r, src_s, weights, margin, count,
     out_r, out_s, flux, x_r, x_s, rows_low, rows_high,
 ):
     var_count, rows, layers, cells = a_r.shape
@@ -418,7 +418,7 @@
         mask //= 2
     tiles = jax.ShapeDtypeStruct((total // 2 + var_count * own_blocks + 1, 16, TILE), jnp.bfloat16)
     listed = jax.ShapeDtypeStruct((rows, spread - 2 + own_blocks, 8, TILE), f32)
-    o_r, o_s, h_r, h_s, q, p, outer, inner = pl.pallas_call(
+    o_r, o_s, h_r, h_s, q, p, inner, outer = pl.pallas_call(
         functools.partial(second_kernel, masks),
         out_shape=(field, field, field, field, listed, listed, tiles, tiles),
         in_specs=[vmem] * 7 + [smem] * 2,
@@ -435,8 +435,8 @@
     bands = lax.axis_size("span")
     near = [(i, i ^ 1) for i in range(bands)]
     far = [pair for i in range(1, bands - 1, 2) for pair in ((i, i + 1), (i + 1, i))]
+    inner = lax.ppermute(inner, "span", near)
     outer = lax.ppermute(outer, "span", far)
-    inner = lax.ppermute(inner, "span", near)
     out_r, out_s = pl.pallas_call(
         third_kernel,
         out_shape=(field, field),
@@ -452,7 +452,7 @@
         compiler_params=params,
         name="final_part",
     )(
-        outer, inner, o_r, o_s, h_r, h_s, q, p, a_r, a_s, jac_diag_rotor, jac_diag_stator,
+        inner, outer, o_r, o_s, h_r, h_s, q, p, a_r, a_s, jac_diag_rotor, jac_diag_stator,
         jac_off_rotor, jac_off_stator, source_rotor, source_stator, weights, margin, count,
     )
     return (out_r, out_s)

time: 27.5 us -> 25.7 us (0.935)
  the two profiles are of different devices: /device:TPU:0 before, /device:TPU:28 now
where the time goes in v3:
time: 25.7 us; the launch traced here: 25.5 us
  waiting for transfers between devices  14.9 us (58%)
  Pallas kernels  5.08 us (20%)
  starting transfers between devices  4.7 us (18%)
  between operations  0.72 us (3%)
    ppermute x3, waiting for transfers between devices, per_device(): other = lax.ppermute(mine, 'circ', [(i, i ^ mask) for i in range(members)])  10.1 us
    ppermute x1, waiting for transfers between devices, per_device(): outer = lax.ppermute(outer, 'span', far)  4.17 us
    ppermute x1, starting transfers between devices, per_device(): outer = lax.ppermute(outer, 'span', far)  2.38 us
    pallas_call x1, Pallas kernels, per_device(): pl.pallas_call(third_kernel, out_shape=(field, field), in_specs=[vmem] *...  1.91 us
    pallas_call x1, Pallas kernels, per_device(): pl.pallas_call(first_kernel, out_shape=(field, field, jax.ShapeDtypeStruc...  1.63 us
    ppermute x1, starting transfers between devices, per_device(): inner = lax.ppermute(inner, 'span', near)  1.55 us
    pallas_call x1, Pallas kernels, per_device(): pl.pallas_call(functools.partial(second_kernel, masks), out_shape=(field,...  1.54 us
    ppermute x3, starting transfers between devices, per_device(): other = lax.ppermute(mine, 'circ', [(i, i ^ mask) for i in range(members)])  0.77 us
  transfers between devices with their start and end apart: 5, of which 5 were waited for; matrix products, arithmetic and copies ran while one was open for 0% of the time, Pallas kernels for 0%

profile of v3, /device:TPU:28, one launch (start us, length us, event | category | flops | bytes accessed | tf_op | source)
XLA Modules:
  0.0 25.5 jit_solution(17137130921288908845)
XLA Ops:
  0.6 1.6 %local_part.1 = (f32[6,2,4,256]{3,2,1,0:T(4,128)S(1)}, f32[6,2,4,256]{3,2,1,0:T(4,128)S(1)}, bf16[2,64,128]{2,1,0:T(8,128)(2,1)S(1)}, f32[6,2,4,256]{3,2,1,0:T(4...) custom-call(f32[6,2,4,256]{3,2,1,0:T(4,128)} %refs_0_.1, ...), custom_call_target="tpu_custom_call" | custom-call | tf_op jit(solution)/shard_map/local_part/pallas_call | solution.py:396
  2.3 0.4 %collective-permute-start = (bf16[2,64,128]{2,1,0:T(8,128)(2,1)S(1)}, bf16[2,64,128]{2,1,0:T(8,128)(2,1)S(1)}, u32[]{:S(2)}, u32[]{:S(2)}) collective-permute-start(bf16[2,64,128]{2,1,0:T(8,128)(2,1)S(1)} %get-tuple-element.18), channel_id=1, source_target_pairs={{0,16},{4,20},{8,24},{12,28},{16,0},{20,4},{24,8},{28,12},{1,17},{... | collective-permute-start | bytes 98312 | tf_op jit(solution)/shard_map/ppermute | solution.py:414
  2.7 4.7 %collective-permute-done = bf16[2,64,128]{2,1,0:T(8,128)(2,1)S(1)} collective-permute-done((bf16[2,64,128]{2,1,0:T(8,128)(2,1)S(1)}, bf16[2,64,128]{2,1,0:T(8,128)(2,1)S(1)}, u32[]{:S(2)}, u32[]{:S(2)}) %collective-permute-start) | collective-permute-done | bytes 32800 | tf_op jit(solution)/shard_map/ppermute | solution.py:414
  7.4 0.3 %collective-permute-start.1 = (bf16[4,64,128]{2,1,0:T(8,128)(2,1)S(1)}, bf16[4,64,128]{2,1,0:T(8,128)(2,1)S(1)}, u32[]{:S(2)}, u32[]{:S(2)}) collective-permute-start(bf16[4,64,128]{2,1,0:T(8,128)(2,1)S(1)} %pad_maximum_fusion), channel_id=1, source_target_pairs={{0,8},{4,12},{8,0},{12,4},{16,24},{20,28},{24,16},{28,20},{1,9},{5... | collective-permute-start | bytes 196616 | tf_op jit(solution)/shard_map/ppermute | solution.py:414
  7.7 4.0 %collective-permute-done.1 = bf16[4,64,128]{2,1,0:T(8,128)(2,1)S(1)} collective-permute-done((bf16[4,64,128]{2,1,0:T(8,128)(2,1)S(1)}, bf16[4,64,128]{2,1,0:T(8,128)(2,1)S(1)}, u32[]{:S(2)}, u32[]{:S(2)}) %collective-permute-start.1) | collective-permute-done | bytes 65568 | tf_op jit(solution)/shard_map/ppermute | solution.py:414
  11.7 0.1 collective-permute-start.2
  11.8 1.3 %collective-permute-done.2.other = bf16[8,64,128]{2,1,0:T(8,128)(2,1)S(1)} collective-permute-done((bf16[8,64,128]{2,1,0:T(8,128)(2,1)S(1)}, bf16[8,64,128]{2,1,0:T(8,128)(2,1)S(1)}, u32[]{:S(2)}, u32[]{:S(2)}) %collective-permute-start.2) | collective-permute-done | bytes 131104 | tf_op jit(solution)/shard_map/ppermute | solution.py:414
  13.2 0.0 copy-start
  13.2 0.0 copy-start.1
  13.2 0.0 copy-start.2
  13.2 0.0 copy-start.3
  13.2 0.0 copy-start.4
  13.2 0.0 copy-start.5
  13.2 1.5 %interface_part.1 = (f32[6,2,4,256]{3,2,1,0:T(4,128)S(1)}, f32[6,2,4,256]{3,2,1,0:T(4,128)S(1)}, f32[6,2,4,256]{3,2,1,0:T(4,128)S(1)}, f32[6,2,4,256]{3,2,1,0:T(...) custom-call(bf16[8,64,128]{2,1,0:T(8,128)(2,1)S(1)} %constant_dynami, ...), custom_call_target="tpu_custom_call" | custom-call | tf_op jit(solution)/shard_map/interface_part/pallas_call | solution.py:421
  14.7 1.6 %collective-permute-start.3 = (bf16[21,16,128]{2,1,0:T(8,128)(2,1)S(1)}, bf16[21,16,128]{2,1,0:T(8,128)(2,1)S(1)}, u32[]{:S(2)}, u32[]{:S(2)}) collective-permute-start(bf16[21,16,128]{2,1,0:T(8,128)(2,1)S(1)} %get-tuple-element.26), channel_id=1, source_target_pairs={{0,1},{1,0},{2,3},{3,2},{4,5},{5,4},{6,7},{7,6},{8,9},{9,8},{10,11... | collective-permute-start | bytes 258056 | tf_op jit(solution)/shard_map/ppermute | solution.py:438
  16.3 2.4 %collective-permute-start.4 = (bf16[21,16,128]{2,1,0:T(8,128)(2,1)S(1)}, bf16[21,16,128]{2,1,0:T(8,128)(2,1)S(1)}, u32[]{:S(2)}, u32[]{:S(2)}) collective-permute-start(bf16[21,16,128]{2,1,0:T(8,128)(2,1)S(1)} %get-tuple-element.27), channel_id=1, source_target_pairs={{1,2},{2,1},{5,6},{6,5},{9,10},{10,9},{13,14},{14,13},{17,18},{18,... | collective-permute-start | bytes 258056 | tf_op jit(solution)/shard_map/ppermute | solution.py:439
  18.7 0.7 %collective-permute-done.3.inner = bf16[21,16,128]{2,1,0:T(8,128)(2,1)S(1)} collective-permute-done((bf16[21,16,128]{2,1,0:T(8,128)(2,1)S(1)}, bf16[21,16,128]{2,1,0:T(8,128)(2,1)S(1)}, u32[]{:S(2)}, u32[]{:S(2)}) %collective-permute-start.3) | collective-permute-done | bytes 86048 | tf_op jit(solution)/shard_map/ppermute | solution.py:438
  19.4 4.2 %collective-permute-done.4.outer = bf16[21,16,128]{2,1,0:T(8,128)(2,1)S(1)} collective-permute-done((bf16[21,16,128]{2,1,0:T(8,128)(2,1)S(1)}, bf16[21,16,128]{2,1,0:T(8,128)(2,1)S(1)}, u32[]{:S(2)}, u32[]{:S(2)}) %collective-permute-start.4) | collective-permute-done | bytes 86048 | tf_op jit(solution)/shard_map/ppermute | solution.py:439
  23.6 0.0 copy-done
  23.6 0.0 copy-done.1
  23.6 0.0 copy-done.2
  23.6 0.0 copy-done.3
  23.6 0.0 copy-done.4
  23.6 0.0 copy-done.5
  23.6 1.9 %final_part.1 = (f32[6,2,4,256]{3,2,1,0:T(4,128)}, f32[6,2,4,256]{3,2,1,0:T(4,128)}) custom-call(bf16[21,16,128]{2,1,0:T(8,128)(2,1)S(1)} %collective-permute-done.3.inner, bf16[21,16,128]{2,1,0:T(8,128)(2,1)S(1)} %collective-permute-done.4.outer, f32[6,2,4,256]{3,2,1,0:T(4,128)S(1)} %get-tuple-element.28.o_r, f32[6,2,4,256]{3,2,1,0:T(4,128)S(1)} %get-tuple-element.29.o_s, ...), custom_call_target="tpu_custom_call" | custom-call | tf_op jit(solution)/shard_map/final_part/pallas_call | solution.py:440
  (4 shorter events, 0.0 us)
Async XLA Ops:
  2.3 5.1 %collective-permute-start = (bf16[2,64,128]{2,1,0:T(8,128)(2,1)S(1)}, bf16[2,64,128]{2,1,0:T(8,128)(2,1)S(1)}, u32[]{:S(2)}, u32[]{:S(2)}) collective-permute-start(bf16[2,64,128]{2,1,0:T(8,128)(2,1)S(1)} %get-tuple-element.18), channel_id=1, source_target_pairs={{0,16},{4,20},{8,24},{12,28},{16,0},{20,4},{24,8},{28,12},{1,17},{... | collective-permute-start | bytes 98312 | tf_op jit(solution)/shard_map/ppermute | solution.py:414
  7.4 4.3 %collective-permute-start.1 = (bf16[4,64,128]{2,1,0:T(8,128)(2,1)S(1)}, bf16[4,64,128]{2,1,0:T(8,128)(2,1)S(1)}, u32[]{:S(2)}, u32[]{:S(2)}) collective-permute-start(bf16[4,64,128]{2,1,0:T(8,128)(2,1)S(1)} %pad_maximum_fusion), channel_id=1, source_target_pairs={{0,8},{4,12},{8,0},{12,4},{16,24},{20,28},{24,16},{28,20},{1,9},{5... | collective-permute-start | bytes 196616 | tf_op jit(solution)/shard_map/ppermute | solution.py:414
  11.7 1.4 %collective-permute-start.2 = (bf16[8,64,128]{2,1,0:T(8,128)(2,1)S(1)}, bf16[8,64,128]{2,1,0:T(8,128)(2,1)S(1)}, u32[]{:S(2)}, u32[]{:S(2)}) collective-permute-start(bf16[8,64,128]{2,1,0:T(8,128)(2,1)S(1)} %constant_dynamic-update-slice_fusion.mine), channel_id=1, source_target_pairs={{0,4},{4,0},{8,12},{12,8},{16,20},{20,16},{24,28},{28,24},{1,5},{5... | collective-permute-start | bytes 393224 | tf_op jit(solution)/shard_map/ppermute | solution.py:414
  13.2 10.4 %copy-start = (bf16[6,6,2,4,256]{4,3,2,1,0:T(4,128)(2,1)S(1)}, bf16[6,6,2,4,256]{4,3,2,1,0:T(4,128)(2,1)}, u32[]{:S(2)}) copy-start(bf16[6,6,2,4,256]{4,3,2,1,0:T(4,128)(2,1)} %jo_r.1) | copy-start | bytes 442372
  13.2 10.4 %copy-start.1 = (bf16[6,6,2,4,256]{4,3,2,1,0:T(4,128)(2,1)S(1)}, bf16[6,6,2,4,256]{4,3,2,1,0:T(4,128)(2,1)}, u32[]{:S(2)}) copy-start(bf16[6,6,2,4,256]{4,3,2,1,0:T(4,128)(2,1)} %jo_s.1) | copy-start | bytes 442372
  13.2 10.4 %copy-start.2 = (f32[6,2,4,256]{3,2,1,0:T(4,128)S(1)}, f32[6,2,4,256]{3,2,1,0:T(4,128)}, u32[]{:S(2)}) copy-start(f32[6,2,4,256]{3,2,1,0:T(4,128)} %jd_r.1) | copy-start | bytes 147460
  13.2 10.4 %copy-start.3 = (f32[6,2,4,256]{3,2,1,0:T(4,128)S(1)}, f32[6,2,4,256]{3,2,1,0:T(4,128)}, u32[]{:S(2)}) copy-start(f32[6,2,4,256]{3,2,1,0:T(4,128)} %jd_s.1) | copy-start | bytes 147460
  13.2 10.4 %copy-start.4 = (f32[6,2,4,256]{3,2,1,0:T(4,128)S(1)}, f32[6,2,4,256]{3,2,1,0:T(4,128)}, u32[]{:S(2)}) copy-start(f32[6,2,4,256]{3,2,1,0:T(4,128)} %src_r.1) | copy-start | bytes 147460
  13.2 10.4 %copy-start.5 = (f32[6,2,4,256]{3,2,1,0:T(4,128)S(1)}, f32[6,2,4,256]{3,2,1,0:T(4,128)}, u32[]{:S(2)}) copy-start(f32[6,2,4,256]{3,2,1,0:T(4,128)} %src_s.1) | copy-start | bytes 147460
  14.7 4.6 %collective-permute-start.3 = (bf16[21,16,128]{2,1,0:T(8,128)(2,1)S(1)}, bf16[21,16,128]{2,1,0:T(8,128)(2,1)S(1)}, u32[]{:S(2)}, u32[]{:S(2)}) collective-permute-start(bf16[21,16,128]{2,1,0:T(8,128)(2,1)S(1)} %get-tuple-element.26), channel_id=1, source_target_pairs={{0,1},{1,0},{2,3},{3,2},{4,5},{5,4},{6,7},{7,6},{8,9},{9,8},{10,11... | collective-permute-start | bytes 258056 | tf_op jit(solution)/shard_map/ppermute | solution.py:438
  16.3 7.3 %collective-permute-start.4 = (bf16[21,16,128]{2,1,0:T(8,128)(2,1)S(1)}, bf16[21,16,128]{2,1,0:T(8,128)(2,1)S(1)}, u32[]{:S(2)}, u32[]{:S(2)}) collective-permute-start(bf16[21,16,128]{2,1,0:T(8,128)(2,1)S(1)} %get-tuple-element.27), channel_id=1, source_target_pairs={{1,2},{2,1},{5,6},{6,5},{9,10},{10,9},{13,14},{14,13},{17,18},{18,... | collective-permute-start | bytes 258056 | tf_op jit(solution)/shard_map/ppermute | solution.py:439

commit v4 on v3

--- a/solution.py
+++ b/solution.py
@@ -51,11 +51,14 @@
     return high, x - high
 
 
-def flux_of(primal, adjoint):
-    speeds = jnp.sqrt(1.0 + primal * primal)
-    over = jnp.sum(primal * adjoint, axis=0, keepdims=True)
-    under = 6.0 + jnp.sum(primal * primal, axis=0, keepdims=True)
-    return speeds * adjoint + 0.5 * primal * (over / under)
+def flux_parts(primal):
+    square = primal * primal
+    under = 6.0 + jnp.sum(square, axis=0, keepdims=True)
+    return jnp.sqrt(1.0 + square), 0.5 * primal / under
+
+
+def flux_of(primal, speeds, scaled, adjoint):
+    return speeds * adjoint + scaled * jnp.sum(primal * adjoint, axis=0, keepdims=True)
 
 
 def jacobian_row(diag, off, state, v, s, var_count):
@@ -65,16 +68,41 @@
     return total
 
 
-def pull_row(flux, weights, margin, count, s, slot, first_block, base, total):
-    target = wrapped(first_block + slot + total, total)
+def pull_row(flux, table, s, slot):
     acc = jnp.zeros((8, TILE), f32)
     for e in range(REACH):
-        b = wrapped(base + slot + e, total)
-        k = wrapped(target - margin[s, 0, b] + total, total)
-        live = jnp.where(k < count[s, b], 1.0, 0.0).astype(f32)
-        kept = jnp.minimum(k, weights.shape[2] - 1)
-        acc = acc + (weights[s, b, pl.ds(kept, 1), :] * live) * flux(slot + e)
+        acc = acc + table[s, slot + 1, e : e + 1, :] * flux(slot + e)
     return acc
+
+
+def window(margin, s, first_block, total):
+    return first_block - margin[s, 0, 0] - 5 + 4 * total
+
+
+def window_blocks(base, first_block, own_blocks, total):
+    found = [wrapped(base - 1 + t, total) for t in range(REACH + own_blocks + 1)]
+    sides = [wrapped(first_block - 1 + total, total), wrapped(first_block + own_blocks, total)]
+    return found + [first_block + i for i in range(own_blocks)] + sides
+
+
+def table_kernel(weights, margin, count, primal_table, pull_table):
+    rows, total, entries, _ = weights.shape
+    own_blocks = pull_table.shape[1] - 2
+    first_block = lax.axis_index("circ") * own_blocks
+    for s in range(rows):
+        base = window(margin, s, first_block, total)
+        blocks = window_blocks(base, first_block, own_blocks, total)
+        entry = iota((entries, TILE), 0)
+        for t, b in enumerate(blocks):
+            primal_table[s, t] = jnp.where(entry < count[s, b], weights[s, b], 0.0)
+        for slot in range(-1, own_blocks + 1):
+            target = wrapped(first_block + slot + total, total)
+            for e in range(REACH):
+                b = blocks[slot + 1 + e]
+                k = wrapped(target - margin[s, 0, b] + total, total)
+                live = jnp.where(k < count[s, b], 1.0, 0.0).astype(f32)
+                kept = jnp.minimum(k, entries - 1)
+                pull_table[s, slot + 1, e : e + 1, :] = weights[s, b, pl.ds(kept, 1), :] * live
 
 
 def first_kernel(*refs):
@@ -147,13 +175,15 @@
 
 
 def second_kernel(
-    masks, mine, other, v_r, v_s, a_r, a_s, weights, margin, count,
-    o_r, o_s, h_r, h_s, q_out, p_out, inner, outer, flux, held, spot, g,
+    masks, mine, other, v_r, v_s, a_r, a_s, primal_table, pull_table, margin_in,
+    o_r, o_s, h_r, h_s, q_out, speeds_out, scaled_out, p_out, inner, outer, flux, held, spot, g, margin, sem,
 ):
     var_count, rows, layers, cells = a_r.shape
+    fetch = pltpu.make_async_copy(margin_in, margin, sem)
+    fetch.start()
     total = 2 * mine.shape[0]
     own_blocks = cells // TILE
-    entries = weights.shape[2]
+    entries = primal_table.shape[2]
     spread = REACH + own_blocks + 1
     first_block = lax.axis_index("circ") * own_blocks
     row8 = iota((8, TILE), 0)
@@ -191,14 +221,19 @@
         for q in range(4)
     ]
 
-    def block(s, b):
+    fetch.wait()
+
+    def block(s, b, t):
         primal = jnp.zeros((8, TILE), f32)
         for k in range(entries):
-            live = jnp.where(k < count[s, b], 1.0, 0.0).astype(f32)
-            primal = primal + (weights[s, b, k : k + 1, :] * live) * g[margin[s, k, b], s]
+            primal = primal + primal_table[s, t, k : k + 1, :] * g[margin[s, k, b], s]
         primal = jnp.where(filled, primal, 0.0)
-        adjoint = g[b, rows + s]
-        return primal, flux_of(primal, adjoint)
+        parts = flux_parts(primal)
+        return (primal, *parts), flux_of(primal, *parts, g[b, rows + s])
+
+    def keep(s, at, b, parts, moved):
+        q_out[s, at], speeds_out[s, at], scaled_out[s, at] = parts
+        p_out[s, at] = advanced(s, b, moved)
 
     def advanced(s, b, moved):
         place = lax.rem(b, own_blocks)
@@ -211,26 +246,21 @@
         return base - step_size * moved
 
     for s in range(rows):
-        base = first_block - margin[s, 0, 0] - 5 + 4 * total
+        base = window(margin, s, first_block, total)
+        blocks = window_blocks(base, first_block, own_blocks, total)
         for t in range(spread):
-            b = wrapped(base - 1 + t, total)
-            primal, moved = block(s, b)
+            parts, moved = block(s, blocks[t], t)
             flux[s, t] = moved.astype(jnp.bfloat16).astype(f32)
             if 0 < t < spread - 1:
-                q_out[s, t - 1] = primal
-                p_out[s, t - 1] = advanced(s, b, moved)
+                keep(s, t - 1, blocks[t], parts, moved)
         own = []
         for i in range(own_blocks):
-            primal, moved = block(s, first_block + i)
+            parts, moved = block(s, first_block + i, spread + i)
             own.append(moved)
-            q_out[s, spread - 2 + i] = primal
-            p_out[s, spread - 2 + i] = advanced(s, first_block + i, moved)
+            keep(s, spread - 2 + i, first_block + i, parts, moved)
         blank = [jnp.zeros((8, TILE), f32)] * (own_blocks - 2)
-        side_flux = [block(s, left)[1], block(s, right)[1]]
-        pulls = [
-            pull_row(lambda t: flux[s, t + 1], weights, margin, count, s, slot, first_block, base, total)
-            for slot in range(-1, own_blocks + 1)
-        ]
+        side_flux = [block(s, at, spread + own_blocks + n)[1] for n, at in enumerate((left, right))]
+        pulls = [pull_row(lambda t: flux[s, t + 1], pull_table, s, slot) for slot in range(-1, own_blocks + 1)]
 
         def at_sides(low, high):
             return jnp.concatenate([pltpu.roll(low, 1, 1), *blank, pltpu.roll(high, TILE - 1, 1)], axis=1)
@@ -267,11 +297,13 @@
 
 
 def third_kernel(
-    inner, outer, o_r, o_s, h_r, h_s, q, p, a_r, a_s, jd_r, jd_s, jo_r, jo_s, src_r, src_s, weights, margin, count,
-    out_r, out_s, flux, x_r, x_s, rows_low, rows_high,
+    inner, outer, o_r, o_s, h_r, h_s, q, speeds, scaled, p, a_r, a_s, jd_r, jd_s, jo_r, jo_s, src_r, src_s,
+    pull_table, margin_in, away_r, away_s, flux, x_r, x_s, rows_low, rows_high, out_r, out_s, margin, sems,
 ):
+    fetch = pltpu.make_async_copy(margin_in, margin, sems.at[0])
+    fetch.start()
     var_count, rows, layers, cells = a_r.shape
-    total = weights.shape[1]
+    total = margin.shape[2]
     own_blocks = cells // TILE
     spread = REACH + own_blocks + 1
     first_block = lax.axis_index("circ") * own_blocks
@@ -305,28 +337,6 @@
     def halo(side, b):
         both = side(lax.shift_right_logical(b, 1))
         return jnp.where(jnp.bitwise_and(b, 1) == 1, both[8:16], both[0:8])
-
-    extra = []
-    for s in range(rows):
-        base = first_block - margin[s, 0, 0] - 5 + 4 * total
-        own = []
-        for t in range(spread - 2 + own_blocks):
-            b = wrapped(base + t, total) if t < spread - 2 else first_block + t - (spread - 2)
-            adjoint = p[s, t]
-            if s == 0:
-                adjoint = adjoint + carry * halo(low, b)
-            if s == rows - 1:
-                adjoint = adjoint + carry * halo(high, b)
-            moved = flux_of(q[s, t], adjoint)
-            if t < spread - 2:
-                flux[s, t] = moved.astype(jnp.bfloat16).astype(f32)
-            else:
-                own.append(moved)
-        pulls = [
-            pull_row(lambda t: flux[s, t], weights, margin, count, s, slot, first_block, base, total)
-            for slot in range(own_blocks)
-        ]
-        extra.append((step_size * jnp.concatenate(pulls, axis=1), -step_size * jnp.concatenate(own, axis=1)))
 
     fields = (
         (o_r, h_r, a_r, jd_r, jo_r, src_r, x_r, out_r, layers - 1),
@@ -359,9 +369,36 @@
                 else:
                     beside = beside + inside[1] * (rows_high[v, new, :] + carry * a[v, rows - 1])
                 res = jacobian_row(jd, jo, state_row, v, s, var_count) - coupling * beside - src[v, s]
-                out[v, s] = (
-                    state_row[v] - step_size * res + jnp.where(layer_all == layer, extra[s][n][v : v + 1], 0.0)
-                )
+                out[v, s] = state_row[v] - step_size * res
+    fetch.wait()
+    extra = []
+    for s in range(rows):
+        base = window(margin, s, first_block, total)
+        own = []
+        for t in range(spread - 2 + own_blocks):
+            b = wrapped(base + t, total) if t < spread - 2 else first_block + t - (spread - 2)
+            adjoint = p[s, t]
+            if s == 0:
+                adjoint = adjoint + carry * halo(low, b)
+            if s == rows - 1:
+                adjoint = adjoint + carry * halo(high, b)
+            moved = flux_of(q[s, t], speeds[s, t], scaled[s, t], adjoint)
+            if t < spread - 2:
+                flux[s, t] = moved.astype(jnp.bfloat16).astype(f32)
+            else:
+                own.append(moved)
+        pulls = [pull_row(lambda t: flux[s, t], pull_table, s, slot) for slot in range(own_blocks)]
+        extra.append((step_size * jnp.concatenate(pulls, axis=1), -step_size * jnp.concatenate(own, axis=1)))
+
+    copies = []
+    for n, (out, away, layer) in enumerate(((out_r, away_r, layers - 1), (out_s, away_s, 0))):
+        for s in range(rows):
+            for v in range(var_count):
+                out[v, s, layer : layer + 1, :] = out[v, s, layer : layer + 1, :] + extra[s][n][v : v + 1]
+        copies.append(pltpu.make_async_copy(out, away, sems.at[1 + n]))
+        copies[-1].start()
+    for copy in copies:
+        copy.wait()
 
 
 def per_device(
@@ -385,6 +422,7 @@
     field = jax.ShapeDtypeStruct(adjoint_rotor.shape, f32)
     vmem = pl.BlockSpec(memory_space=pltpu.VMEM)
     smem = pl.BlockSpec(memory_space=pltpu.SMEM)
+    anywhere = pl.BlockSpec(memory_space=pl.ANY)
     padded = pltpu.VMEM((TILE // 8, 8, cells), f32)
 
     margin = jnp.swapaxes(margin_block, 1, 2)
@@ -407,6 +445,17 @@
         compiler_params=params,
         name="local_part",
     )(*[pltpu.with_memory_space_constraint(x, pltpu.HBM) for x in arguments])
+    primal_table, pull_table = pl.pallas_call(
+        table_kernel,
+        out_shape=(
+            jax.ShapeDtypeStruct((rows, spread + own_blocks + 2, margin_weight.shape[2], TILE), f32),
+            jax.ShapeDtypeStruct((rows, own_blocks + 2, REACH, TILE), f32),
+        ),
+        in_specs=[vmem] + [smem] * 2,
+        out_specs=(vmem,) * 2,
+        compiler_params=params,
+        name="weight_tables",
+    )(weights, margin, count)
     members = lax.axis_size("circ")
     mine, masks = share, []
     mask = members // 2
@@ -418,20 +467,22 @@
         mask //= 2
     tiles = jax.ShapeDtypeStruct((total // 2 + var_count * own_blocks + 1, 16, TILE), jnp.bfloat16)
     listed = jax.ShapeDtypeStruct((rows, spread - 2 + own_blocks, 8, TILE), f32)
-    o_r, o_s, h_r, h_s, q, p, inner, outer = pl.pallas_call(
+    o_r, o_s, h_r, h_s, q, speeds, scaled, p, inner, outer = pl.pallas_call(
         functools.partial(second_kernel, masks),
-        out_shape=(field, field, field, field, listed, listed, tiles, tiles),
-        in_specs=[vmem] * 7 + [smem] * 2,
-        out_specs=(vmem,) * 8,
+        out_shape=(field,) * 4 + (listed,) * 4 + (tiles,) * 2,
+        in_specs=[vmem] * 8 + [anywhere],
+        out_specs=(vmem,) * 10,
         scratch_shapes=[
             pltpu.VMEM((rows, spread, 8, TILE), f32),
             pltpu.VMEM((var_count, 4 * layers, cells), f32),
             pltpu.VMEM((8, TILE), f32),
             pltpu.VMEM((total, 3 * rows, 8, TILE), f32),
+            pltpu.SMEM(margin.shape, jnp.int32),
+            pltpu.SemaphoreType.DMA(()),
         ],
         compiler_params=params,
         name="interface_part",
-    )(mine, other, v_r, v_s, a_r, a_s, weights, margin, count)
+    )(mine, other, v_r, v_s, a_r, a_s, primal_table, pull_table, margin)
     bands = lax.axis_size("span")
     near = [(i, i ^ 1) for i in range(bands)]
     far = [pair for i in range(1, bands - 1, 2) for pair in ((i, i + 1), (i + 1, i))]
@@ -440,20 +491,24 @@
     out_r, out_s = pl.pallas_call(
         third_kernel,
         out_shape=(field, field),
-        in_specs=[vmem] * 17 + [smem] * 2,
-        out_specs=(vmem,) * 2,
+        in_specs=[vmem] * 19 + [anywhere],
+        out_specs=(anywhere,) * 2,
         scratch_shapes=[
             pltpu.VMEM((rows, spread - 2, 8, TILE), f32),
             padded,
             padded,
             pltpu.VMEM((var_count, 4 * layers, cells), f32),
             pltpu.VMEM((var_count, 4 * layers, cells), f32),
+            pltpu.VMEM(field.shape, f32),
+            pltpu.VMEM(field.shape, f32),
+            pltpu.SMEM(margin.shape, jnp.int32),
+            pltpu.SemaphoreType.DMA((3,)),
         ],
         compiler_params=params,
         name="final_part",
     )(
-        inner, outer, o_r, o_s, h_r, h_s, q, p, a_r, a_s, jac_diag_rotor, jac_diag_stator,
-        jac_off_rotor, jac_off_stator, source_rotor, source_stator, weights, margin, count,
+        inner, outer, o_r, o_s, h_r, h_s, q, speeds, scaled, p, a_r, a_s, jac_diag_rotor, jac_diag_stator,
+        jac_off_rotor, jac_off_stator, source_rotor, source_stator, pull_table, margin,
     )
     return (out_r, out_s)
 

time: 25.7 us -> 24.8 us (0.965)
  waiting for transfers between devices: 14.9 us -> 14 us
    ppermute x3, waiting for transfers between devices: 10.1 us -> 9.12 us  [per_device(): other = lax.ppermute(mine, 'circ', [(i, i ^ mask) for i in range(members)])]
    pallas_call x0 -> x1, Pallas kernels: none -> 0.94 us  [per_device(): pl.pallas_call(table_kernel, out_shape=(jax.ShapeDtypeStruct((rows, sprea...]
    pallas_call x1, Pallas kernels: 1.91 us -> 1.37 us  [per_device(): pl.pallas_call(third_kernel, out_shape=(field, field), in_specs=[vmem] *...]
    pallas_call x1, Pallas kernels: 1.54 us -> 1.17 us  [per_device(): pl.pallas_call(functools.partial(second_kernel, masks), out_shape=(field,...]
  transfers between devices with their start and end apart: 5 -> 5, of which waited for: 5 -> 5; matrix products, arithmetic and copies ran while one was open for 0% -> 0% of each run, Pallas kernels for 0% -> 4%
where the time goes in v4:
time: 24.8 us; the launch traced here: 24.6 us
  waiting for transfers between devices  14 us (56%)
  Pallas kernels  5.11 us (21%)
  starting transfers between devices  4.7 us (19%)
  between operations  0.73 us (3%)
    ppermute x3, waiting for transfers between devices, per_device(): other = lax.ppermute(mine, 'circ', [(i, i ^ mask) for i in range(members)])  9.12 us
    ppermute x1, waiting for transfers between devices, per_device(): outer = lax.ppermute(outer, 'span', far)  4.17 us
    ppermute x1, starting transfers between devices, per_device(): outer = lax.ppermute(outer, 'span', far)  2.38 us
    pallas_call x1, Pallas kernels, per_device(): pl.pallas_call(first_kernel, out_shape=(field, field, jax.ShapeDtypeStruc...  1.63 us
    ppermute x1, starting transfers between devices, per_device(): inner = lax.ppermute(inner, 'span', near)  1.55 us
    pallas_call x1, Pallas kernels, per_device(): pl.pallas_call(third_kernel, out_shape=(field, field), in_specs=[vmem] *...  1.37 us
    pallas_call x1, Pallas kernels, per_device(): pl.pallas_call(functools.partial(second_kernel, masks), out_shape=(field,...  1.17 us
    pallas_call x1, Pallas kernels, per_device(): pl.pallas_call(table_kernel, out_shape=(jax.ShapeDtypeStruct((rows, sprea...  0.94 us
  transfers between devices with their start and end apart: 5, of which 5 were waited for; matrix products, arithmetic and copies ran while one was open for 0% of the time, Pallas kernels for 4%

profile of v4, /device:TPU:28, one launch (start us, length us, event | category | flops | bytes accessed | tf_op | source)
XLA Modules:
  0.0 24.6 jit_solution(14231856024638069907)
XLA Ops:
  0.6 1.6 %local_part.1 = (f32[6,2,4,256]{3,2,1,0:T(4,128)S(1)}, f32[6,2,4,256]{3,2,1,0:T(4,128)S(1)}, bf16[2,64,128]{2,1,0:T(8,128)(2,1)S(1)}, f32[6,2,4,256]{3,2,1,0:T(4...) custom-call(f32[6,2,4,256]{3,2,1,0:T(4,128)} %refs_0_.1, ...), custom_call_target="tpu_custom_call" | custom-call | tf_op jit(solution)/shard_map/local_part/pallas_call | solution.py:434
  2.3 0.4 %collective-permute-start = (bf16[2,64,128]{2,1,0:T(8,128)(2,1)S(1)}, bf16[2,64,128]{2,1,0:T(8,128)(2,1)S(1)}, u32[]{:S(2)}, u32[]{:S(2)}) collective-permute-start(bf16[2,64,128]{2,1,0:T(8,128)(2,1)S(1)} %get-tuple-element.22), channel_id=1, source_target_pairs={{0,16},{4,20},{8,24},{12,28},{16,0},{20,4},{24,8},{28,12},{1,17},{... | collective-permute-start | bytes 98312 | tf_op jit(solution)/shard_map/ppermute | solution.py:463
  2.7 4.7 %collective-permute-done = bf16[2,64,128]{2,1,0:T(8,128)(2,1)S(1)} collective-permute-done((bf16[2,64,128]{2,1,0:T(8,128)(2,1)S(1)}, bf16[2,64,128]{2,1,0:T(8,128)(2,1)S(1)}, u32[]{:S(2)}, u32[]{:S(2)}) %collective-permute-start) | collective-permute-done | bytes 32800 | tf_op jit(solution)/shard_map/ppermute | solution.py:463
  7.4 0.3 %collective-permute-start.1 = (bf16[4,64,128]{2,1,0:T(8,128)(2,1)S(1)}, bf16[4,64,128]{2,1,0:T(8,128)(2,1)S(1)}, u32[]{:S(2)}, u32[]{:S(2)}) collective-permute-start(bf16[4,64,128]{2,1,0:T(8,128)(2,1)S(1)} %pad_maximum_fusion), channel_id=1, source_target_pairs={{0,8},{4,12},{8,0},{12,4},{16,24},{20,28},{24,16},{28,20},{1,9},{5... | collective-permute-start | bytes 196616 | tf_op jit(solution)/shard_map/ppermute | solution.py:463
  7.7 4.0 %collective-permute-done.1 = bf16[4,64,128]{2,1,0:T(8,128)(2,1)S(1)} collective-permute-done((bf16[4,64,128]{2,1,0:T(8,128)(2,1)S(1)}, bf16[4,64,128]{2,1,0:T(8,128)(2,1)S(1)}, u32[]{:S(2)}, u32[]{:S(2)}) %collective-permute-start.1) | collective-permute-done | bytes 65568 | tf_op jit(solution)/shard_map/ppermute | solution.py:463
  11.7 0.1 collective-permute-start.2
  11.8 0.9 %weight_tables.1 = (f32[2,15,4,128]{3,2,1,0:T(4,128)S(1)}, f32[2,4,8,128]{3,2,1,0:T(8,128)S(1)}) custom-call(f32[2,16,4,128]{3,2,1,0:T(4,128)S(1)} %get-tuple-element.27.weights, s32[2,4,16]{2,1,0:T(4,128)S(1)} %get-tuple-element.28.margin.margin_in, s32[2,16]{1,0:T(2,128)S(1)} %get-tuple-element.29.count), custom_call_target="tpu_custom_call" | custom-call | tf_op jit(solution)/shard_map/weight_tables/pallas_call | solution.py:448
  12.8 0.4 %collective-permute-done.2.other = bf16[8,64,128]{2,1,0:T(8,128)(2,1)S(1)} collective-permute-done((bf16[8,64,128]{2,1,0:T(8,128)(2,1)S(1)}, bf16[8,64,128]{2,1,0:T(8,128)(2,1)S(1)}, u32[]{:S(2)}, u32[]{:S(2)}) %collective-permute-start.2) | collective-permute-done | bytes 131104 | tf_op jit(solution)/shard_map/ppermute | solution.py:463
  13.2 0.0 copy-start
  13.2 0.0 copy-start.1
  13.2 0.0 copy-start.2
  13.2 0.0 copy-start.3
  13.2 0.0 copy-start.4
  13.2 0.0 copy-start.5
  13.2 1.2 %interface_part.1 = (f32[6,2,4,256]{3,2,1,0:T(4,128)S(1)}, f32[6,2,4,256]{3,2,1,0:T(4,128)S(1)}, f32[6,2,4,256]{3,2,1,0:T(4,128)S(1)}, f32[6,2,4,256]{3,2,1,0:T(...) custom-call(bf16[8,64,128]{2,1,0:T(8,128)(2,1)S(1)} %constant_dynami, ...), custom_call_target="tpu_custom_call" | custom-call | tf_op jit(solution)/shard_map/interface_part/pallas_call | solution.py:470
  14.4 1.6 %collective-permute-start.3 = (bf16[21,16,128]{2,1,0:T(8,128)(2,1)S(1)}, bf16[21,16,128]{2,1,0:T(8,128)(2,1)S(1)}, u32[]{:S(2)}, u32[]{:S(2)}) collective-permute-start(bf16[21,16,128]{2,1,0:T(8,128)(2,1)S(1)} %get-tuple-element.32), channel_id=1, source_target_pairs={{0,1},{1,0},{2,3},{3,2},{4,5},{5,4},{6,7},{7,6},{8,9},{9,8},{10,11... | collective-permute-start | bytes 258056 | tf_op jit(solution)/shard_map/ppermute | solution.py:489
  15.9 2.4 %collective-permute-start.4 = (bf16[21,16,128]{2,1,0:T(8,128)(2,1)S(1)}, bf16[21,16,128]{2,1,0:T(8,128)(2,1)S(1)}, u32[]{:S(2)}, u32[]{:S(2)}) collective-permute-start(bf16[21,16,128]{2,1,0:T(8,128)(2,1)S(1)} %get-tuple-element.33), channel_id=1, source_target_pairs={{1,2},{2,1},{5,6},{6,5},{9,10},{10,9},{13,14},{14,13},{17,18},{18,... | collective-permute-start | bytes 258056 | tf_op jit(solution)/shard_map/ppermute | solution.py:490
  18.3 0.7 %collective-permute-done.3.inner = bf16[21,16,128]{2,1,0:T(8,128)(2,1)S(1)} collective-permute-done((bf16[21,16,128]{2,1,0:T(8,128)(2,1)S(1)}, bf16[21,16,128]{2,1,0:T(8,128)(2,1)S(1)}, u32[]{:S(2)}, u32[]{:S(2)}) %collective-permute-start.3) | collective-permute-done | bytes 86048 | tf_op jit(solution)/shard_map/ppermute | solution.py:489
  19.0 4.2 %collective-permute-done.4.outer = bf16[21,16,128]{2,1,0:T(8,128)(2,1)S(1)} collective-permute-done((bf16[21,16,128]{2,1,0:T(8,128)(2,1)S(1)}, bf16[21,16,128]{2,1,0:T(8,128)(2,1)S(1)}, u32[]{:S(2)}, u32[]{:S(2)}) %collective-permute-start.4) | collective-permute-done | bytes 86048 | tf_op jit(solution)/shard_map/ppermute | solution.py:490
  23.2 0.0 copy-done
  23.2 0.0 copy-done.1
  23.2 0.0 copy-done.2
  23.2 0.0 copy-done.3
  23.2 0.0 copy-done.4
  23.2 0.0 copy-done.5
  23.2 1.4 %final_part.1 = (f32[6,2,4,256]{3,2,1,0:T(4,128)}, f32[6,2,4,256]{3,2,1,0:T(4,128)}) custom-call(bf16[21,16,128]{2,1,0:T(8,128)(2,1)S(1)} %collective-permute-done.3.inner, bf16[21,16,128]{2,1,0:T(8,128)(2,1)S(1)} %collective-permute-done.4.outer, f32[6,2,4,256]{3,2,1,0:T(4,128)S(1)} %get-tuple-element.34.o_r, f32[6,2,4,256]{3,2,1,0:T(4,128)S(1)} %get-tuple-element.35.o_s, ...), custom_call_target="tpu_custom_call" | custom-call | tf_op jit(solution)/shard_map/final_part/pallas_call | solution.py:491
  (4 shorter events, 0.0 us)
Async XLA Ops:
  2.3 5.1 %collective-permute-start = (bf16[2,64,128]{2,1,0:T(8,128)(2,1)S(1)}, bf16[2,64,128]{2,1,0:T(8,128)(2,1)S(1)}, u32[]{:S(2)}, u32[]{:S(2)}) collective-permute-start(bf16[2,64,128]{2,1,0:T(8,128)(2,1)S(1)} %get-tuple-element.22), channel_id=1, source_target_pairs={{0,16},{4,20},{8,24},{12,28},{16,0},{20,4},{24,8},{28,12},{1,17},{... | collective-permute-start | bytes 98312 | tf_op jit(solution)/shard_map/ppermute | solution.py:463
  7.4 4.3 %collective-permute-start.1 = (bf16[4,64,128]{2,1,0:T(8,128)(2,1)S(1)}, bf16[4,64,128]{2,1,0:T(8,128)(2,1)S(1)}, u32[]{:S(2)}, u32[]{:S(2)}) collective-permute-start(bf16[4,64,128]{2,1,0:T(8,128)(2,1)S(1)} %pad_maximum_fusion), channel_id=1, source_target_pairs={{0,8},{4,12},{8,0},{12,4},{16,24},{20,28},{24,16},{28,20},{1,9},{5... | collective-permute-start | bytes 196616 | tf_op jit(solution)/shard_map/ppermute | solution.py:463
  11.7 1.4 %collective-permute-start.2 = (bf16[8,64,128]{2,1,0:T(8,128)(2,1)S(1)}, bf16[8,64,128]{2,1,0:T(8,128)(2,1)S(1)}, u32[]{:S(2)}, u32[]{:S(2)}) collective-permute-start(bf16[8,64,128]{2,1,0:T(8,128)(2,1)S(1)} %constant_dynamic-update-slice_fusion.mine), channel_id=1, source_target_pairs={{0,4},{4,0},{8,12},{12,8},{16,20},{20,16},{24,28},{28,24},{1,5},{5... | collective-permute-start | bytes 393224 | tf_op jit(solution)/shard_map/ppermute | solution.py:463
  13.2 10.0 %copy-start = (bf16[6,6,2,4,256]{4,3,2,1,0:T(4,128)(2,1)S(1)}, bf16[6,6,2,4,256]{4,3,2,1,0:T(4,128)(2,1)}, u32[]{:S(2)}) copy-start(bf16[6,6,2,4,256]{4,3,2,1,0:T(4,128)(2,1)} %jo_r.1) | copy-start | bytes 442372
  13.2 10.0 %copy-start.1 = (bf16[6,6,2,4,256]{4,3,2,1,0:T(4,128)(2,1)S(1)}, bf16[6,6,2,4,256]{4,3,2,1,0:T(4,128)(2,1)}, u32[]{:S(2)}) copy-start(bf16[6,6,2,4,256]{4,3,2,1,0:T(4,128)(2,1)} %jo_s.1) | copy-start | bytes 442372
  13.2 10.0 %copy-start.2 = (f32[6,2,4,256]{3,2,1,0:T(4,128)S(1)}, f32[6,2,4,256]{3,2,1,0:T(4,128)}, u32[]{:S(2)}) copy-start(f32[6,2,4,256]{3,2,1,0:T(4,128)} %jd_r.1) | copy-start | bytes 147460
  13.2 10.0 %copy-start.3 = (f32[6,2,4,256]{3,2,1,0:T(4,128)S(1)}, f32[6,2,4,256]{3,2,1,0:T(4,128)}, u32[]{:S(2)}) copy-start(f32[6,2,4,256]{3,2,1,0:T(4,128)} %jd_s.1) | copy-start | bytes 147460
  13.2 10.0 %copy-start.4 = (f32[6,2,4,256]{3,2,1,0:T(4,128)S(1)}, f32[6,2,4,256]{3,2,1,0:T(4,128)}, u32[]{:S(2)}) copy-start(f32[6,2,4,256]{3,2,1,0:T(4,128)} %src_r.1) | copy-start | bytes 147460
  13.2 10.0 %copy-start.5 = (f32[6,2,4,256]{3,2,1,0:T(4,128)S(1)}, f32[6,2,4,256]{3,2,1,0:T(4,128)}, u32[]{:S(2)}) copy-start(f32[6,2,4,256]{3,2,1,0:T(4,128)} %src_s.1) | copy-start | bytes 147460
  14.4 4.7 %collective-permute-start.3 = (bf16[21,16,128]{2,1,0:T(8,128)(2,1)S(1)}, bf16[21,16,128]{2,1,0:T(8,128)(2,1)S(1)}, u32[]{:S(2)}, u32[]{:S(2)}) collective-permute-start(bf16[21,16,128]{2,1,0:T(8,128)(2,1)S(1)} %get-tuple-element.32), channel_id=1, source_target_pairs={{0,1},{1,0},{2,3},{3,2},{4,5},{5,4},{6,7},{7,6},{8,9},{9,8},{10,11... | collective-permute-start | bytes 258056 | tf_op jit(solution)/shard_map/ppermute | solution.py:489
  15.9 7.3 %collective-permute-start.4 = (bf16[21,16,128]{2,1,0:T(8,128)(2,1)S(1)}, bf16[21,16,128]{2,1,0:T(8,128)(2,1)S(1)}, u32[]{:S(2)}, u32[]{:S(2)}) collective-permute-start(bf16[21,16,128]{2,1,0:T(8,128)(2,1)S(1)} %get-tuple-element.33), channel_id=1, source_target_pairs={{1,2},{2,1},{5,6},{6,5},{9,10},{10,9},{13,14},{14,13},{17,18},{18,... | collective-permute-start | bytes 258056 | tf_op jit(solution)/shard_map/ppermute | solution.py:490

commit v5 on v4

--- a/solution.py
+++ b/solution.py
@@ -199,7 +199,9 @@
     for at in range(total):
         half, part = divmod(at, total // 2)
         place, i = divmod(part, own_blocks)
-        mask = half + sum(m for n, m in enumerate(masks) if place >> n & 1)
+        mask = half
+        for n, m in enumerate(masks):
+            mask ^= m if place >> n & 1 else 0
         b = jnp.bitwise_xor(here, mask) * own_blocks + i
         whole = other if half else mine
         tiles = [whole[part, n * 16 : n * 16 + 16, :].astype(f32) for n in range(4)]
@@ -460,10 +462,11 @@
     mine, masks = share, []
     mask = members // 2
     while mask > 0:
-        other = lax.ppermute(mine, "circ", [(i, i ^ mask) for i in range(members)])
+        hop = mask | 1
+        other = lax.ppermute(mine, "circ", [(i, i ^ hop) for i in range(members)])
         if mask > 1:
             mine = jnp.concatenate([mine, other], axis=0)
-            masks.append(mask)
+            masks.append(hop)
         mask //= 2
     tiles = jax.ShapeDtypeStruct((total // 2 + var_count * own_blocks + 1, 16, TILE), jnp.bfloat16)
     listed = jax.ShapeDtypeStruct((rows, spread - 2 + own_blocks, 8, TILE), f32)

time: 24.8 us -> 24.7 us (level)
  starting transfers between devices: 4.7 us -> 4.25 us
  waiting for transfers between devices: 14 us -> 14.4 us
    ppermute x3, starting transfers between devices: 0.77 us -> 0.32 us  [per_device(): other = lax.ppermute(mine, 'circ', [(i, i ^ hop) for i in range(members)])]
    ppermute x3, waiting for transfers between devices: 9.12 us -> 9.52 us  [per_device(): other = lax.ppermute(mine, 'circ', [(i, i ^ hop) for i in range(members)])]
where the time goes in v5:
time: 24.7 us; the launch traced here: 24.6 us
  waiting for transfers between devices  14.4 us (58%)
  Pallas kernels  5.11 us (21%)
  starting transfers between devices  4.25 us (17%)
  between operations  0.75 us (3%)
    ppermute x3, waiting for transfers between devices, per_device(): other = lax.ppermute(mine, 'circ', [(i, i ^ hop) for i in range(members)])  9.52 us
    ppermute x1, waiting for transfers between devices, per_device(): outer = lax.ppermute(outer, 'span', far)  4.17 us
    ppermute x1, starting transfers between devices, per_device(): outer = lax.ppermute(outer, 'span', far)  2.37 us
    pallas_call x1, Pallas kernels, per_device(): pl.pallas_call(first_kernel, out_shape=(field, field, jax.ShapeDtypeStruc...  1.63 us
    ppermute x1, starting transfers between devices, per_device(): inner = lax.ppermute(inner, 'span', near)  1.55 us
    pallas_call x1, Pallas kernels, per_device(): pl.pallas_call(third_kernel, out_shape=(field, field), in_specs=[vmem] *...  1.37 us
    pallas_call x1, Pallas kernels, per_device(): pl.pallas_call(functools.partial(second_kernel, masks), out_shape=(field,...  1.17 us
    pallas_call x1, Pallas kernels, per_device(): pl.pallas_call(table_kernel, out_shape=(jax.ShapeDtypeStruct((rows, sprea...  0.93 us
  transfers between devices with their start and end apart: 5, of which 5 were waited for; matrix products, arithmetic and copies ran while one was open for 0% of the time, Pallas kernels for 4%

profile of v5, /device:TPU:28, one launch (start us, length us, event | category | flops | bytes accessed | tf_op | source)
XLA Modules:
  0.0 24.6 jit_solution(11047300104699266671)
XLA Ops:
  0.6 1.6 %local_part.1 = (f32[6,2,4,256]{3,2,1,0:T(4,128)S(1)}, f32[6,2,4,256]{3,2,1,0:T(4,128)S(1)}, bf16[2,64,128]{2,1,0:T(8,128)(2,1)S(1)}, f32[6,2,4,256]{3,2,1,0:T(4...) custom-call(f32[6,2,4,256]{3,2,1,0:T(4,128)} %refs_0_.1, ...), custom_call_target="tpu_custom_call" | custom-call | tf_op jit(solution)/shard_map/local_part/pallas_call | solution.py:436
  2.3 0.1 collective-permute-start
  2.4 5.2 %collective-permute-done = bf16[2,64,128]{2,1,0:T(8,128)(2,1)S(1)} collective-permute-done((bf16[2,64,128]{2,1,0:T(8,128)(2,1)S(1)}, bf16[2,64,128]{2,1,0:T(8,128)(2,1)S(1)}, u32[]{:S(2)}, u32[]{:S(2)}) %collective-permute-start) | collective-permute-done | bytes 32800 | tf_op jit(solution)/shard_map/ppermute | solution.py:466
  7.5 0.1 collective-permute-start.1
  7.6 4.1 %collective-permute-done.1 = bf16[4,64,128]{2,1,0:T(8,128)(2,1)S(1)} collective-permute-done((bf16[4,64,128]{2,1,0:T(8,128)(2,1)S(1)}, bf16[4,64,128]{2,1,0:T(8,128)(2,1)S(1)}, u32[]{:S(2)}, u32[]{:S(2)}) %collective-permute-start.1) | collective-permute-done | bytes 65568 | tf_op jit(solution)/shard_map/ppermute | solution.py:466
  11.7 0.2 collective-permute-start.2
  11.9 0.9 %weight_tables.1 = (f32[2,15,4,128]{3,2,1,0:T(4,128)S(1)}, f32[2,4,8,128]{3,2,1,0:T(8,128)S(1)}) custom-call(f32[2,16,4,128]{3,2,1,0:T(4,128)S(1)} %get-tuple-element.27.weights, s32[2,4,16]{2,1,0:T(4,128)S(1)} %get-tuple-element.28.margin.margin_in, s32[2,16]{1,0:T(2,128)S(1)} %get-tuple-element.29.count), custom_call_target="tpu_custom_call" | custom-call | tf_op jit(solution)/shard_map/weight_tables/pallas_call | solution.py:450
  12.8 0.3 %collective-permute-done.2.other = bf16[8,64,128]{2,1,0:T(8,128)(2,1)S(1)} collective-permute-done((bf16[8,64,128]{2,1,0:T(8,128)(2,1)S(1)}, bf16[8,64,128]{2,1,0:T(8,128)(2,1)S(1)}, u32[]{:S(2)}, u32[]{:S(2)}) %collective-permute-start.2) | collective-permute-done | bytes 131104 | tf_op jit(solution)/shard_map/ppermute | solution.py:466
  13.1 0.0 copy-start
  13.1 0.0 copy-start.1
  13.1 0.0 copy-start.2
  13.1 0.0 copy-start.3
  13.1 0.0 copy-start.4
  13.1 0.0 copy-start.5
  13.2 1.2 %interface_part.1 = (f32[6,2,4,256]{3,2,1,0:T(4,128)S(1)}, f32[6,2,4,256]{3,2,1,0:T(4,128)S(1)}, f32[6,2,4,256]{3,2,1,0:T(4,128)S(1)}, f32[6,2,4,256]{3,2,1,0:T(...) custom-call(bf16[8,64,128]{2,1,0:T(8,128)(2,1)S(1)} %constant_dynami, ...), custom_call_target="tpu_custom_call" | custom-call | tf_op jit(solution)/shard_map/interface_part/pallas_call | solution.py:473
  14.3 1.6 %collective-permute-start.3 = (bf16[21,16,128]{2,1,0:T(8,128)(2,1)S(1)}, bf16[21,16,128]{2,1,0:T(8,128)(2,1)S(1)}, u32[]{:S(2)}, u32[]{:S(2)}) collective-permute-start(bf16[21,16,128]{2,1,0:T(8,128)(2,1)S(1)} %get-tuple-element.32), channel_id=1, source_target_pairs={{0,1},{1,0},{2,3},{3,2},{4,5},{5,4},{6,7},{7,6},{8,9},{9,8},{10,11... | collective-permute-start | bytes 258056 | tf_op jit(solution)/shard_map/ppermute | solution.py:492
  15.9 2.4 %collective-permute-start.4 = (bf16[21,16,128]{2,1,0:T(8,128)(2,1)S(1)}, bf16[21,16,128]{2,1,0:T(8,128)(2,1)S(1)}, u32[]{:S(2)}, u32[]{:S(2)}) collective-permute-start(bf16[21,16,128]{2,1,0:T(8,128)(2,1)S(1)} %get-tuple-element.33), channel_id=1, source_target_pairs={{1,2},{2,1},{5,6},{6,5},{9,10},{10,9},{13,14},{14,13},{17,18},{18,... | collective-permute-start | bytes 258056 | tf_op jit(solution)/shard_map/ppermute | solution.py:493
  18.3 0.7 %collective-permute-done.3.inner = bf16[21,16,128]{2,1,0:T(8,128)(2,1)S(1)} collective-permute-done((bf16[21,16,128]{2,1,0:T(8,128)(2,1)S(1)}, bf16[21,16,128]{2,1,0:T(8,128)(2,1)S(1)}, u32[]{:S(2)}, u32[]{:S(2)}) %collective-permute-start.3) | collective-permute-done | bytes 86048 | tf_op jit(solution)/shard_map/ppermute | solution.py:492
  19.0 4.2 %collective-permute-done.4.outer = bf16[21,16,128]{2,1,0:T(8,128)(2,1)S(1)} collective-permute-done((bf16[21,16,128]{2,1,0:T(8,128)(2,1)S(1)}, bf16[21,16,128]{2,1,0:T(8,128)(2,1)S(1)}, u32[]{:S(2)}, u32[]{:S(2)}) %collective-permute-start.4) | collective-permute-done | bytes 86048 | tf_op jit(solution)/shard_map/ppermute | solution.py:493
  23.2 0.0 copy-done
  23.2 0.0 copy-done.1
  23.2 0.0 copy-done.2
  23.2 0.0 copy-done.3
  23.2 0.0 copy-done.4
  23.2 0.0 copy-done.5
  23.2 1.4 %final_part.1 = (f32[6,2,4,256]{3,2,1,0:T(4,128)}, f32[6,2,4,256]{3,2,1,0:T(4,128)}) custom-call(bf16[21,16,128]{2,1,0:T(8,128)(2,1)S(1)} %collective-permute-done.3.inner, bf16[21,16,128]{2,1,0:T(8,128)(2,1)S(1)} %collective-permute-done.4.outer, f32[6,2,4,256]{3,2,1,0:T(4,128)S(1)} %get-tuple-element.34.o_r, f32[6,2,4,256]{3,2,1,0:T(4,128)S(1)} %get-tuple-element.35.o_s, ...), custom_call_target="tpu_custom_call" | custom-call | tf_op jit(solution)/shard_map/final_part/pallas_call | solution.py:494
  (4 shorter events, 0.0 us)
Async XLA Ops:
  2.3 5.2 %collective-permute-start = (bf16[2,64,128]{2,1,0:T(8,128)(2,1)S(1)}, bf16[2,64,128]{2,1,0:T(8,128)(2,1)S(1)}, u32[]{:S(2)}, u32[]{:S(2)}) collective-permute-start(bf16[2,64,128]{2,1,0:T(8,128)(2,1)S(1)} %get-tuple-element.22), channel_id=1, source_target_pairs={{0,20},{4,16},{8,28},{12,24},{16,4},{20,0},{24,12},{28,8},{1,21},{... | collective-permute-start | bytes 98312 | tf_op jit(solution)/shard_map/ppermute | solution.py:466
  7.5 4.2 %collective-permute-start.1 = (bf16[4,64,128]{2,1,0:T(8,128)(2,1)S(1)}, bf16[4,64,128]{2,1,0:T(8,128)(2,1)S(1)}, u32[]{:S(2)}, u32[]{:S(2)}) collective-permute-start(bf16[4,64,128]{2,1,0:T(8,128)(2,1)S(1)} %pad_maximum_fusion), channel_id=1, source_target_pairs={{0,12},{4,8},{8,4},{12,0},{16,28},{20,24},{24,20},{28,16},{1,13},{... | collective-permute-start | bytes 196616 | tf_op jit(solution)/shard_map/ppermute | solution.py:466
  11.7 1.4 %collective-permute-start.2 = (bf16[8,64,128]{2,1,0:T(8,128)(2,1)S(1)}, bf16[8,64,128]{2,1,0:T(8,128)(2,1)S(1)}, u32[]{:S(2)}, u32[]{:S(2)}) collective-permute-start(bf16[8,64,128]{2,1,0:T(8,128)(2,1)S(1)} %constant_dynamic-update-slice_fusion.mine), channel_id=1, source_target_pairs={{0,4},{4,0},{8,12},{12,8},{16,20},{20,16},{24,28},{28,24},{1,5},{5... | collective-permute-start | bytes 393224 | tf_op jit(solution)/shard_map/ppermute | solution.py:466
  13.1 10.0 %copy-start = (bf16[6,6,2,4,256]{4,3,2,1,0:T(4,128)(2,1)S(1)}, bf16[6,6,2,4,256]{4,3,2,1,0:T(4,128)(2,1)}, u32[]{:S(2)}) copy-start(bf16[6,6,2,4,256]{4,3,2,1,0:T(4,128)(2,1)} %jo_r.1) | copy-start | bytes 442372
  13.1 10.0 %copy-start.1 = (bf16[6,6,2,4,256]{4,3,2,1,0:T(4,128)(2,1)S(1)}, bf16[6,6,2,4,256]{4,3,2,1,0:T(4,128)(2,1)}, u32[]{:S(2)}) copy-start(bf16[6,6,2,4,256]{4,3,2,1,0:T(4,128)(2,1)} %jo_s.1) | copy-start | bytes 442372
  13.1 10.0 %copy-start.2 = (f32[6,2,4,256]{3,2,1,0:T(4,128)S(1)}, f32[6,2,4,256]{3,2,1,0:T(4,128)}, u32[]{:S(2)}) copy-start(f32[6,2,4,256]{3,2,1,0:T(4,128)} %jd_r.1) | copy-start | bytes 147460
  13.1 10.0 %copy-start.3 = (f32[6,2,4,256]{3,2,1,0:T(4,128)S(1)}, f32[6,2,4,256]{3,2,1,0:T(4,128)}, u32[]{:S(2)}) copy-start(f32[6,2,4,256]{3,2,1,0:T(4,128)} %jd_s.1) | copy-start | bytes 147460
  13.1 10.0 %copy-start.4 = (f32[6,2,4,256]{3,2,1,0:T(4,128)S(1)}, f32[6,2,4,256]{3,2,1,0:T(4,128)}, u32[]{:S(2)}) copy-start(f32[6,2,4,256]{3,2,1,0:T(4,128)} %src_r.1) | copy-start | bytes 147460
  13.1 10.0 %copy-start.5 = (f32[6,2,4,256]{3,2,1,0:T(4,128)S(1)}, f32[6,2,4,256]{3,2,1,0:T(4,128)}, u32[]{:S(2)}) copy-start(f32[6,2,4,256]{3,2,1,0:T(4,128)} %src_s.1) | copy-start | bytes 147460
  14.3 4.7 %collective-permute-start.3 = (bf16[21,16,128]{2,1,0:T(8,128)(2,1)S(1)}, bf16[21,16,128]{2,1,0:T(8,128)(2,1)S(1)}, u32[]{:S(2)}, u32[]{:S(2)}) collective-permute-start(bf16[21,16,128]{2,1,0:T(8,128)(2,1)S(1)} %get-tuple-element.32), channel_id=1, source_target_pairs={{0,1},{1,0},{2,3},{3,2},{4,5},{5,4},{6,7},{7,6},{8,9},{9,8},{10,11... | collective-permute-start | bytes 258056 | tf_op jit(solution)/shard_map/ppermute | solution.py:492
  15.9 7.3 %collective-permute-start.4 = (bf16[21,16,128]{2,1,0:T(8,128)(2,1)S(1)}, bf16[21,16,128]{2,1,0:T(8,128)(2,1)S(1)}, u32[]{:S(2)}, u32[]{:S(2)}) collective-permute-start(bf16[21,16,128]{2,1,0:T(8,128)(2,1)S(1)} %get-tuple-element.33), channel_id=1, source_target_pairs={{1,2},{2,1},{5,6},{6,5},{9,10},{10,9},{13,14},{14,13},{17,18},{18,... | collective-permute-start | bytes 258056 | tf_op jit(solution)/shard_map/ppermute | solution.py:493

commit v6 on v5

--- a/solution.py
+++ b/solution.py
@@ -466,6 +466,8 @@
         other = lax.ppermute(mine, "circ", [(i, i ^ hop) for i in range(members)])
         if mask > 1:
             mine = jnp.concatenate([mine, other], axis=0)
+            if not masks:
+                mine, primal_table, pull_table = lax.optimization_barrier((mine, primal_table, pull_table))
             masks.append(hop)
         mask //= 2
     tiles = jax.ShapeDtypeStruct((total // 2 + var_count * own_blocks + 1, 16, TILE), jnp.bfloat16)

time: 24.7 us -> 24.7 us (level)
  no operation moved by 1% of the time
where the time goes in v6:
time: 24.7 us; the launch traced here: 24.6 us
  waiting for transfers between devices  14.4 us (58%)
  Pallas kernels  5.11 us (21%)
  starting transfers between devices  4.25 us (17%)
  between operations  0.74 us (3%)
    ppermute x3, waiting for transfers between devices, per_device(): other = lax.ppermute(mine, 'circ', [(i, i ^ hop) for i in range(members)])  9.53 us
    ppermute x1, waiting for transfers between devices, per_device(): outer = lax.ppermute(outer, 'span', far)  4.18 us
    ppermute x1, starting transfers between devices, per_device(): outer = lax.ppermute(outer, 'span', far)  2.38 us
    pallas_call x1, Pallas kernels, per_device(): pl.pallas_call(first_kernel, out_shape=(field, field, jax.ShapeDtypeStruc...  1.63 us
    ppermute x1, starting transfers between devices, per_device(): inner = lax.ppermute(inner, 'span', near)  1.55 us
    pallas_call x1, Pallas kernels, per_device(): pl.pallas_call(third_kernel, out_shape=(field, field), in_specs=[vmem] *...  1.37 us
    pallas_call x1, Pallas kernels, per_device(): pl.pallas_call(functools.partial(second_kernel, masks), out_shape=(field,...  1.17 us
    pallas_call x1, Pallas kernels, per_device(): pl.pallas_call(table_kernel, out_shape=(jax.ShapeDtypeStruct((rows, sprea...  0.94 us
  transfers between devices with their start and end apart: 5, of which 5 were waited for; matrix products, arithmetic and copies ran while one was open for 0% of the time, Pallas kernels for 4%

profile of v6, /device:TPU:28, one launch (start us, length us, event | category | flops | bytes accessed | tf_op | source)
XLA Modules:
  0.0 24.6 jit_solution(3325706096747916096)
XLA Ops:
  0.6 1.6 %local_part.1 = (f32[6,2,4,256]{3,2,1,0:T(4,128)S(1)}, f32[6,2,4,256]{3,2,1,0:T(4,128)S(1)}, bf16[2,64,128]{2,1,0:T(8,128)(2,1)S(1)}, f32[6,2,4,256]{3,2,1,0:T(4...) custom-call(f32[6,2,4,256]{3,2,1,0:T(4,128)} %refs_0_.1, ...), custom_call_target="tpu_custom_call" | custom-call | tf_op jit(solution)/shard_map/local_part/pallas_call | solution.py:436
  2.3 0.1 collective-permute-start
  2.4 0.9 %weight_tables.1 = (f32[2,15,4,128]{3,2,1,0:T(4,128)S(1)}, f32[2,4,8,128]{3,2,1,0:T(8,128)S(1)}) custom-call(f32[2,16,4,128]{3,2,1,0:T(4,128)S(1)} %get-tuple-element.26.weights, s32[2,4,16]{2,1,0:T(4,128)S(1)} %get-tuple-element.27.margin.margin_in, s32[2,16]{1,0:T(2,128)S(1)} %get-tuple-element.28.count), custom_call_target="tpu_custom_call" | custom-call | tf_op jit(solution)/shard_map/weight_tables/pallas_call | solution.py:450
  3.3 4.2 %collective-permute-done = bf16[2,64,128]{2,1,0:T(8,128)(2,1)S(1)} collective-permute-done((bf16[2,64,128]{2,1,0:T(8,128)(2,1)S(1)}, bf16[2,64,128]{2,1,0:T(8,128)(2,1)S(1)}, u32[]{:S(2)}, u32[]{:S(2)}) %collective-permute-start) | collective-permute-done | bytes 32800 | tf_op jit(solution)/shard_map/ppermute | solution.py:466
  7.5 0.1 collective-permute-start.1
  7.6 4.1 %collective-permute-done.1 = bf16[4,64,128]{2,1,0:T(8,128)(2,1)S(1)} collective-permute-done((bf16[4,64,128]{2,1,0:T(8,128)(2,1)S(1)}, bf16[4,64,128]{2,1,0:T(8,128)(2,1)S(1)}, u32[]{:S(2)}, u32[]{:S(2)}) %collective-permute-start.1) | collective-permute-done | bytes 65568 | tf_op jit(solution)/shard_map/ppermute | solution.py:466
  11.7 0.2 collective-permute-start.2
  11.9 1.2 %collective-permute-done.2.other = bf16[8,64,128]{2,1,0:T(8,128)(2,1)S(1)} collective-permute-done((bf16[8,64,128]{2,1,0:T(8,128)(2,1)S(1)}, bf16[8,64,128]{2,1,0:T(8,128)(2,1)S(1)}, u32[]{:S(2)}, u32[]{:S(2)}) %collective-permute-start.2) | collective-permute-done | bytes 131104 | tf_op jit(solution)/shard_map/ppermute | solution.py:466
  13.1 0.0 copy-start
  13.1 0.0 copy-start.1
  13.1 0.0 copy-start.2
  13.1 0.0 copy-start.3
  13.1 0.0 copy-start.4
  13.1 0.0 copy-start.5
  13.2 1.2 %interface_part.1 = (f32[6,2,4,256]{3,2,1,0:T(4,128)S(1)}, f32[6,2,4,256]{3,2,1,0:T(4,128)S(1)}, f32[6,2,4,256]{3,2,1,0:T(4,128)S(1)}, f32[6,2,4,256]{3,2,1,0:T(...) custom-call(bf16[8,64,128]{2,1,0:T(8,128)(2,1)S(1)} %constant_dynami, ...), custom_call_target="tpu_custom_call" | custom-call | tf_op jit(solution)/shard_map/interface_part/pallas_call | solution.py:475
  14.3 1.6 %collective-permute-start.3 = (bf16[21,16,128]{2,1,0:T(8,128)(2,1)S(1)}, bf16[21,16,128]{2,1,0:T(8,128)(2,1)S(1)}, u32[]{:S(2)}, u32[]{:S(2)}) collective-permute-start(bf16[21,16,128]{2,1,0:T(8,128)(2,1)S(1)} %get-tuple-element.38), channel_id=1, source_target_pairs={{0,1},{1,0},{2,3},{3,2},{4,5},{5,4},{6,7},{7,6},{8,9},{9,8},{10,11... | collective-permute-start | bytes 258056 | tf_op jit(solution)/shard_map/ppermute | solution.py:494
  15.9 2.4 %collective-permute-start.4 = (bf16[21,16,128]{2,1,0:T(8,128)(2,1)S(1)}, bf16[21,16,128]{2,1,0:T(8,128)(2,1)S(1)}, u32[]{:S(2)}, u32[]{:S(2)}) collective-permute-start(bf16[21,16,128]{2,1,0:T(8,128)(2,1)S(1)} %get-tuple-element.39), channel_id=1, source_target_pairs={{1,2},{2,1},{5,6},{6,5},{9,10},{10,9},{13,14},{14,13},{17,18},{18,... | collective-permute-start | bytes 258056 | tf_op jit(solution)/shard_map/ppermute | solution.py:495
  18.3 0.7 %collective-permute-done.3.inner = bf16[21,16,128]{2,1,0:T(8,128)(2,1)S(1)} collective-permute-done((bf16[21,16,128]{2,1,0:T(8,128)(2,1)S(1)}, bf16[21,16,128]{2,1,0:T(8,128)(2,1)S(1)}, u32[]{:S(2)}, u32[]{:S(2)}) %collective-permute-start.3) | collective-permute-done | bytes 86048 | tf_op jit(solution)/shard_map/ppermute | solution.py:494
  19.0 4.2 %collective-permute-done.4.outer = bf16[21,16,128]{2,1,0:T(8,128)(2,1)S(1)} collective-permute-done((bf16[21,16,128]{2,1,0:T(8,128)(2,1)S(1)}, bf16[21,16,128]{2,1,0:T(8,128)(2,1)S(1)}, u32[]{:S(2)}, u32[]{:S(2)}) %collective-permute-start.4) | collective-permute-done | bytes 86048 | tf_op jit(solution)/shard_map/ppermute | solution.py:495
  23.2 0.0 copy-done
  23.2 0.0 copy-done.1
  23.2 0.0 copy-done.2
  23.2 0.0 copy-done.3
  23.2 0.0 copy-done.4
  23.2 0.0 copy-done.5
  23.2 1.4 %final_part.1 = (f32[6,2,4,256]{3,2,1,0:T(4,128)}, f32[6,2,4,256]{3,2,1,0:T(4,128)}) custom-call(bf16[21,16,128]{2,1,0:T(8,128)(2,1)S(1)} %collective-permute-done.3.inner, bf16[21,16,128]{2,1,0:T(8,128)(2,1)S(1)} %collective-permute-done.4.outer, f32[6,2,4,256]{3,2,1,0:T(4,128)S(1)} %get-tuple-element.40.o_r, f32[6,2,4,256]{3,2,1,0:T(4,128)S(1)} %get-tuple-element.41.o_s, ...), custom_call_target="tpu_custom_call" | custom-call | tf_op jit(solution)/shard_map/final_part/pallas_call | solution.py:496
  (3 shorter events, 0.0 us)
Async XLA Ops:
  2.3 5.2 %collective-permute-start = (bf16[2,64,128]{2,1,0:T(8,128)(2,1)S(1)}, bf16[2,64,128]{2,1,0:T(8,128)(2,1)S(1)}, u32[]{:S(2)}, u32[]{:S(2)}) collective-permute-start(bf16[2,64,128]{2,1,0:T(8,128)(2,1)S(1)} %get-tuple-element.25), channel_id=1, source_target_pairs={{0,20},{4,16},{8,28},{12,24},{16,4},{20,0},{24,12},{28,8},{1,21},{... | collective-permute-start | bytes 98312 | tf_op jit(solution)/shard_map/ppermute | solution.py:466
  7.5 4.2 %collective-permute-start.1 = (bf16[4,64,128]{2,1,0:T(8,128)(2,1)S(1)}, bf16[4,64,128]{2,1,0:T(8,128)(2,1)S(1)}, u32[]{:S(2)}, u32[]{:S(2)}) collective-permute-start(bf16[4,64,128]{2,1,0:T(8,128)(2,1)S(1)} %pad_maximum_fusion), channel_id=1, source_target_pairs={{0,12},{4,8},{8,4},{12,0},{16,28},{20,24},{24,20},{28,16},{1,13},{... | collective-permute-start | bytes 196616 | tf_op jit(solution)/shard_map/ppermute | solution.py:466
  11.7 1.4 %collective-permute-start.2 = (bf16[8,64,128]{2,1,0:T(8,128)(2,1)S(1)}, bf16[8,64,128]{2,1,0:T(8,128)(2,1)S(1)}, u32[]{:S(2)}, u32[]{:S(2)}) collective-permute-start(bf16[8,64,128]{2,1,0:T(8,128)(2,1)S(1)} %constant_dynamic-update-slice_fusion.mine), channel_id=1, source_target_pairs={{0,4},{4,0},{8,12},{12,8},{16,20},{20,16},{24,28},{28,24},{1,5},{5... | collective-permute-start | bytes 393224 | tf_op jit(solution)/shard_map/ppermute | solution.py:466
  13.1 10.0 %copy-start = (bf16[6,6,2,4,256]{4,3,2,1,0:T(4,128)(2,1)S(1)}, bf16[6,6,2,4,256]{4,3,2,1,0:T(4,128)(2,1)}, u32[]{:S(2)}) copy-start(bf16[6,6,2,4,256]{4,3,2,1,0:T(4,128)(2,1)} %jo_r.1) | copy-start | bytes 442372
  13.1 10.0 %copy-start.1 = (bf16[6,6,2,4,256]{4,3,2,1,0:T(4,128)(2,1)S(1)}, bf16[6,6,2,4,256]{4,3,2,1,0:T(4,128)(2,1)}, u32[]{:S(2)}) copy-start(bf16[6,6,2,4,256]{4,3,2,1,0:T(4,128)(2,1)} %jo_s.1) | copy-start | bytes 442372
  13.1 10.0 %copy-start.2 = (f32[6,2,4,256]{3,2,1,0:T(4,128)S(1)}, f32[6,2,4,256]{3,2,1,0:T(4,128)}, u32[]{:S(2)}) copy-start(f32[6,2,4,256]{3,2,1,0:T(4,128)} %jd_r.1) | copy-start | bytes 147460
  13.1 10.0 %copy-start.3 = (f32[6,2,4,256]{3,2,1,0:T(4,128)S(1)}, f32[6,2,4,256]{3,2,1,0:T(4,128)}, u32[]{:S(2)}) copy-start(f32[6,2,4,256]{3,2,1,0:T(4,128)} %jd_s.1) | copy-start | bytes 147460
  13.1 10.0 %copy-start.4 = (f32[6,2,4,256]{3,2,1,0:T(4,128)S(1)}, f32[6,2,4,256]{3,2,1,0:T(4,128)}, u32[]{:S(2)}) copy-start(f32[6,2,4,256]{3,2,1,0:T(4,128)} %src_r.1) | copy-start | bytes 147460
  13.1 10.0 %copy-start.5 = (f32[6,2,4,256]{3,2,1,0:T(4,128)S(1)}, f32[6,2,4,256]{3,2,1,0:T(4,128)}, u32[]{:S(2)}) copy-start(f32[6,2,4,256]{3,2,1,0:T(4,128)} %src_s.1) | copy-start | bytes 147460
  14.3 4.6 %collective-permute-start.3 = (bf16[21,16,128]{2,1,0:T(8,128)(2,1)S(1)}, bf16[21,16,128]{2,1,0:T(8,128)(2,1)S(1)}, u32[]{:S(2)}, u32[]{:S(2)}) collective-permute-start(bf16[21,16,128]{2,1,0:T(8,128)(2,1)S(1)} %get-tuple-element.38), channel_id=1, source_target_pairs={{0,1},{1,0},{2,3},{3,2},{4,5},{5,4},{6,7},{7,6},{8,9},{9,8},{10,11... | collective-permute-start | bytes 258056 | tf_op jit(solution)/shard_map/ppermute | solution.py:494
  15.9 7.3 %collective-permute-start.4 = (bf16[21,16,128]{2,1,0:T(8,128)(2,1)S(1)}, bf16[21,16,128]{2,1,0:T(8,128)(2,1)S(1)}, u32[]{:S(2)}, u32[]{:S(2)}) collective-permute-start(bf16[21,16,128]{2,1,0:T(8,128)(2,1)S(1)} %get-tuple-element.39), channel_id=1, source_target_pairs={{1,2},{2,1},{5,6},{6,5},{9,10},{10,9},{13,14},{14,13},{17,18},{18,... | collective-permute-start | bytes 258056 | tf_op jit(solution)/shard_map/ppermute | solution.py:495

commit v7 on v6

--- a/solution.py
+++ b/solution.py
@@ -298,105 +298,143 @@
         to[total // 2 + var_count * own_blocks] = last
 
 
+def corner_of(tile, row, rows):
+    lane = iota((8, TILE), 1)
+    group = lax.rem(lax.shift_right_logical(lane, 3), rows)
+    spot = tile.astype(f32)[0:8]
+    first = jnp.where(group == 0, pltpu.roll(spot, (TILE - 8 * (rows - 1)) % TILE, 1), 0.0)
+    final = jnp.where(group == rows - 1, pltpu.roll(spot, 8 * (rows - 1), 1), 0.0)
+    return jnp.where(row == 0, first, final)
+
+
+def corner_columns(corner, cells):
+    return [
+        lax.dot_general(corner, edge_pick(n, cells), (((0,), (0,)), ((), ())), preferred_element_type=f32)
+        for n in range(2)
+    ]
+
+
+def row_flux(halo, row, margin, q, speeds, scaled, p, pull_table, flux, first_block, own_blocks, total):
+    base = window(margin, row, first_block, total)
+    spread = REACH + own_blocks + 1
+    own = []
+    for t in range(spread - 2 + own_blocks):
+        b = wrapped(base + t, total) if t < spread - 2 else first_block + t - (spread - 2)
+        both = halo[lax.shift_right_logical(b, 1)].astype(f32)
+        beyond = jnp.where(jnp.bitwise_and(b, 1) == 1, both[8:16], both[0:8])
+        moved = flux_of(q[row, t], speeds[row, t], scaled[row, t], p[row, t] + carry * beyond)
+        if t < spread - 2:
+            flux[t] = moved.astype(jnp.bfloat16).astype(f32)
+        else:
+            own.append(moved)
+    pulls = [pull_row(lambda t: flux[t], pull_table, row, slot) for slot in range(own_blocks)]
+    return step_size * jnp.concatenate(pulls, axis=1), -step_size * jnp.concatenate(own, axis=1)
+
+
 def third_kernel(
-    inner, outer, o_r, o_s, h_r, h_s, q, speeds, scaled, p, a_r, a_s, jd_r, jd_s, jo_r, jo_s, src_r, src_s,
-    pull_table, margin_in, away_r, away_s, flux, x_r, x_s, rows_low, rows_high, out_r, out_s, margin, sems,
+    inner, o_r, o_s, h_r, h_s, q, speeds, scaled, p, a_r, a_s, jd_r, jd_s, jo_r, jo_s, src_r, src_s,
+    pull_table, margin_in, part_r, part_s, flux, x_r, x_s, held, margin, sem,
+):
+    fetch = pltpu.make_async_copy(margin_in, margin, sem)
+    fetch.start()
+    var_count, rows, layers, cells = a_r.shape
+    total = margin.shape[2]
+    own_blocks = cells // TILE
+    first_block = lax.axis_index("circ") * own_blocks
+    end = total // 2 + var_count * own_blocks
+    near_row = (1 - jnp.bitwise_and(lax.axis_index("span"), 1)) * (rows - 1)
+    near = [jnp.where(near_row == s, 1.0, 0.0).astype(f32) for s in range(rows)]
+    for x in (x_r, x_s):
+        x[...] = jnp.zeros(x.shape, f32)
+    for v in range(var_count):
+        for i in range(own_blocks):
+            held[v, :, i * TILE : (i + 1) * TILE] = inner[total // 2 + v * own_blocks + i].astype(f32)
+    columns = corner_columns(corner_of(inner[end], near_row, rows), cells)
+    fields = (
+        (o_r, h_r, a_r, jd_r, jo_r, src_r, x_r, part_r),
+        (o_s, h_s, a_s, jd_s, jo_s, src_s, x_s, part_s),
+    )
+    for n, (o, h, a, jd, jo, src, x, part) in enumerate(fields):
+        old = slice(n * layers, (n + 1) * layers)
+        new = slice((2 + n) * layers, (3 + n) * layers)
+        for v in range(var_count):
+            for s in range(rows):
+                x[v * rows + s, 0:layers, :] = o[v, s] + (carry * near[s]) * held[v, old, :]
+        for s in range(rows):
+            state_row = [x[v * rows + s, 0:layers, :] for v in range(var_count)]
+            for v in range(var_count):
+                wide = x[v * rows + s]
+                at = (v * rows + s) * 8
+                beside = (lanes_apart(wide) + layers_apart(wide))[0:layers]
+                beside = beside + h[v, s] + carry * columns[n][at : at + layers]
+                beside = beside + near[s] * (held[v, new, :] + carry * a[v, s])
+                if s > 0:
+                    beside = beside + x[v * rows + s - 1, 0:layers, :]
+                if s < rows - 1:
+                    beside = beside + x[v * rows + s + 1, 0:layers, :]
+                res = jacobian_row(jd, jo, state_row, v, s, var_count) - coupling * beside - src[v, s]
+                part[v, s] = state_row[v] - step_size * res
+    fetch.wait()
+    extra = row_flux(
+        inner, near_row, margin, q, speeds, scaled, p, pull_table, flux, first_block, own_blocks, total
+    )
+    for n, (part, layer) in enumerate(((part_r, layers - 1), (part_s, 0))):
+        at = slice(layer, layer + 1)
+        for v in range(var_count):
+            part[v, near_row, at, :] = part[v, near_row, at, :] + extra[n][v : v + 1]
+
+
+def fourth_kernel(
+    bands, outer, part_r, part_s, q, speeds, scaled, p, a_r, a_s, jd_r, jd_s, jo_r, jo_s, pull_table, margin_in,
+    away_r, away_s, flux, x_r, x_s, held, out_r, out_s, margin, sems,
 ):
     fetch = pltpu.make_async_copy(margin_in, margin, sems.at[0])
     fetch.start()
     var_count, rows, layers, cells = a_r.shape
     total = margin.shape[2]
     own_blocks = cells // TILE
-    spread = REACH + own_blocks + 1
     first_block = lax.axis_index("circ") * own_blocks
-    lane = iota((8, TILE), 1)
-    layer_all = iota((layers, cells), 0)
     end = total // 2 + var_count * own_blocks
+    band = lax.axis_index("span")
+    odd = jnp.bitwise_and(band, 1)
+    far_row = odd * (rows - 1)
+    inside = jnp.logical_and(band > 0, band < bands - 1)
+    live = jnp.where(inside, carry, 0.0).astype(f32)
+    next_row = far_row + 1 - 2 * odd
     for x in (x_r, x_s):
         x[...] = jnp.zeros(x.shape, f32)
-    odd = jnp.bitwise_and(lax.axis_index("span"), 1) == 1
-
-    def low(n):
-        return jnp.where(odd, inner[n].astype(f32), outer[n].astype(f32))
-
-    def high(n):
-        return jnp.where(odd, outer[n].astype(f32), inner[n].astype(f32))
-
-    for side, to in ((low, rows_low), (high, rows_high)):
-        for v in range(var_count):
-            for i in range(own_blocks):
-                to[v, :, i * TILE : (i + 1) * TILE] = side(total // 2 + v * own_blocks + i)
-    ends = [low(end), high(end)]
-    inside = [jnp.concatenate([x[8:9]] * own_blocks, axis=1) for x in ends]
-    group = lax.rem(lax.shift_right_logical(lane, 3), rows)
-    corner = jnp.where(group == 0, pltpu.roll(ends[0][0:8], (TILE - 8 * (rows - 1)) % TILE, 1), 0.0)
-    corner = corner + jnp.where(group == rows - 1, pltpu.roll(ends[1][0:8], 8 * (rows - 1), 1), 0.0)
-    columns = [
-        lax.dot_general(corner, edge_pick(n, cells), (((0,), (0,)), ((), ())), preferred_element_type=f32)
-        for n in range(2)
-    ]
-
-    def halo(side, b):
-        both = side(lax.shift_right_logical(b, 1))
-        return jnp.where(jnp.bitwise_and(b, 1) == 1, both[8:16], both[0:8])
-
-    fields = (
-        (o_r, h_r, a_r, jd_r, jo_r, src_r, x_r, out_r, layers - 1),
-        (o_s, h_s, a_s, jd_s, jo_s, src_s, x_s, out_s, 0),
-    )
-    for n, (o, h, a, jd, jo, src, x, out, layer) in enumerate(fields):
+    for v in range(var_count):
+        for i in range(own_blocks):
+            held[v, :, i * TILE : (i + 1) * TILE] = outer[total // 2 + v * own_blocks + i].astype(f32)
+    columns = corner_columns(corner_of(outer[end], far_row, rows), cells)
+    fields = ((part_r, a_r, jd_r, jo_r, x_r, out_r), (part_s, a_s, jd_s, jo_s, x_s, out_s))
+    for n, (part, a, jd, jo, x, out) in enumerate(fields):
         old = slice(n * layers, (n + 1) * layers)
         new = slice((2 + n) * layers, (3 + n) * layers)
         for v in range(var_count):
+            x[v, 0:layers, :] = carry * held[v, old, :]
+        state_row = [x[v, 0:layers, :] for v in range(var_count)]
+        for v in range(var_count):
+            wide = x[v]
+            beside = (lanes_apart(wide) + layers_apart(wide))[0:layers]
+            for s in (0, rows - 1):
+                at = (v * rows + s) * 8
+                beside = beside + carry * columns[n][at : at + layers]
+            extra = carry * (beside + held[v, new, :]) + (carry * live) * a[v, far_row]
+            gone = jacobian_row(jd, jo, state_row, v, far_row, var_count)
             for s in range(rows):
-                value = o[v, s]
-                if s == 0:
-                    value = value + carry * rows_low[v, old, :]
-                if s == rows - 1:
-                    value = value + carry * rows_high[v, old, :]
-                x[v * rows + s, 0:layers, :] = value
-        for s in range(rows):
-            state_row = [x[v * rows + s, 0:layers, :] for v in range(var_count)]
-            for v in range(var_count):
-                wide = x[v * rows + s]
-                beside = (lanes_apart(wide) + layers_apart(wide))[0:layers]
-                at = (v * rows + s) * 8
-                beside = beside + h[v, s] + carry * columns[n][at : at + layers]
-                if s > 0:
-                    beside = beside + x[v * rows + s - 1, 0:layers, :]
-                else:
-                    beside = beside + inside[0] * (rows_low[v, new, :] + carry * a[v, 0])
-                if s < rows - 1:
-                    beside = beside + x[v * rows + s + 1, 0:layers, :]
-                else:
-                    beside = beside + inside[1] * (rows_high[v, new, :] + carry * a[v, rows - 1])
-                res = jacobian_row(jd, jo, state_row, v, s, var_count) - coupling * beside - src[v, s]
-                out[v, s] = state_row[v] - step_size * res
+                out[v, s] = part[v, s]
+            out[v, far_row] = part[v, far_row] + state_row[v] - step_size * gone + extra
+            out[v, next_row] = part[v, next_row] + carry * state_row[v]
     fetch.wait()
-    extra = []
-    for s in range(rows):
-        base = window(margin, s, first_block, total)
-        own = []
-        for t in range(spread - 2 + own_blocks):
-            b = wrapped(base + t, total) if t < spread - 2 else first_block + t - (spread - 2)
-            adjoint = p[s, t]
-            if s == 0:
-                adjoint = adjoint + carry * halo(low, b)
-            if s == rows - 1:
-                adjoint = adjoint + carry * halo(high, b)
-            moved = flux_of(q[s, t], speeds[s, t], scaled[s, t], adjoint)
-            if t < spread - 2:
-                flux[s, t] = moved.astype(jnp.bfloat16).astype(f32)
-            else:
-                own.append(moved)
-        pulls = [pull_row(lambda t: flux[s, t], pull_table, s, slot) for slot in range(own_blocks)]
-        extra.append((step_size * jnp.concatenate(pulls, axis=1), -step_size * jnp.concatenate(own, axis=1)))
-
+    extra = row_flux(
+        outer, far_row, margin, q, speeds, scaled, p, pull_table, flux, first_block, own_blocks, total
+    )
     copies = []
     for n, (out, away, layer) in enumerate(((out_r, away_r, layers - 1), (out_s, away_s, 0))):
-        for s in range(rows):
-            for v in range(var_count):
-                out[v, s, layer : layer + 1, :] = out[v, s, layer : layer + 1, :] + extra[s][n][v : v + 1]
+        at = slice(layer, layer + 1)
+        for v in range(var_count):
+            out[v, far_row, at, :] = out[v, far_row, at, :] + extra[n][v : v + 1]
         copies.append(pltpu.make_async_copy(out, away, sems.at[1 + n]))
         copies[-1].start()
     for copy in copies:
@@ -493,27 +531,36 @@
     far = [pair for i in range(1, bands - 1, 2) for pair in ((i, i + 1), (i + 1, i))]
     inner = lax.ppermute(inner, "span", near)
     outer = lax.ppermute(outer, "span", far)
-    out_r, out_s = pl.pallas_call(
+    held = pltpu.VMEM((var_count, 4 * layers, cells), f32)
+    flux = pltpu.VMEM((spread - 2, 8, TILE), f32)
+    listing = pltpu.SMEM(margin.shape, jnp.int32)
+    small = pltpu.VMEM((8, 8, cells), f32)
+    part_r, part_s = pl.pallas_call(
         third_kernel,
         out_shape=(field, field),
-        in_specs=[vmem] * 19 + [anywhere],
+        in_specs=[vmem] * 18 + [anywhere],
+        out_specs=(vmem,) * 2,
+        scratch_shapes=[flux, padded, padded, held, listing, pltpu.SemaphoreType.DMA(())],
+        compiler_params=params,
+        name="near_part",
+    )(
+        inner, o_r, o_s, h_r, h_s, q, speeds, scaled, p, a_r, a_s, jac_diag_rotor, jac_diag_stator,
+        jac_off_rotor, jac_off_stator, source_rotor, source_stator, pull_table, margin,
+    )
+    out_r, out_s = pl.pallas_call(
+        functools.partial(fourth_kernel, bands),
+        out_shape=(field, field),
+        in_specs=[vmem] * 14 + [anywhere],
         out_specs=(anywhere,) * 2,
         scratch_shapes=[
-            pltpu.VMEM((rows, spread - 2, 8, TILE), f32),
-            padded,
-            padded,
-            pltpu.VMEM((var_count, 4 * layers, cells), f32),
-            pltpu.VMEM((var_count, 4 * layers, cells), f32),
-            pltpu.VMEM(field.shape, f32),
-            pltpu.VMEM(field.shape, f32),
-            pltpu.SMEM(margin.shape, jnp.int32),
+            flux, small, small, held, pltpu.VMEM(field.shape, f32), pltpu.VMEM(field.shape, f32), listing,
             pltpu.SemaphoreType.DMA((3,)),
         ],
         compiler_params=params,
         name="final_part",
     )(
-        inner, outer, o_r, o_s, h_r, h_s, q, speeds, scaled, p, a_r, a_s, jac_diag_rotor, jac_diag_stator,
-        jac_off_rotor, jac_off_stator, source_rotor, source_stator, pull_table, margin,
+        outer, part_r, part_s, q, speeds, scaled, p, a_r, a_s, jac_diag_rotor, jac_diag_stator,
+        jac_off_rotor, jac_off_stator, pull_table, margin,
     )
     return (out_r, out_s)
 

time: 24.7 us -> 24.6 us (level)
  waiting for transfers between devices: 14.4 us -> 13.5 us
  Pallas kernels: 5.11 us -> 5.98 us
    pallas_call x0 -> x1, Pallas kernels: none -> 1.34 us  [per_device(): pl.pallas_call(functools.partial(fourth_kernel, bands), out_shape=(field,...]
    ppermute x1, waiting for transfers between devices: 4.18 us -> 3.23 us  [per_device(): outer = lax.ppermute(outer, 'span', far)]
    pallas_call x1, Pallas kernels: 1.37 us -> 0.9 us  [per_device(): pl.pallas_call(third_kernel, out_shape=(field, field), in_specs=[vmem] *...]
  transfers between devices with their start and end apart: 5 -> 5, of which waited for: 5 -> 5; matrix products, arithmetic and copies ran while one was open for 0% -> 0% of each run, Pallas kernels for 4% -> 7%
where the time goes in v7:
time: 24.6 us; the launch traced here: 24.5 us
  waiting for transfers between devices  13.5 us (55%)
  Pallas kernels  5.98 us (24%)
  starting transfers between devices  4.25 us (17%)
  between operations  0.75 us (3%)
    ppermute x3, waiting for transfers between devices, per_device(): other = lax.ppermute(mine, 'circ', [(i, i ^ hop) for i in range(members)])  9.53 us
    ppermute x1, waiting for transfers between devices, per_device(): outer = lax.ppermute(outer, 'span', far)  3.23 us
    ppermute x1, starting transfers between devices, per_device(): outer = lax.ppermute(outer, 'span', far)  2.38 us
    pallas_call x1, Pallas kernels, per_device(): pl.pallas_call(first_kernel, out_shape=(field, field, jax.ShapeDtypeStruc...  1.64 us
    ppermute x1, starting transfers between devices, per_device(): inner = lax.ppermute(inner, 'span', near)  1.55 us
    pallas_call x1, Pallas kernels, per_device(): pl.pallas_call(functools.partial(fourth_kernel, bands), out_shape=(field,...  1.34 us
    pallas_call x1, Pallas kernels, per_device(): pl.pallas_call(functools.partial(second_kernel, masks), out_shape=(field,...  1.17 us
    pallas_call x1, Pallas kernels, per_device(): pl.pallas_call(table_kernel, out_shape=(jax.ShapeDtypeStruct((rows, sprea...  0.94 us
  transfers between devices with their start and end apart: 5, of which 5 were waited for; matrix products, arithmetic and copies ran while one was open for 0% of the time, Pallas kernels for 7%

profile of v7, /device:TPU:28, one launch (start us, length us, event | category | flops | bytes accessed | tf_op | source)
XLA Modules:
  0.0 24.5 jit_solution(603486572039732719)
XLA Ops:
  0.6 1.6 %local_part.1 = (f32[6,2,4,256]{3,2,1,0:T(4,128)S(1)}, f32[6,2,4,256]{3,2,1,0:T(4,128)S(1)}, bf16[2,64,128]{2,1,0:T(8,128)(2,1)S(1)}, f32[6,2,4,256]{3,2,1,0:T(4...) custom-call(f32[6,2,4,256]{3,2,1,0:T(4,128)} %refs_0_.1, ...), custom_call_target="tpu_custom_call" | custom-call | tf_op jit(solution)/shard_map/local_part/pallas_call | solution.py:474
  2.3 0.1 collective-permute-start
  2.4 0.9 %weight_tables.1 = (f32[2,15,4,128]{3,2,1,0:T(4,128)S(1)}, f32[2,4,8,128]{3,2,1,0:T(8,128)S(1)}) custom-call(f32[2,16,4,128]{3,2,1,0:T(4,128)S(1)} %get-tuple-element.28.weights, s32[2,4,16]{2,1,0:T(4,128)S(1)} %get-tuple-element.29.margin.margin_in, s32[2,16]{1,0:T(2,128)S(1)} %get-tuple-element.30.count), custom_call_target="tpu_custom_call" | custom-call | tf_op jit(solution)/shard_map/weight_tables/pallas_call | solution.py:488
  3.3 4.2 %collective-permute-done = bf16[2,64,128]{2,1,0:T(8,128)(2,1)S(1)} collective-permute-done((bf16[2,64,128]{2,1,0:T(8,128)(2,1)S(1)}, bf16[2,64,128]{2,1,0:T(8,128)(2,1)S(1)}, u32[]{:S(2)}, u32[]{:S(2)}) %collective-permute-start) | collective-permute-done | bytes 32800 | tf_op jit(solution)/shard_map/ppermute | solution.py:504
  7.5 0.1 collective-permute-start.1
  7.6 4.1 %collective-permute-done.1 = bf16[4,64,128]{2,1,0:T(8,128)(2,1)S(1)} collective-permute-done((bf16[4,64,128]{2,1,0:T(8,128)(2,1)S(1)}, bf16[4,64,128]{2,1,0:T(8,128)(2,1)S(1)}, u32[]{:S(2)}, u32[]{:S(2)}) %collective-permute-start.1) | collective-permute-done | bytes 65568 | tf_op jit(solution)/shard_map/ppermute | solution.py:504
  11.7 0.2 collective-permute-start.2
  11.9 1.2 %collective-permute-done.2.other = bf16[8,64,128]{2,1,0:T(8,128)(2,1)S(1)} collective-permute-done((bf16[8,64,128]{2,1,0:T(8,128)(2,1)S(1)}, bf16[8,64,128]{2,1,0:T(8,128)(2,1)S(1)}, u32[]{:S(2)}, u32[]{:S(2)}) %collective-permute-start.2) | collective-permute-done | bytes 131104 | tf_op jit(solution)/shard_map/ppermute | solution.py:504
  13.1 0.0 copy-start
  13.1 0.0 copy-start.1
  13.1 0.0 copy-start.2
  13.1 0.0 copy-start.3
  13.1 0.0 copy-start.4
  13.1 0.0 copy-start.5
  13.2 1.2 %interface_part.1 = (f32[6,2,4,256]{3,2,1,0:T(4,128)S(1)}, f32[6,2,4,256]{3,2,1,0:T(4,128)S(1)}, f32[6,2,4,256]{3,2,1,0:T(4,128)S(1)}, f32[6,2,4,256]{3,2,1,0:T(...) custom-call(bf16[8,64,128]{2,1,0:T(8,128)(2,1)S(1)} %constant_dynami, ...), custom_call_target="tpu_custom_call" | custom-call | tf_op jit(solution)/shard_map/interface_part/pallas_call | solution.py:513
  14.3 1.6 %collective-permute-start.4 = (bf16[21,16,128]{2,1,0:T(8,128)(2,1)S(1)}, bf16[21,16,128]{2,1,0:T(8,128)(2,1)S(1)}, u32[]{:S(2)}, u32[]{:S(2)}) collective-permute-start(bf16[21,16,128]{2,1,0:T(8,128)(2,1)S(1)} %get-tuple-element.41), channel_id=1, source_target_pairs={{0,1},{1,0},{2,3},{3,2},{4,5},{5,4},{6,7},{7,6},{8,9},{9,8},{10,11... | collective-permute-start | bytes 258056 | tf_op jit(solution)/shard_map/ppermute | solution.py:532
  15.9 2.4 %collective-permute-start.3 = (bf16[21,16,128]{2,1,0:T(8,128)(2,1)S(1)}, bf16[21,16,128]{2,1,0:T(8,128)(2,1)S(1)}, u32[]{:S(2)}, u32[]{:S(2)}) collective-permute-start(bf16[21,16,128]{2,1,0:T(8,128)(2,1)S(1)} %get-tuple-element.40), channel_id=1, source_target_pairs={{1,2},{2,1},{5,6},{6,5},{9,10},{10,9},{13,14},{14,13},{17,18},{18,... | collective-permute-start | bytes 258056 | tf_op jit(solution)/shard_map/ppermute | solution.py:533
  18.3 0.7 %collective-permute-done.4.inner = bf16[21,16,128]{2,1,0:T(8,128)(2,1)S(1)} collective-permute-done((bf16[21,16,128]{2,1,0:T(8,128)(2,1)S(1)}, bf16[21,16,128]{2,1,0:T(8,128)(2,1)S(1)}, u32[]{:S(2)}, u32[]{:S(2)}) %collective-permute-start.4) | collective-permute-done | bytes 86048 | tf_op jit(solution)/shard_map/ppermute | solution.py:532
  19.0 0.0 copy-done
  19.0 0.0 copy-done.1
  19.0 0.0 copy-done.2
  19.0 0.0 copy-done.3
  19.0 0.0 copy-done.4
  19.0 0.0 copy-done.5
  19.0 0.9 %near_part.1 = (f32[6,2,4,256]{3,2,1,0:T(4,128)S(1)}, f32[6,2,4,256]{3,2,1,0:T(4,128)S(1)}) custom-call(bf16[21,16,128]{2,1,0:T(8,128)(2,1)S(1)} %collective-permute-done.4.inner, f32[6,2,4,256]{3,2,1,0:T(4,128)S(1)} %get-tuple-element.42.o_r, f32[6,2,4,256]{3,2,1,0:T(4,128)S(1)} %get-tuple-element.43.o_s, f32[6,2,4,256]{3,2,1,0:T(4,128)S(1)} %get-tuple-element.44.h_r, ...), custom_call_target="tpu_custom_call" | custom-call | tf_op jit(solution)/shard_map/near_part/pallas_call | solution.py:538
  19.9 3.2 %collective-permute-done.3.outer = bf16[21,16,128]{2,1,0:T(8,128)(2,1)S(1)} collective-permute-done((bf16[21,16,128]{2,1,0:T(8,128)(2,1)S(1)}, bf16[21,16,128]{2,1,0:T(8,128)(2,1)S(1)}, u32[]{:S(2)}, u32[]{:S(2)}) %collective-permute-start.3) | collective-permute-done | bytes 86048 | tf_op jit(solution)/shard_map/ppermute | solution.py:533
  23.2 1.3 %final_part.1 = (f32[6,2,4,256]{3,2,1,0:T(4,128)}, f32[6,2,4,256]{3,2,1,0:T(4,128)}) custom-call(bf16[21,16,128]{2,1,0:T(8,128)(2,1)S(1)} %collective-permute-done.3.outer, f32[6,2,4,256]{3,2,1,0:T(4,128)S(1)} %get-tuple-element.50.part_r, f32[6,2,4,256]{3,2,1,0:T(4,128)S(1)} %get-tuple-element.51.part_s, f32[2,11,8,128]{3,2,1,0:T(8,128)S(1)} %get-tuple-element.46.q, ...), custom_call_target="tpu_custom_call" | custom-call | tf_op jit(solution)/shard_map/final_part/pallas_call | solution.py:550
  (3 shorter events, 0.0 us)
Async XLA Ops:
  2.3 5.2 %collective-permute-start = (bf16[2,64,128]{2,1,0:T(8,128)(2,1)S(1)}, bf16[2,64,128]{2,1,0:T(8,128)(2,1)S(1)}, u32[]{:S(2)}, u32[]{:S(2)}) collective-permute-start(bf16[2,64,128]{2,1,0:T(8,128)(2,1)S(1)} %get-tuple-element.27), channel_id=1, source_target_pairs={{0,20},{4,16},{8,28},{12,24},{16,4},{20,0},{24,12},{28,8},{1,21},{... | collective-permute-start | bytes 98312 | tf_op jit(solution)/shard_map/ppermute | solution.py:504
  7.5 4.2 %collective-permute-start.1 = (bf16[4,64,128]{2,1,0:T(8,128)(2,1)S(1)}, bf16[4,64,128]{2,1,0:T(8,128)(2,1)S(1)}, u32[]{:S(2)}, u32[]{:S(2)}) collective-permute-start(bf16[4,64,128]{2,1,0:T(8,128)(2,1)S(1)} %pad_maximum_fusion), channel_id=1, source_target_pairs={{0,12},{4,8},{8,4},{12,0},{16,28},{20,24},{24,20},{28,16},{1,13},{... | collective-permute-start | bytes 196616 | tf_op jit(solution)/shard_map/ppermute | solution.py:504
  11.7 1.4 %collective-permute-start.2 = (bf16[8,64,128]{2,1,0:T(8,128)(2,1)S(1)}, bf16[8,64,128]{2,1,0:T(8,128)(2,1)S(1)}, u32[]{:S(2)}, u32[]{:S(2)}) collective-permute-start(bf16[8,64,128]{2,1,0:T(8,128)(2,1)S(1)} %constant_dynamic-update-slice_fusion.mine), channel_id=1, source_target_pairs={{0,4},{4,0},{8,12},{12,8},{16,20},{20,16},{24,28},{28,24},{1,5},{5... | collective-permute-start | bytes 393224 | tf_op jit(solution)/shard_map/ppermute | solution.py:504
  13.1 5.9 %copy-start = (bf16[6,6,2,4,256]{4,3,2,1,0:T(4,128)(2,1)S(1)}, bf16[6,6,2,4,256]{4,3,2,1,0:T(4,128)(2,1)}, u32[]{:S(2)}) copy-start(bf16[6,6,2,4,256]{4,3,2,1,0:T(4,128)(2,1)} %jo_r.3) | copy-start | bytes 442372
  13.1 5.9 %copy-start.1 = (bf16[6,6,2,4,256]{4,3,2,1,0:T(4,128)(2,1)S(1)}, bf16[6,6,2,4,256]{4,3,2,1,0:T(4,128)(2,1)}, u32[]{:S(2)}) copy-start(bf16[6,6,2,4,256]{4,3,2,1,0:T(4,128)(2,1)} %jo_s.3) | copy-start | bytes 442372
  13.1 5.9 %copy-start.2 = (f32[6,2,4,256]{3,2,1,0:T(4,128)S(1)}, f32[6,2,4,256]{3,2,1,0:T(4,128)}, u32[]{:S(2)}) copy-start(f32[6,2,4,256]{3,2,1,0:T(4,128)} %jd_r.3) | copy-start | bytes 147460
  13.1 5.9 %copy-start.3 = (f32[6,2,4,256]{3,2,1,0:T(4,128)S(1)}, f32[6,2,4,256]{3,2,1,0:T(4,128)}, u32[]{:S(2)}) copy-start(f32[6,2,4,256]{3,2,1,0:T(4,128)} %jd_s.3) | copy-start | bytes 147460
  13.1 5.9 %copy-start.4 = (f32[6,2,4,256]{3,2,1,0:T(4,128)S(1)}, f32[6,2,4,256]{3,2,1,0:T(4,128)}, u32[]{:S(2)}) copy-start(f32[6,2,4,256]{3,2,1,0:T(4,128)} %src_r.1) | copy-start | bytes 147460
  13.1 5.9 %copy-start.5 = (f32[6,2,4,256]{3,2,1,0:T(4,128)S(1)}, f32[6,2,4,256]{3,2,1,0:T(4,128)}, u32[]{:S(2)}) copy-start(f32[6,2,4,256]{3,2,1,0:T(4,128)} %src_s.1) | copy-start | bytes 147460
  14.3 4.6 %collective-permute-start.4 = (bf16[21,16,128]{2,1,0:T(8,128)(2,1)S(1)}, bf16[21,16,128]{2,1,0:T(8,128)(2,1)S(1)}, u32[]{:S(2)}, u32[]{:S(2)}) collective-permute-start(bf16[21,16,128]{2,1,0:T(8,128)(2,1)S(1)} %get-tuple-element.41), channel_id=1, source_target_pairs={{0,1},{1,0},{2,3},{3,2},{4,5},{5,4},{6,7},{7,6},{8,9},{9,8},{10,11... | collective-permute-start | bytes 258056 | tf_op jit(solution)/shard_map/ppermute | solution.py:532
  15.9 7.3 %collective-permute-start.3 = (bf16[21,16,128]{2,1,0:T(8,128)(2,1)S(1)}, bf16[21,16,128]{2,1,0:T(8,128)(2,1)S(1)}, u32[]{:S(2)}, u32[]{:S(2)}) collective-permute-start(bf16[21,16,128]{2,1,0:T(8,128)(2,1)S(1)} %get-tuple-element.40), channel_id=1, source_target_pairs={{1,2},{2,1},{5,6},{6,5},{9,10},{10,9},{13,14},{14,13},{17,18},{18,... | collective-permute-start | bytes 258056 | tf_op jit(solution)/shard_map/ppermute | solution.py:533

commit v8 on v7

--- a/solution.py
+++ b/solution.py
@@ -314,8 +314,7 @@
     ]
 
 
-def row_flux(halo, row, margin, q, speeds, scaled, p, pull_table, flux, first_block, own_blocks, total):
-    base = window(margin, row, first_block, total)
+def row_flux(halo, row, base, q, speeds, scaled, p, pull_table, flux, first_block, own_blocks, total):
     spread = REACH + own_blocks + 1
     own = []
     for t in range(spread - 2 + own_blocks):
@@ -333,7 +332,7 @@
 
 def third_kernel(
     inner, o_r, o_s, h_r, h_s, q, speeds, scaled, p, a_r, a_s, jd_r, jd_s, jo_r, jo_s, src_r, src_s,
-    pull_table, margin_in, part_r, part_s, flux, x_r, x_s, held, margin, sem,
+    pull_table, margin_in, part_r, part_s, start, flux, x_r, x_s, held, margin, sem,
 ):
     fetch = pltpu.make_async_copy(margin_in, margin, sem)
     fetch.start()
@@ -376,8 +375,10 @@
                 part[v, s] = state_row[v] - step_size * res
     fetch.wait()
     extra = row_flux(
-        inner, near_row, margin, q, speeds, scaled, p, pull_table, flux, first_block, own_blocks, total
-    )
+        inner, near_row, window(margin, near_row, first_block, total), q, speeds, scaled, p, pull_table, flux,
+        first_block, own_blocks, total,
+    )
+    start[...] = jnp.full((8, TILE), window(margin, rows - 1 - near_row, first_block, total)).astype(f32)
     for n, (part, layer) in enumerate(((part_r, layers - 1), (part_s, 0))):
         at = slice(layer, layer + 1)
         for v in range(var_count):
@@ -385,13 +386,13 @@
 
 
 def fourth_kernel(
-    bands, outer, part_r, part_s, q, speeds, scaled, p, a_r, a_s, jd_r, jd_s, jo_r, jo_s, pull_table, margin_in,
-    away_r, away_s, flux, x_r, x_s, held, out_r, out_s, margin, sems,
+    bands, outer, part_r, part_s, q, speeds, scaled, p, a_r, a_s, jd_r, jd_s, jo_r, jo_s, pull_table, start,
+    away_r, away_s, flux, x_r, x_s, held, out_r, out_s, sems,
 ):
-    fetch = pltpu.make_async_copy(margin_in, margin, sems.at[0])
-    fetch.start()
     var_count, rows, layers, cells = a_r.shape
-    total = margin.shape[2]
+    own_blocks = cells // TILE
+    total = 2 * (outer.shape[0] - 1 - var_count * own_blocks)
+    base = jnp.max(start[...]).astype(jnp.int32)
     own_blocks = cells // TILE
     first_block = lax.axis_index("circ") * own_blocks
     end = total // 2 + var_count * own_blocks
@@ -426,16 +427,15 @@
                 out[v, s] = part[v, s]
             out[v, far_row] = part[v, far_row] + state_row[v] - step_size * gone + extra
             out[v, next_row] = part[v, next_row] + carry * state_row[v]
-    fetch.wait()
     extra = row_flux(
-        outer, far_row, margin, q, speeds, scaled, p, pull_table, flux, first_block, own_blocks, total
+        outer, far_row, base, q, speeds, scaled, p, pull_table, flux, first_block, own_blocks, total
     )
     copies = []
     for n, (out, away, layer) in enumerate(((out_r, away_r, layers - 1), (out_s, away_s, 0))):
         at = slice(layer, layer + 1)
         for v in range(var_count):
             out[v, far_row, at, :] = out[v, far_row, at, :] + extra[n][v : v + 1]
-        copies.append(pltpu.make_async_copy(out, away, sems.at[1 + n]))
+        copies.append(pltpu.make_async_copy(out, away, sems.at[n]))
         copies[-1].start()
     for copy in copies:
         copy.wait()
@@ -535,11 +535,11 @@
     flux = pltpu.VMEM((spread - 2, 8, TILE), f32)
     listing = pltpu.SMEM(margin.shape, jnp.int32)
     small = pltpu.VMEM((8, 8, cells), f32)
-    part_r, part_s = pl.pallas_call(
+    part_r, part_s, start = pl.pallas_call(
         third_kernel,
-        out_shape=(field, field),
+        out_shape=(field, field, jax.ShapeDtypeStruct((8, TILE), f32)),
         in_specs=[vmem] * 18 + [anywhere],
-        out_specs=(vmem,) * 2,
+        out_specs=(vmem,) * 3,
         scratch_shapes=[flux, padded, padded, held, listing, pltpu.SemaphoreType.DMA(())],
         compiler_params=params,
         name="near_part",
@@ -550,17 +550,17 @@
     out_r, out_s = pl.pallas_call(
         functools.partial(fourth_kernel, bands),
         out_shape=(field, field),
-        in_specs=[vmem] * 14 + [anywhere],
+        in_specs=[vmem] * 15,
         out_specs=(anywhere,) * 2,
         scratch_shapes=[
-            flux, small, small, held, pltpu.VMEM(field.shape, f32), pltpu.VMEM(field.shape, f32), listing,
-            pltpu.SemaphoreType.DMA((3,)),
+            flux, small, small, held, pltpu.VMEM(field.shape, f32), pltpu.VMEM(field.shape, f32),
+            pltpu.SemaphoreType.DMA((2,)),
         ],
         compiler_params=params,
         name="final_part",
     )(
         outer, part_r, part_s, q, speeds, scaled, p, a_r, a_s, jac_diag_rotor, jac_diag_stator,
-        jac_off_rotor, jac_off_stator, pull_table, margin,
+        jac_off_rotor, jac_off_stator, pull_table, start,
     )
     return (out_r, out_s)
 

time: 24.6 us -> 24.3 us (0.988)
  Pallas kernels: 5.98 us -> 5.67 us
    pallas_call x1, Pallas kernels: 1.34 us -> 1.02 us  [per_device(): pl.pallas_call(functools.partial(fourth_kernel, bands), out_shape=(field,...]
  transfers between devices with their start and end apart: 5 -> 5, of which waited for: 5 -> 5; matrix products, arithmetic and copies ran while one was open for 0% -> 0% of each run, Pallas kernels for 7% -> 8%
where the time goes in v8:
time: 24.3 us; the launch traced here: 24.2 us
  waiting for transfers between devices  13.4 us (55%)
  Pallas kernels  5.67 us (23%)
  starting transfers between devices  4.25 us (17%)
  between operations  0.75 us (3%)
    ppermute x3, waiting for transfers between devices, per_device(): other = lax.ppermute(mine, 'circ', [(i, i ^ hop) for i in range(members)])  9.53 us
    ppermute x1, waiting for transfers between devices, per_device(): outer = lax.ppermute(outer, 'span', far)  3.22 us
    ppermute x1, starting transfers between devices, per_device(): outer = lax.ppermute(outer, 'span', far)  2.38 us
    pallas_call x1, Pallas kernels, per_device(): pl.pallas_call(first_kernel, out_shape=(field, field, jax.ShapeDtypeStruc...  1.63 us
    ppermute x1, starting transfers between devices, per_device(): inner = lax.ppermute(inner, 'span', near)  1.55 us
    pallas_call x1, Pallas kernels, per_device(): pl.pallas_call(functools.partial(second_kernel, masks), out_shape=(field,...  1.17 us
    pallas_call x1, Pallas kernels, per_device(): pl.pallas_call(functools.partial(fourth_kernel, bands), out_shape=(field,...  1.02 us
    pallas_call x1, Pallas kernels, per_device(): pl.pallas_call(table_kernel, out_shape=(jax.ShapeDtypeStruct((rows, sprea...  0.94 us
  transfers between devices with their start and end apart: 5, of which 5 were waited for; matrix products, arithmetic and copies ran while one was open for 0% of the time, Pallas kernels for 8%

profile of v8, /device:TPU:28, one launch (start us, length us, event | category | flops | bytes accessed | tf_op | source)
XLA Modules:
  0.0 24.2 jit_solution(4503530641596501471)
XLA Ops:
  0.6 1.6 %local_part.1 = (f32[6,2,4,256]{3,2,1,0:T(4,128)S(1)}, f32[6,2,4,256]{3,2,1,0:T(4,128)S(1)}, bf16[2,64,128]{2,1,0:T(8,128)(2,1)S(1)}, f32[6,2,4,256]{3,2,1,0:T(4...) custom-call(f32[6,2,4,256]{3,2,1,0:T(4,128)} %refs_0_.1, ...), custom_call_target="tpu_custom_call" | custom-call | tf_op jit(solution)/shard_map/local_part/pallas_call | solution.py:474
  2.3 0.1 collective-permute-start
  2.4 0.9 %weight_tables.1 = (f32[2,15,4,128]{3,2,1,0:T(4,128)S(1)}, f32[2,4,8,128]{3,2,1,0:T(8,128)S(1)}) custom-call(f32[2,16,4,128]{3,2,1,0:T(4,128)S(1)} %get-tuple-element.29.weights, s32[2,4,16]{2,1,0:T(4,128)S(1)} %get-tuple-element.30.margin.margin_in, s32[2,16]{1,0:T(2,128)S(1)} %get-tuple-element.31.count), custom_call_target="tpu_custom_call" | custom-call | tf_op jit(solution)/shard_map/weight_tables/pallas_call | solution.py:488
  3.3 4.2 %collective-permute-done = bf16[2,64,128]{2,1,0:T(8,128)(2,1)S(1)} collective-permute-done((bf16[2,64,128]{2,1,0:T(8,128)(2,1)S(1)}, bf16[2,64,128]{2,1,0:T(8,128)(2,1)S(1)}, u32[]{:S(2)}, u32[]{:S(2)}) %collective-permute-start) | collective-permute-done | bytes 32800 | tf_op jit(solution)/shard_map/ppermute | solution.py:504
  7.5 0.1 collective-permute-start.1
  7.6 4.1 %collective-permute-done.1 = bf16[4,64,128]{2,1,0:T(8,128)(2,1)S(1)} collective-permute-done((bf16[4,64,128]{2,1,0:T(8,128)(2,1)S(1)}, bf16[4,64,128]{2,1,0:T(8,128)(2,1)S(1)}, u32[]{:S(2)}, u32[]{:S(2)}) %collective-permute-start.1) | collective-permute-done | bytes 65568 | tf_op jit(solution)/shard_map/ppermute | solution.py:504
  11.7 0.2 collective-permute-start.2
  11.9 1.2 %collective-permute-done.2.other = bf16[8,64,128]{2,1,0:T(8,128)(2,1)S(1)} collective-permute-done((bf16[8,64,128]{2,1,0:T(8,128)(2,1)S(1)}, bf16[8,64,128]{2,1,0:T(8,128)(2,1)S(1)}, u32[]{:S(2)}, u32[]{:S(2)}) %collective-permute-start.2) | collective-permute-done | bytes 131104 | tf_op jit(solution)/shard_map/ppermute | solution.py:504
  13.1 0.0 copy-start
  13.1 0.0 copy-start.1
  13.1 0.0 copy-start.2
  13.1 0.0 copy-start.3
  13.1 0.0 copy-start.4
  13.1 0.0 copy-start.5
  13.2 1.2 %interface_part.1 = (f32[6,2,4,256]{3,2,1,0:T(4,128)S(1)}, f32[6,2,4,256]{3,2,1,0:T(4,128)S(1)}, f32[6,2,4,256]{3,2,1,0:T(4,128)S(1)}, f32[6,2,4,256]{3,2,1,0:T(...) custom-call(bf16[8,64,128]{2,1,0:T(8,128)(2,1)S(1)} %constant_dynami, ...), custom_call_target="tpu_custom_call" | custom-call | tf_op jit(solution)/shard_map/interface_part/pallas_call | solution.py:513
  14.3 1.6 %collective-permute-start.4 = (bf16[21,16,128]{2,1,0:T(8,128)(2,1)S(1)}, bf16[21,16,128]{2,1,0:T(8,128)(2,1)S(1)}, u32[]{:S(2)}, u32[]{:S(2)}) collective-permute-start(bf16[21,16,128]{2,1,0:T(8,128)(2,1)S(1)} %get-tuple-element.42), channel_id=1, source_target_pairs={{0,1},{1,0},{2,3},{3,2},{4,5},{5,4},{6,7},{7,6},{8,9},{9,8},{10,11... | collective-permute-start | bytes 258056 | tf_op jit(solution)/shard_map/ppermute | solution.py:532
  15.9 2.4 %collective-permute-start.3 = (bf16[21,16,128]{2,1,0:T(8,128)(2,1)S(1)}, bf16[21,16,128]{2,1,0:T(8,128)(2,1)S(1)}, u32[]{:S(2)}, u32[]{:S(2)}) collective-permute-start(bf16[21,16,128]{2,1,0:T(8,128)(2,1)S(1)} %get-tuple-element.41), channel_id=1, source_target_pairs={{1,2},{2,1},{5,6},{6,5},{9,10},{10,9},{13,14},{14,13},{17,18},{18,... | collective-permute-start | bytes 258056 | tf_op jit(solution)/shard_map/ppermute | solution.py:533
  18.3 0.7 %collective-permute-done.4.inner = bf16[21,16,128]{2,1,0:T(8,128)(2,1)S(1)} collective-permute-done((bf16[21,16,128]{2,1,0:T(8,128)(2,1)S(1)}, bf16[21,16,128]{2,1,0:T(8,128)(2,1)S(1)}, u32[]{:S(2)}, u32[]{:S(2)}) %collective-permute-start.4) | collective-permute-done | bytes 86048 | tf_op jit(solution)/shard_map/ppermute | solution.py:532
  19.0 0.0 copy-done
  19.0 0.0 copy-done.1
  19.0 0.0 copy-done.2
  19.0 0.0 copy-done.3
  19.0 0.0 copy-done.4
  19.0 0.0 copy-done.5
  19.0 0.9 %near_part.1 = (f32[6,2,4,256]{3,2,1,0:T(4,128)S(1)}, f32[6,2,4,256]{3,2,1,0:T(4,128)S(1)}, f32[8,128]{1,0:T(8,128)S(1)}) custom-call(bf16[21,16,128]{2,1,0:T(8,128)(2,1)S(1)} %collective-permute-done.4.inner, f32[6,2,4,256]{3,2,1,0:T(4,128)S(1)} %get-tuple-element.43.o_r, f32[6,2,4,256]{3,2,1,0:T(4,128)S(1)} %get-tuple-element.44.o_s, ...), custom_call_target="tpu_custom_call" | custom-call | tf_op jit(solution)/shard_map/near_part/pallas_call | solution.py:538
  19.9 3.2 %collective-permute-done.3.outer = bf16[21,16,128]{2,1,0:T(8,128)(2,1)S(1)} collective-permute-done((bf16[21,16,128]{2,1,0:T(8,128)(2,1)S(1)}, bf16[21,16,128]{2,1,0:T(8,128)(2,1)S(1)}, u32[]{:S(2)}, u32[]{:S(2)}) %collective-permute-start.3) | collective-permute-done | bytes 86048 | tf_op jit(solution)/shard_map/ppermute | solution.py:533
  23.2 1.0 %final_part.1 = (f32[6,2,4,256]{3,2,1,0:T(4,128)}, f32[6,2,4,256]{3,2,1,0:T(4,128)}) custom-call(bf16[21,16,128]{2,1,0:T(8,128)(2,1)S(1)} %collective-permute-done.3.outer, f32[6,2,4,256]{3,2,1,0:T(4,128)S(1)} %get-tuple-element.51.part_r, f32[6,2,4,256]{3,2,1,0:T(4,128)S(1)} %get-tuple-element.52.part_s, f32[2,11,8,128]{3,2,1,0:T(8,128)S(1)} %get-tuple-element.47.q, ...), custom_call_target="tpu_custom_call" | custom-call | tf_op jit(solution)/shard_map/final_part/pallas_call | solution.py:550
  (3 shorter events, 0.0 us)
Async XLA Ops:
  2.3 5.2 %collective-permute-start = (bf16[2,64,128]{2,1,0:T(8,128)(2,1)S(1)}, bf16[2,64,128]{2,1,0:T(8,128)(2,1)S(1)}, u32[]{:S(2)}, u32[]{:S(2)}) collective-permute-start(bf16[2,64,128]{2,1,0:T(8,128)(2,1)S(1)} %get-tuple-element.28), channel_id=1, source_target_pairs={{0,20},{4,16},{8,28},{12,24},{16,4},{20,0},{24,12},{28,8},{1,21},{... | collective-permute-start | bytes 98312 | tf_op jit(solution)/shard_map/ppermute | solution.py:504
  7.5 4.2 %collective-permute-start.1 = (bf16[4,64,128]{2,1,0:T(8,128)(2,1)S(1)}, bf16[4,64,128]{2,1,0:T(8,128)(2,1)S(1)}, u32[]{:S(2)}, u32[]{:S(2)}) collective-permute-start(bf16[4,64,128]{2,1,0:T(8,128)(2,1)S(1)} %pad_maximum_fusion), channel_id=1, source_target_pairs={{0,12},{4,8},{8,4},{12,0},{16,28},{20,24},{24,20},{28,16},{1,13},{... | collective-permute-start | bytes 196616 | tf_op jit(solution)/shard_map/ppermute | solution.py:504
  11.7 1.4 %collective-permute-start.2 = (bf16[8,64,128]{2,1,0:T(8,128)(2,1)S(1)}, bf16[8,64,128]{2,1,0:T(8,128)(2,1)S(1)}, u32[]{:S(2)}, u32[]{:S(2)}) collective-permute-start(bf16[8,64,128]{2,1,0:T(8,128)(2,1)S(1)} %constant_dynamic-update-slice_fusion.mine), channel_id=1, source_target_pairs={{0,4},{4,0},{8,12},{12,8},{16,20},{20,16},{24,28},{28,24},{1,5},{5... | collective-permute-start | bytes 393224 | tf_op jit(solution)/shard_map/ppermute | solution.py:504
  13.1 5.9 %copy-start = (bf16[6,6,2,4,256]{4,3,2,1,0:T(4,128)(2,1)S(1)}, bf16[6,6,2,4,256]{4,3,2,1,0:T(4,128)(2,1)}, u32[]{:S(2)}) copy-start(bf16[6,6,2,4,256]{4,3,2,1,0:T(4,128)(2,1)} %jo_r.3) | copy-start | bytes 442372
  13.1 5.9 %copy-start.1 = (bf16[6,6,2,4,256]{4,3,2,1,0:T(4,128)(2,1)S(1)}, bf16[6,6,2,4,256]{4,3,2,1,0:T(4,128)(2,1)}, u32[]{:S(2)}) copy-start(bf16[6,6,2,4,256]{4,3,2,1,0:T(4,128)(2,1)} %jo_s.3) | copy-start | bytes 442372
  13.1 5.9 %copy-start.2 = (f32[6,2,4,256]{3,2,1,0:T(4,128)S(1)}, f32[6,2,4,256]{3,2,1,0:T(4,128)}, u32[]{:S(2)}) copy-start(f32[6,2,4,256]{3,2,1,0:T(4,128)} %jd_r.3) | copy-start | bytes 147460
  13.1 5.9 %copy-start.3 = (f32[6,2,4,256]{3,2,1,0:T(4,128)S(1)}, f32[6,2,4,256]{3,2,1,0:T(4,128)}, u32[]{:S(2)}) copy-start(f32[6,2,4,256]{3,2,1,0:T(4,128)} %jd_s.3) | copy-start | bytes 147460
  13.1 5.9 %copy-start.4 = (f32[6,2,4,256]{3,2,1,0:T(4,128)S(1)}, f32[6,2,4,256]{3,2,1,0:T(4,128)}, u32[]{:S(2)}) copy-start(f32[6,2,4,256]{3,2,1,0:T(4,128)} %src_r.1) | copy-start | bytes 147460
  13.1 5.9 %copy-start.5 = (f32[6,2,4,256]{3,2,1,0:T(4,128)S(1)}, f32[6,2,4,256]{3,2,1,0:T(4,128)}, u32[]{:S(2)}) copy-start(f32[6,2,4,256]{3,2,1,0:T(4,128)} %src_s.1) | copy-start | bytes 147460
  14.3 4.6 %collective-permute-start.4 = (bf16[21,16,128]{2,1,0:T(8,128)(2,1)S(1)}, bf16[21,16,128]{2,1,0:T(8,128)(2,1)S(1)}, u32[]{:S(2)}, u32[]{:S(2)}) collective-permute-start(bf16[21,16,128]{2,1,0:T(8,128)(2,1)S(1)} %get-tuple-element.42), channel_id=1, source_target_pairs={{0,1},{1,0},{2,3},{3,2},{4,5},{5,4},{6,7},{7,6},{8,9},{9,8},{10,11... | collective-permute-start | bytes 258056 | tf_op jit(solution)/shard_map/ppermute | solution.py:532
  15.9 7.3 %collective-permute-start.3 = (bf16[21,16,128]{2,1,0:T(8,128)(2,1)S(1)}, bf16[21,16,128]{2,1,0:T(8,128)(2,1)S(1)}, u32[]{:S(2)}, u32[]{:S(2)}) collective-permute-start(bf16[21,16,128]{2,1,0:T(8,128)(2,1)S(1)} %get-tuple-element.41), channel_id=1, source_target_pairs={{1,2},{2,1},{5,6},{6,5},{9,10},{10,9},{13,14},{14,13},{17,18},{18,... | collective-permute-start | bytes 258056 | tf_op jit(solution)/shard_map/ppermute | solution.py:533

commit v9 on v8

--- a/solution.py
+++ b/solution.py
@@ -176,7 +176,7 @@
 
 def second_kernel(
     masks, mine, other, v_r, v_s, a_r, a_s, primal_table, pull_table, margin_in,
-    o_r, o_s, h_r, h_s, q_out, speeds_out, scaled_out, p_out, inner, outer, flux, held, spot, g, margin, sem,
+    o_r, o_s, side_r, side_s, q_out, speeds_out, scaled_out, moved_out, inner, outer, spot, g, flux, held, margin, sem,
 ):
     var_count, rows, layers, cells = a_r.shape
     fetch = pltpu.make_async_copy(margin_in, margin, sem)
@@ -187,10 +187,7 @@
     spread = REACH + own_blocks + 1
     first_block = lax.axis_index("circ") * own_blocks
     row8 = iota((8, TILE), 0)
-    lane = iota((8, TILE), 1)
-    lane_all = iota((layers, cells), 1)
     layer_all = iota((layers, cells), 0)
-    edge = jnp.logical_or(lane_all == 0, lane_all == cells - 1)
     left = wrapped(first_block - 1 + total, total)
     right = wrapped(first_block + own_blocks, total)
 
@@ -220,7 +217,7 @@
     spots = spot[...]
     columns = [
         lax.dot_general(spots, edge_pick(q, cells), (((0,), (0,)), ((), ())), preferred_element_type=f32)
-        for q in range(4)
+        for q in range(2)
     ]
 
     fetch.wait()
@@ -235,17 +232,7 @@
 
     def keep(s, at, b, parts, moved):
         q_out[s, at], speeds_out[s, at], scaled_out[s, at] = parts
-        p_out[s, at] = advanced(s, b, moved)
-
-    def advanced(s, b, moved):
-        place = lax.rem(b, own_blocks)
-        before = jnp.where(place == 0, carry, 0.0).astype(f32)
-        after = jnp.where(place == own_blocks - 1, carry, 0.0).astype(f32)
-        low = pltpu.roll(g[wrapped(b - 1 + total, total), rows + s], 1, 1)
-        high = pltpu.roll(g[wrapped(b + 1, total), rows + s], TILE - 1, 1)
-        base = g[b, 2 * rows + s]
-        base = base + jnp.where(lane == 0, low * before, 0.0) + jnp.where(lane == TILE - 1, high * after, 0.0)
-        return base - step_size * moved
+        moved_out[s, at] = moved
 
     for s in range(rows):
         base = window(margin, s, first_block, total)
@@ -268,9 +255,9 @@
             return jnp.concatenate([pltpu.roll(low, 1, 1), *blank, pltpu.roll(high, TILE - 1, 1)], axis=1)
 
         pulled = step_size * jnp.concatenate(pulls[1:-1], axis=1)
-        pulled_side = step_size * at_sides(pulls[0], pulls[-1])
+        side_r[s] = step_size * at_sides(pulls[0], pulls[-1])
         pushed = step_size * jnp.concatenate(own, axis=1)
-        pushed_side = step_size * at_sides(*side_flux)
+        side_s[s] = -step_size * at_sides(*side_flux)
         for v in range(var_count):
             at = (v * rows + s) * 8
             cut = slice(at, at + layers)
@@ -278,12 +265,6 @@
                 v_r[v, s] + carry * columns[0][cut] + jnp.where(layer_all == layers - 1, pulled[v : v + 1], 0.0)
             )
             o_s[v, s] = v_s[v, s] + carry * columns[1][cut] - jnp.where(layer_all == 0, pushed[v : v + 1], 0.0)
-            h_r[v, s] = columns[2][cut] + jnp.where(
-                edge, carry * a_r[v, s] + jnp.where(layer_all == layers - 1, pulled_side[v : v + 1], 0.0), 0.0
-            )
-            h_s[v, s] = columns[3][cut] + jnp.where(
-                edge, carry * a_s[v, s] - jnp.where(layer_all == 0, pushed_side[v : v + 1], 0.0), 0.0
-            )
 
     last = jnp.concatenate([spots, jnp.ones((8, TILE), f32)], axis=0).astype(jnp.bfloat16)
     odd = jnp.bitwise_and(lax.axis_index("span"), 1)
@@ -331,8 +312,8 @@
 
 
 def third_kernel(
-    inner, o_r, o_s, h_r, h_s, q, speeds, scaled, p, a_r, a_s, jd_r, jd_s, jo_r, jo_s, src_r, src_s,
-    pull_table, margin_in, part_r, part_s, start, flux, x_r, x_s, held, margin, sem,
+    inner, o_r, o_s, side_r, side_s, q, speeds, scaled, pushed, spot, g, a_r, a_s, jd_r, jd_s, jo_r, jo_s, src_r, src_s,
+    pull_table, margin_in, part_r, part_s, start, p, flux, x_r, x_s, held, margin, sem,
 ):
     fetch = pltpu.make_async_copy(margin_in, margin, sem)
     fetch.start()
@@ -348,12 +329,20 @@
     for v in range(var_count):
         for i in range(own_blocks):
             held[v, :, i * TILE : (i + 1) * TILE] = inner[total // 2 + v * own_blocks + i].astype(f32)
+    lane_all = iota((layers, cells), 1)
+    layer_all = iota((layers, cells), 0)
+    lane = iota((8, TILE), 1)
+    edge = jnp.logical_or(lane_all == 0, lane_all == cells - 1)
+    beyond = [
+        lax.dot_general(spot[...], edge_pick(n, cells), (((0,), (0,)), ((), ())), preferred_element_type=f32)
+        for n in (2, 3)
+    ]
     columns = corner_columns(corner_of(inner[end], near_row, rows), cells)
     fields = (
-        (o_r, h_r, a_r, jd_r, jo_r, src_r, x_r, part_r),
-        (o_s, h_s, a_s, jd_s, jo_s, src_s, x_s, part_s),
-    )
-    for n, (o, h, a, jd, jo, src, x, part) in enumerate(fields):
+        (o_r, side_r, a_r, jd_r, jo_r, src_r, x_r, part_r, layers - 1),
+        (o_s, side_s, a_s, jd_s, jo_s, src_s, x_s, part_s, 0),
+    )
+    for n, (o, side, a, jd, jo, src, x, part, layer) in enumerate(fields):
         old = slice(n * layers, (n + 1) * layers)
         new = slice((2 + n) * layers, (3 + n) * layers)
         for v in range(var_count):
@@ -365,7 +354,10 @@
                 wide = x[v * rows + s]
                 at = (v * rows + s) * 8
                 beside = (lanes_apart(wide) + layers_apart(wide))[0:layers]
-                beside = beside + h[v, s] + carry * columns[n][at : at + layers]
+                beside = beside + beyond[n][at : at + layers] + carry * columns[n][at : at + layers]
+                beside = beside + jnp.where(
+                    edge, carry * a[v, s] + jnp.where(layer_all == layer, side[s, v : v + 1, :], 0.0), 0.0
+                )
                 beside = beside + near[s] * (held[v, new, :] + carry * a[v, s])
                 if s > 0:
                     beside = beside + x[v * rows + s - 1, 0:layers, :]
@@ -374,6 +366,22 @@
                 res = jacobian_row(jd, jo, state_row, v, s, var_count) - coupling * beside - src[v, s]
                 part[v, s] = state_row[v] - step_size * res
     fetch.wait()
+
+    def advanced(s, b, moved):
+        place = lax.rem(b, own_blocks)
+        before = jnp.where(place == 0, carry, 0.0).astype(f32)
+        after = jnp.where(place == own_blocks - 1, carry, 0.0).astype(f32)
+        low = pltpu.roll(g[wrapped(b - 1 + total, total), rows + s], 1, 1)
+        high = pltpu.roll(g[wrapped(b + 1, total), rows + s], TILE - 1, 1)
+        base = g[b, 2 * rows + s]
+        base = base + jnp.where(lane == 0, low * before, 0.0) + jnp.where(lane == TILE - 1, high * after, 0.0)
+        return base - step_size * moved
+
+    spread = REACH + own_blocks + 1
+    for s in range(rows):
+        blocks = window_blocks(window(margin, s, first_block, total), first_block, own_blocks, total)
+        for t, b in enumerate(blocks[1 : spread - 1] + blocks[spread : spread + own_blocks]):
+            p[s, t] = advanced(s, b, pushed[s, t])
     extra = row_flux(
         inner, near_row, window(margin, near_row, first_block, total), q, speeds, scaled, p, pull_table, flux,
         first_block, own_blocks, total,
@@ -509,17 +517,18 @@
             masks.append(hop)
         mask //= 2
     tiles = jax.ShapeDtypeStruct((total // 2 + var_count * own_blocks + 1, 16, TILE), jnp.bfloat16)
+    sides = jax.ShapeDtypeStruct((rows, 8, cells), f32)
+    corner = jax.ShapeDtypeStruct((8, TILE), f32)
+    gathered = jax.ShapeDtypeStruct((total, 3 * rows, 8, TILE), f32)
     listed = jax.ShapeDtypeStruct((rows, spread - 2 + own_blocks, 8, TILE), f32)
-    o_r, o_s, h_r, h_s, q, speeds, scaled, p, inner, outer = pl.pallas_call(
+    o_r, o_s, side_r, side_s, q, speeds, scaled, pushed, inner, outer, spot, g = pl.pallas_call(
         functools.partial(second_kernel, masks),
-        out_shape=(field,) * 4 + (listed,) * 4 + (tiles,) * 2,
+        out_shape=(field,) * 2 + (sides,) * 2 + (listed,) * 4 + (tiles,) * 2 + (corner, gathered),
         in_specs=[vmem] * 8 + [anywhere],
-        out_specs=(vmem,) * 10,
+        out_specs=(vmem,) * 12,
         scratch_shapes=[
             pltpu.VMEM((rows, spread, 8, TILE), f32),
             pltpu.VMEM((var_count, 4 * layers, cells), f32),
-            pltpu.VMEM((8, TILE), f32),
-            pltpu.VMEM((total, 3 * rows, 8, TILE), f32),
             pltpu.SMEM(margin.shape, jnp.int32),
             pltpu.SemaphoreType.DMA(()),
         ],
@@ -535,16 +544,16 @@
     flux = pltpu.VMEM((spread - 2, 8, TILE), f32)
     listing = pltpu.SMEM(margin.shape, jnp.int32)
     small = pltpu.VMEM((8, 8, cells), f32)
-    part_r, part_s, start = pl.pallas_call(
+    part_r, part_s, start, p = pl.pallas_call(
         third_kernel,
-        out_shape=(field, field, jax.ShapeDtypeStruct((8, TILE), f32)),
-        in_specs=[vmem] * 18 + [anywhere],
-        out_specs=(vmem,) * 3,
+        out_shape=(field, field, corner, listed),
+        in_specs=[vmem] * 20 + [anywhere],
+        out_specs=(vmem,) * 4,
         scratch_shapes=[flux, padded, padded, held, listing, pltpu.SemaphoreType.DMA(())],
         compiler_params=params,
         name="near_part",
     )(
-        inner, o_r, o_s, h_r, h_s, q, speeds, scaled, p, a_r, a_s, jac_diag_rotor, jac_diag_stator,
+        inner, o_r, o_s, side_r, side_s, q, speeds, scaled, pushed, spot, g, a_r, a_s, jac_diag_rotor, jac_diag_stator,
         jac_off_rotor, jac_off_stator, source_rotor, source_stator, pull_table, margin,
     )
     out_r, out_s = pl.pallas_call(

time: 24.3 us -> 24.2 us (level)
  Pallas kernels: 5.67 us -> 5.42 us
  transfers between devices with their start and end apart: 5 -> 5, of which waited for: 5 -> 5; matrix products, arithmetic and copies ran while one was open for 0% -> 0% of each run, Pallas kernels for 8% -> 7%
where the time goes in v9:
time: 24.2 us; the launch traced here: 24 us
  waiting for transfers between devices  13.5 us (56%)
  Pallas kernels  5.42 us (22%)
  starting transfers between devices  4.25 us (18%)
  between operations  0.75 us (3%)
    ppermute x3, waiting for transfers between devices, per_device(): other = lax.ppermute(mine, 'circ', [(i, i ^ hop) for i in range(members)])  9.53 us
    ppermute x1, waiting for transfers between devices, per_device(): outer = lax.ppermute(outer, 'span', far)  3.3 us
    ppermute x1, starting transfers between devices, per_device(): outer = lax.ppermute(outer, 'span', far)  2.38 us
    pallas_call x1, Pallas kernels, per_device(): pl.pallas_call(first_kernel, out_shape=(field, field, jax.ShapeDtypeStruc...  1.64 us
    ppermute x1, starting transfers between devices, per_device(): inner = lax.ppermute(inner, 'span', near)  1.55 us
    pallas_call x1, Pallas kernels, per_device(): pl.pallas_call(functools.partial(fourth_kernel, bands), out_shape=(field,...  1.01 us
    pallas_call x1, Pallas kernels, per_device(): pl.pallas_call(functools.partial(second_kernel, masks), out_shape=(field,...  1 us
    pallas_call x1, Pallas kernels, per_device(): pl.pallas_call(table_kernel, out_shape=(jax.ShapeDtypeStruct((rows, sprea...  0.94 us
  transfers between devices with their start and end apart: 5, of which 5 were waited for; matrix products, arithmetic and copies ran while one was open for 0% of the time, Pallas kernels for 7%

profile of v9, /device:TPU:28, one launch (start us, length us, event | category | flops | bytes accessed | tf_op | source)
XLA Modules:
  0.0 24.0 jit_solution(1523283423458228267)
XLA Ops:
  0.6 1.6 %local_part.1 = (f32[6,2,4,256]{3,2,1,0:T(4,128)S(1)}, f32[6,2,4,256]{3,2,1,0:T(4,128)S(1)}, bf16[2,64,128]{2,1,0:T(8,128)(2,1)S(1)}, f32[6,2,4,256]{3,2,1,0:T(4...) custom-call(f32[6,2,4,256]{3,2,1,0:T(4,128)} %refs_0_.1, ...), custom_call_target="tpu_custom_call" | custom-call | tf_op jit(solution)/shard_map/local_part/pallas_call | solution.py:482
  2.3 0.1 collective-permute-start
  2.4 0.9 %weight_tables.1 = (f32[2,15,4,128]{3,2,1,0:T(4,128)S(1)}, f32[2,4,8,128]{3,2,1,0:T(8,128)S(1)}) custom-call(f32[2,16,4,128]{3,2,1,0:T(4,128)S(1)} %get-tuple-element.32.weights, s32[2,4,16]{2,1,0:T(4,128)S(1)} %get-tuple-element.33.margin.margin_in, s32[2,16]{1,0:T(2,128)S(1)} %get-tuple-element.34.count), custom_call_target="tpu_custom_call" | custom-call | tf_op jit(solution)/shard_map/weight_tables/pallas_call | solution.py:496
  3.3 4.2 %collective-permute-done = bf16[2,64,128]{2,1,0:T(8,128)(2,1)S(1)} collective-permute-done((bf16[2,64,128]{2,1,0:T(8,128)(2,1)S(1)}, bf16[2,64,128]{2,1,0:T(8,128)(2,1)S(1)}, u32[]{:S(2)}, u32[]{:S(2)}) %collective-permute-start) | collective-permute-done | bytes 32800 | tf_op jit(solution)/shard_map/ppermute | solution.py:512
  7.5 0.1 collective-permute-start.1
  7.6 4.1 %collective-permute-done.1 = bf16[4,64,128]{2,1,0:T(8,128)(2,1)S(1)} collective-permute-done((bf16[4,64,128]{2,1,0:T(8,128)(2,1)S(1)}, bf16[4,64,128]{2,1,0:T(8,128)(2,1)S(1)}, u32[]{:S(2)}, u32[]{:S(2)}) %collective-permute-start.1) | collective-permute-done | bytes 65568 | tf_op jit(solution)/shard_map/ppermute | solution.py:512
  11.7 0.2 collective-permute-start.2
  11.9 1.2 %collective-permute-done.2.other = bf16[8,64,128]{2,1,0:T(8,128)(2,1)S(1)} collective-permute-done((bf16[8,64,128]{2,1,0:T(8,128)(2,1)S(1)}, bf16[8,64,128]{2,1,0:T(8,128)(2,1)S(1)}, u32[]{:S(2)}, u32[]{:S(2)}) %collective-permute-start.2) | collective-permute-done | bytes 131104 | tf_op jit(solution)/shard_map/ppermute | solution.py:512
  13.1 0.0 copy-start
  13.1 0.0 copy-start.1
  13.1 0.0 copy-start.2
  13.1 0.0 copy-start.3
  13.1 0.0 copy-start.4
  13.1 0.0 copy-start.5
  13.2 1.0 %interface_part.1 = (f32[6,2,4,256]{3,2,1,0:T(4,128)S(1)}, f32[6,2,4,256]{3,2,1,0:T(4,128)S(1)}, f32[2,8,256]{2,1,0:T(8,128)S(1)}, f32[2,8,256]{2,1,0:T(8,128)S(...) custom-call(bf16[8,64,128]{2,1,0:T(8,128)(2,1)S(1)} %constant_dynami, ...), custom_call_target="tpu_custom_call" | custom-call | tf_op jit(solution)/shard_map/interface_part/pallas_call | solution.py:524
  14.2 1.6 %collective-permute-start.4 = (bf16[21,16,128]{2,1,0:T(8,128)(2,1)S(1)}, bf16[21,16,128]{2,1,0:T(8,128)(2,1)S(1)}, u32[]{:S(2)}, u32[]{:S(2)}) collective-permute-start(bf16[21,16,128]{2,1,0:T(8,128)(2,1)S(1)} %get-tuple-element.45), channel_id=1, source_target_pairs={{0,1},{1,0},{2,3},{3,2},{4,5},{5,4},{6,7},{7,6},{8,9},{9,8},{10,11... | collective-permute-start | bytes 258056 | tf_op jit(solution)/shard_map/ppermute | solution.py:541
  15.7 2.4 %collective-permute-start.3 = (bf16[21,16,128]{2,1,0:T(8,128)(2,1)S(1)}, bf16[21,16,128]{2,1,0:T(8,128)(2,1)S(1)}, u32[]{:S(2)}, u32[]{:S(2)}) collective-permute-start(bf16[21,16,128]{2,1,0:T(8,128)(2,1)S(1)} %get-tuple-element.44), channel_id=1, source_target_pairs={{1,2},{2,1},{5,6},{6,5},{9,10},{10,9},{13,14},{14,13},{17,18},{18,... | collective-permute-start | bytes 258056 | tf_op jit(solution)/shard_map/ppermute | solution.py:542
  18.1 0.7 %collective-permute-done.4.inner = bf16[21,16,128]{2,1,0:T(8,128)(2,1)S(1)} collective-permute-done((bf16[21,16,128]{2,1,0:T(8,128)(2,1)S(1)}, bf16[21,16,128]{2,1,0:T(8,128)(2,1)S(1)}, u32[]{:S(2)}, u32[]{:S(2)}) %collective-permute-start.4) | collective-permute-done | bytes 86048 | tf_op jit(solution)/shard_map/ppermute | solution.py:541
  18.8 0.0 copy-done
  18.8 0.0 copy-done.1
  18.8 0.0 copy-done.2
  18.8 0.0 copy-done.3
  18.8 0.0 copy-done.4
  18.8 0.0 copy-done.5
  18.9 0.8 %near_part.1 = (f32[6,2,4,256]{3,2,1,0:T(4,128)S(1)}, f32[6,2,4,256]{3,2,1,0:T(4,128)S(1)}, f32[8,128]{1,0:T(8,128)S(1)}, f32[2,11,8,128]{3,2,1,0:T(8,128)S(1)}) custom-call(bf16[21,16,128]{2,1,0:T(8,128)(2,1)S(1)} %collective-permute-done.4.inner, f32[6,2,4,256]{3,2,1,0:T(4,128)S(1)} %get-tuple-element.46.o_r, f32[6,2,4,256]{3,2,1,0:T(4,128)S(1)} %get-tuple-element.47.o_s, ...), custom_call_target="tpu_custom_call" | custom-call | tf_op jit(solution)/shard_map/near_part/pallas_call | solution.py:547
  19.7 3.3 %collective-permute-done.3.outer = bf16[21,16,128]{2,1,0:T(8,128)(2,1)S(1)} collective-permute-done((bf16[21,16,128]{2,1,0:T(8,128)(2,1)S(1)}, bf16[21,16,128]{2,1,0:T(8,128)(2,1)S(1)}, u32[]{:S(2)}, u32[]{:S(2)}) %collective-permute-start.3) | collective-permute-done | bytes 86048 | tf_op jit(solution)/shard_map/ppermute | solution.py:542
  23.0 1.0 %final_part.1 = (f32[6,2,4,256]{3,2,1,0:T(4,128)}, f32[6,2,4,256]{3,2,1,0:T(4,128)}) custom-call(bf16[21,16,128]{2,1,0:T(8,128)(2,1)S(1)} %collective-permute-done.3.outer, f32[6,2,4,256]{3,2,1,0:T(4,128)S(1)} %get-tuple-element.56.part_r, f32[6,2,4,256]{3,2,1,0:T(4,128)S(1)} %get-tuple-element.57.part_s, f32[2,11,8,128]{3,2,1,0:T(8,128)S(1)} %get-tuple-element.50.q, ...), custom_call_target="tpu_custom_call" | custom-call | tf_op jit(solution)/shard_map/final_part/pallas_call | solution.py:559
  (3 shorter events, 0.0 us)
Async XLA Ops:
  2.3 5.2 %collective-permute-start = (bf16[2,64,128]{2,1,0:T(8,128)(2,1)S(1)}, bf16[2,64,128]{2,1,0:T(8,128)(2,1)S(1)}, u32[]{:S(2)}, u32[]{:S(2)}) collective-permute-start(bf16[2,64,128]{2,1,0:T(8,128)(2,1)S(1)} %get-tuple-element.31), channel_id=1, source_target_pairs={{0,20},{4,16},{8,28},{12,24},{16,4},{20,0},{24,12},{28,8},{1,21},{... | collective-permute-start | bytes 98312 | tf_op jit(solution)/shard_map/ppermute | solution.py:512
  7.5 4.2 %collective-permute-start.1 = (bf16[4,64,128]{2,1,0:T(8,128)(2,1)S(1)}, bf16[4,64,128]{2,1,0:T(8,128)(2,1)S(1)}, u32[]{:S(2)}, u32[]{:S(2)}) collective-permute-start(bf16[4,64,128]{2,1,0:T(8,128)(2,1)S(1)} %pad_maximum_fusion), channel_id=1, source_target_pairs={{0,12},{4,8},{8,4},{12,0},{16,28},{20,24},{24,20},{28,16},{1,13},{... | collective-permute-start | bytes 196616 | tf_op jit(solution)/shard_map/ppermute | solution.py:512
  11.7 1.4 %collective-permute-start.2 = (bf16[8,64,128]{2,1,0:T(8,128)(2,1)S(1)}, bf16[8,64,128]{2,1,0:T(8,128)(2,1)S(1)}, u32[]{:S(2)}, u32[]{:S(2)}) collective-permute-start(bf16[8,64,128]{2,1,0:T(8,128)(2,1)S(1)} %constant_dynamic-update-slice_fusion.mine), channel_id=1, source_target_pairs={{0,4},{4,0},{8,12},{12,8},{16,20},{20,16},{24,28},{28,24},{1,5},{5... | collective-permute-start | bytes 393224 | tf_op jit(solution)/shard_map/ppermute | solution.py:512
  13.1 5.7 %copy-start = (bf16[6,6,2,4,256]{4,3,2,1,0:T(4,128)(2,1)S(1)}, bf16[6,6,2,4,256]{4,3,2,1,0:T(4,128)(2,1)}, u32[]{:S(2)}) copy-start(bf16[6,6,2,4,256]{4,3,2,1,0:T(4,128)(2,1)} %jo_r.3) | copy-start | bytes 442372
  13.1 5.7 %copy-start.1 = (bf16[6,6,2,4,256]{4,3,2,1,0:T(4,128)(2,1)S(1)}, bf16[6,6,2,4,256]{4,3,2,1,0:T(4,128)(2,1)}, u32[]{:S(2)}) copy-start(bf16[6,6,2,4,256]{4,3,2,1,0:T(4,128)(2,1)} %jo_s.3) | copy-start | bytes 442372
  13.1 5.7 %copy-start.2 = (f32[6,2,4,256]{3,2,1,0:T(4,128)S(1)}, f32[6,2,4,256]{3,2,1,0:T(4,128)}, u32[]{:S(2)}) copy-start(f32[6,2,4,256]{3,2,1,0:T(4,128)} %jd_r.3) | copy-start | bytes 147460
  13.1 5.7 %copy-start.3 = (f32[6,2,4,256]{3,2,1,0:T(4,128)S(1)}, f32[6,2,4,256]{3,2,1,0:T(4,128)}, u32[]{:S(2)}) copy-start(f32[6,2,4,256]{3,2,1,0:T(4,128)} %jd_s.3) | copy-start | bytes 147460
  13.1 5.7 %copy-start.4 = (f32[6,2,4,256]{3,2,1,0:T(4,128)S(1)}, f32[6,2,4,256]{3,2,1,0:T(4,128)}, u32[]{:S(2)}) copy-start(f32[6,2,4,256]{3,2,1,0:T(4,128)} %src_r.1) | copy-start | bytes 147460
  13.1 5.7 %copy-start.5 = (f32[6,2,4,256]{3,2,1,0:T(4,128)S(1)}, f32[6,2,4,256]{3,2,1,0:T(4,128)}, u32[]{:S(2)}) copy-start(f32[6,2,4,256]{3,2,1,0:T(4,128)} %src_s.1) | copy-start | bytes 147460
  14.2 4.6 %collective-permute-start.4 = (bf16[21,16,128]{2,1,0:T(8,128)(2,1)S(1)}, bf16[21,16,128]{2,1,0:T(8,128)(2,1)S(1)}, u32[]{:S(2)}, u32[]{:S(2)}) collective-permute-start(bf16[21,16,128]{2,1,0:T(8,128)(2,1)S(1)} %get-tuple-element.45), channel_id=1, source_target_pairs={{0,1},{1,0},{2,3},{3,2},{4,5},{5,4},{6,7},{7,6},{8,9},{9,8},{10,11... | collective-permute-start | bytes 258056 | tf_op jit(solution)/shard_map/ppermute | solution.py:541
  15.7 7.3 %collective-permute-start.3 = (bf16[21,16,128]{2,1,0:T(8,128)(2,1)S(1)}, bf16[21,16,128]{2,1,0:T(8,128)(2,1)S(1)}, u32[]{:S(2)}, u32[]{:S(2)}) collective-permute-start(bf16[21,16,128]{2,1,0:T(8,128)(2,1)S(1)} %get-tuple-element.44), channel_id=1, source_target_pairs={{1,2},{2,1},{5,6},{6,5},{9,10},{10,9},{13,14},{14,13},{17,18},{18,... | collective-permute-start | bytes 258056 | tf_op jit(solution)/shard_map/ppermute | solution.py:542

commit v10 on v9

--- a/solution.py
+++ b/solution.py
@@ -119,7 +119,7 @@
     wide_out[...] = jnp.zeros(wide_out.shape, f32)
     for x in xs:
         x[...] = jnp.zeros(x.shape, f32)
-    for copy in copies:
+    for copy in copies[:9]:
         copy.wait()
     fields = ((a_r, jd_r, jo_r, src_r, v_r, xs[0], xs[2]), (a_s, jd_s, jo_s, src_s, v_s, xs[1], xs[3]))
     for a, jd, jo, src, partial, x_a, x_p in fields:
@@ -172,6 +172,8 @@
             ))
         for n in range(4):
             out[i, n * 16 : n * 16 + 16, :] = jnp.concatenate([x[n] for x in groups], axis=0).astype(jnp.bfloat16)
+    for copy in copies[9:]:
+        copy.wait()
 
 
 def second_kernel(
@@ -431,7 +433,7 @@
                 beside = beside + carry * columns[n][at : at + layers]
             extra = carry * (beside + held[v, new, :]) + (carry * live) * a[v, far_row]
             gone = jacobian_row(jd, jo, state_row, v, far_row, var_count)
-            for s in range(rows):
+            for s in range(1, rows - 1):
                 out[v, s] = part[v, s]
             out[v, far_row] = part[v, far_row] + state_row[v] - step_size * gone + extra
             out[v, next_row] = part[v, next_row] + carry * state_row[v]

time: 24.2 us -> 24.1 us (level)
  no operation moved by 1% of the time
where the time goes in v10:
time: 24.1 us; the launch traced here: 24 us
  waiting for transfers between devices  13.5 us (56%)
  Pallas kernels  5.38 us (22%)
  starting transfers between devices  4.25 us (18%)
  between operations  0.75 us (3%)
    ppermute x3, waiting for transfers between devices, per_device(): other = lax.ppermute(mine, 'circ', [(i, i ^ hop) for i in range(members)])  9.53 us
    ppermute x1, waiting for transfers between devices, per_device(): outer = lax.ppermute(outer, 'span', far)  3.3 us
    ppermute x1, starting transfers between devices, per_device(): outer = lax.ppermute(outer, 'span', far)  2.38 us
    pallas_call x1, Pallas kernels, per_device(): pl.pallas_call(first_kernel, out_shape=(field, field, jax.ShapeDtypeStruc...  1.6 us
    ppermute x1, starting transfers between devices, per_device(): inner = lax.ppermute(inner, 'span', near)  1.55 us
    pallas_call x1, Pallas kernels, per_device(): pl.pallas_call(functools.partial(fourth_kernel, bands), out_shape=(field,...  1.01 us
    pallas_call x1, Pallas kernels, per_device(): pl.pallas_call(functools.partial(second_kernel, masks), out_shape=(field,...  1 us
    pallas_call x1, Pallas kernels, per_device(): pl.pallas_call(table_kernel, out_shape=(jax.ShapeDtypeStruct((rows, sprea...  0.94 us
  transfers between devices with their start and end apart: 5, of which 5 were waited for; matrix products, arithmetic and copies ran while one was open for 0% of the time, Pallas kernels for 7%

profile of v10, /device:TPU:28, one launch (start us, length us, event | category | flops | bytes accessed | tf_op | source)
XLA Modules:
  0.0 24.0 jit_solution(781629159700023035)
XLA Ops:
  0.6 1.6 %local_part.1 = (f32[6,2,4,256]{3,2,1,0:T(4,128)S(1)}, f32[6,2,4,256]{3,2,1,0:T(4,128)S(1)}, bf16[2,64,128]{2,1,0:T(8,128)(2,1)S(1)}, f32[6,2,4,256]{3,2,1,0:T(4...) custom-call(f32[6,2,4,256]{3,2,1,0:T(4,128)} %refs_0_.1, ...), custom_call_target="tpu_custom_call" | custom-call | tf_op jit(solution)/shard_map/local_part/pallas_call | solution.py:484
  2.2 0.1 collective-permute-start
  2.3 0.9 %weight_tables.1 = (f32[2,15,4,128]{3,2,1,0:T(4,128)S(1)}, f32[2,4,8,128]{3,2,1,0:T(8,128)S(1)}) custom-call(f32[2,16,4,128]{3,2,1,0:T(4,128)S(1)} %get-tuple-element.32.weights, s32[2,4,16]{2,1,0:T(4,128)S(1)} %get-tuple-element.33.margin.margin_in, s32[2,16]{1,0:T(2,128)S(1)} %get-tuple-element.34.count), custom_call_target="tpu_custom_call" | custom-call | tf_op jit(solution)/shard_map/weight_tables/pallas_call | solution.py:498
  3.3 4.2 %collective-permute-done = bf16[2,64,128]{2,1,0:T(8,128)(2,1)S(1)} collective-permute-done((bf16[2,64,128]{2,1,0:T(8,128)(2,1)S(1)}, bf16[2,64,128]{2,1,0:T(8,128)(2,1)S(1)}, u32[]{:S(2)}, u32[]{:S(2)}) %collective-permute-start) | collective-permute-done | bytes 32800 | tf_op jit(solution)/shard_map/ppermute | solution.py:514
  7.5 0.1 collective-permute-start.1
  7.6 4.1 %collective-permute-done.1 = bf16[4,64,128]{2,1,0:T(8,128)(2,1)S(1)} collective-permute-done((bf16[4,64,128]{2,1,0:T(8,128)(2,1)S(1)}, bf16[4,64,128]{2,1,0:T(8,128)(2,1)S(1)}, u32[]{:S(2)}, u32[]{:S(2)}) %collective-permute-start.1) | collective-permute-done | bytes 65568 | tf_op jit(solution)/shard_map/ppermute | solution.py:514
  11.7 0.2 collective-permute-start.2
  11.9 1.2 %collective-permute-done.2.other = bf16[8,64,128]{2,1,0:T(8,128)(2,1)S(1)} collective-permute-done((bf16[8,64,128]{2,1,0:T(8,128)(2,1)S(1)}, bf16[8,64,128]{2,1,0:T(8,128)(2,1)S(1)}, u32[]{:S(2)}, u32[]{:S(2)}) %collective-permute-start.2) | collective-permute-done | bytes 131104 | tf_op jit(solution)/shard_map/ppermute | solution.py:514
  13.1 0.0 copy-start
  13.1 0.0 copy-start.1
  13.1 0.0 copy-start.2
  13.1 0.0 copy-start.3
  13.1 0.0 copy-start.4
  13.1 0.0 copy-start.5
  13.1 1.0 %interface_part.1 = (f32[6,2,4,256]{3,2,1,0:T(4,128)S(1)}, f32[6,2,4,256]{3,2,1,0:T(4,128)S(1)}, f32[2,8,256]{2,1,0:T(8,128)S(1)}, f32[2,8,256]{2,1,0:T(8,128)S(...) custom-call(bf16[8,64,128]{2,1,0:T(8,128)(2,1)S(1)} %constant_dynami, ...), custom_call_target="tpu_custom_call" | custom-call | tf_op jit(solution)/shard_map/interface_part/pallas_call | solution.py:526
  14.1 1.6 %collective-permute-start.4 = (bf16[21,16,128]{2,1,0:T(8,128)(2,1)S(1)}, bf16[21,16,128]{2,1,0:T(8,128)(2,1)S(1)}, u32[]{:S(2)}, u32[]{:S(2)}) collective-permute-start(bf16[21,16,128]{2,1,0:T(8,128)(2,1)S(1)} %get-tuple-element.45), channel_id=1, source_target_pairs={{0,1},{1,0},{2,3},{3,2},{4,5},{5,4},{6,7},{7,6},{8,9},{9,8},{10,11... | collective-permute-start | bytes 258056 | tf_op jit(solution)/shard_map/ppermute | solution.py:543
  15.7 2.4 %collective-permute-start.3 = (bf16[21,16,128]{2,1,0:T(8,128)(2,1)S(1)}, bf16[21,16,128]{2,1,0:T(8,128)(2,1)S(1)}, u32[]{:S(2)}, u32[]{:S(2)}) collective-permute-start(bf16[21,16,128]{2,1,0:T(8,128)(2,1)S(1)} %get-tuple-element.44), channel_id=1, source_target_pairs={{1,2},{2,1},{5,6},{6,5},{9,10},{10,9},{13,14},{14,13},{17,18},{18,... | collective-permute-start | bytes 258056 | tf_op jit(solution)/shard_map/ppermute | solution.py:544
  18.1 0.7 %collective-permute-done.4.inner = bf16[21,16,128]{2,1,0:T(8,128)(2,1)S(1)} collective-permute-done((bf16[21,16,128]{2,1,0:T(8,128)(2,1)S(1)}, bf16[21,16,128]{2,1,0:T(8,128)(2,1)S(1)}, u32[]{:S(2)}, u32[]{:S(2)}) %collective-permute-start.4) | collective-permute-done | bytes 86048 | tf_op jit(solution)/shard_map/ppermute | solution.py:543
  18.8 0.0 copy-done
  18.8 0.0 copy-done.1
  18.8 0.0 copy-done.2
  18.8 0.0 copy-done.3
  18.8 0.0 copy-done.4
  18.8 0.0 copy-done.5
  18.8 0.8 %near_part.1 = (f32[6,2,4,256]{3,2,1,0:T(4,128)S(1)}, f32[6,2,4,256]{3,2,1,0:T(4,128)S(1)}, f32[8,128]{1,0:T(8,128)S(1)}, f32[2,11,8,128]{3,2,1,0:T(8,128)S(1)}) custom-call(bf16[21,16,128]{2,1,0:T(8,128)(2,1)S(1)} %collective-permute-done.4.inner, f32[6,2,4,256]{3,2,1,0:T(4,128)S(1)} %get-tuple-element.46.o_r, f32[6,2,4,256]{3,2,1,0:T(4,128)S(1)} %get-tuple-element.47.o_s, ...), custom_call_target="tpu_custom_call" | custom-call | tf_op jit(solution)/shard_map/near_part/pallas_call | solution.py:549
  19.7 3.3 %collective-permute-done.3.outer = bf16[21,16,128]{2,1,0:T(8,128)(2,1)S(1)} collective-permute-done((bf16[21,16,128]{2,1,0:T(8,128)(2,1)S(1)}, bf16[21,16,128]{2,1,0:T(8,128)(2,1)S(1)}, u32[]{:S(2)}, u32[]{:S(2)}) %collective-permute-start.3) | collective-permute-done | bytes 86048 | tf_op jit(solution)/shard_map/ppermute | solution.py:544
  23.0 1.0 %final_part.1 = (f32[6,2,4,256]{3,2,1,0:T(4,128)}, f32[6,2,4,256]{3,2,1,0:T(4,128)}) custom-call(bf16[21,16,128]{2,1,0:T(8,128)(2,1)S(1)} %collective-permute-done.3.outer, f32[6,2,4,256]{3,2,1,0:T(4,128)S(1)} %get-tuple-element.56.part_r, f32[6,2,4,256]{3,2,1,0:T(4,128)S(1)} %get-tuple-element.57.part_s, f32[2,11,8,128]{3,2,1,0:T(8,128)S(1)} %get-tuple-element.50.q, ...), custom_call_target="tpu_custom_call" | custom-call | tf_op jit(solution)/shard_map/final_part/pallas_call | solution.py:561
  (3 shorter events, 0.0 us)
Async XLA Ops:
  2.2 5.2 %collective-permute-start = (bf16[2,64,128]{2,1,0:T(8,128)(2,1)S(1)}, bf16[2,64,128]{2,1,0:T(8,128)(2,1)S(1)}, u32[]{:S(2)}, u32[]{:S(2)}) collective-permute-start(bf16[2,64,128]{2,1,0:T(8,128)(2,1)S(1)} %get-tuple-element.31), channel_id=1, source_target_pairs={{0,20},{4,16},{8,28},{12,24},{16,4},{20,0},{24,12},{28,8},{1,21},{... | collective-permute-start | bytes 98312 | tf_op jit(solution)/shard_map/ppermute | solution.py:514
  7.5 4.2 %collective-permute-start.1 = (bf16[4,64,128]{2,1,0:T(8,128)(2,1)S(1)}, bf16[4,64,128]{2,1,0:T(8,128)(2,1)S(1)}, u32[]{:S(2)}, u32[]{:S(2)}) collective-permute-start(bf16[4,64,128]{2,1,0:T(8,128)(2,1)S(1)} %pad_maximum_fusion), channel_id=1, source_target_pairs={{0,12},{4,8},{8,4},{12,0},{16,28},{20,24},{24,20},{28,16},{1,13},{... | collective-permute-start | bytes 196616 | tf_op jit(solution)/shard_map/ppermute | solution.py:514
  11.7 1.4 %collective-permute-start.2 = (bf16[8,64,128]{2,1,0:T(8,128)(2,1)S(1)}, bf16[8,64,128]{2,1,0:T(8,128)(2,1)S(1)}, u32[]{:S(2)}, u32[]{:S(2)}) collective-permute-start(bf16[8,64,128]{2,1,0:T(8,128)(2,1)S(1)} %constant_dynamic-update-slice_fusion.mine), channel_id=1, source_target_pairs={{0,4},{4,0},{8,12},{12,8},{16,20},{20,16},{24,28},{28,24},{1,5},{5... | collective-permute-start | bytes 393224 | tf_op jit(solution)/shard_map/ppermute | solution.py:514
  13.1 5.7 %copy-start = (bf16[6,6,2,4,256]{4,3,2,1,0:T(4,128)(2,1)S(1)}, bf16[6,6,2,4,256]{4,3,2,1,0:T(4,128)(2,1)}, u32[]{:S(2)}) copy-start(bf16[6,6,2,4,256]{4,3,2,1,0:T(4,128)(2,1)} %jo_r.3) | copy-start | bytes 442372
  13.1 5.7 %copy-start.1 = (bf16[6,6,2,4,256]{4,3,2,1,0:T(4,128)(2,1)S(1)}, bf16[6,6,2,4,256]{4,3,2,1,0:T(4,128)(2,1)}, u32[]{:S(2)}) copy-start(bf16[6,6,2,4,256]{4,3,2,1,0:T(4,128)(2,1)} %jo_s.3) | copy-start | bytes 442372
  13.1 5.7 %copy-start.2 = (f32[6,2,4,256]{3,2,1,0:T(4,128)S(1)}, f32[6,2,4,256]{3,2,1,0:T(4,128)}, u32[]{:S(2)}) copy-start(f32[6,2,4,256]{3,2,1,0:T(4,128)} %jd_r.3) | copy-start | bytes 147460
  13.1 5.7 %copy-start.3 = (f32[6,2,4,256]{3,2,1,0:T(4,128)S(1)}, f32[6,2,4,256]{3,2,1,0:T(4,128)}, u32[]{:S(2)}) copy-start(f32[6,2,4,256]{3,2,1,0:T(4,128)} %jd_s.3) | copy-start | bytes 147460
  13.1 5.7 %copy-start.4 = (f32[6,2,4,256]{3,2,1,0:T(4,128)S(1)}, f32[6,2,4,256]{3,2,1,0:T(4,128)}, u32[]{:S(2)}) copy-start(f32[6,2,4,256]{3,2,1,0:T(4,128)} %src_r.1) | copy-start | bytes 147460
  13.1 5.7 %copy-start.5 = (f32[6,2,4,256]{3,2,1,0:T(4,128)S(1)}, f32[6,2,4,256]{3,2,1,0:T(4,128)}, u32[]{:S(2)}) copy-start(f32[6,2,4,256]{3,2,1,0:T(4,128)} %src_s.1) | copy-start | bytes 147460
  14.1 4.6 %collective-permute-start.4 = (bf16[21,16,128]{2,1,0:T(8,128)(2,1)S(1)}, bf16[21,16,128]{2,1,0:T(8,128)(2,1)S(1)}, u32[]{:S(2)}, u32[]{:S(2)}) collective-permute-start(bf16[21,16,128]{2,1,0:T(8,128)(2,1)S(1)} %get-tuple-element.45), channel_id=1, source_target_pairs={{0,1},{1,0},{2,3},{3,2},{4,5},{5,4},{6,7},{7,6},{8,9},{9,8},{10,11... | collective-permute-start | bytes 258056 | tf_op jit(solution)/shard_map/ppermute | solution.py:543
  15.7 7.3 %collective-permute-start.3 = (bf16[21,16,128]{2,1,0:T(8,128)(2,1)S(1)}, bf16[21,16,128]{2,1,0:T(8,128)(2,1)S(1)}, u32[]{:S(2)}, u32[]{:S(2)}) collective-permute-start(bf16[21,16,128]{2,1,0:T(8,128)(2,1)S(1)} %get-tuple-element.44), channel_id=1, source_target_pairs={{1,2},{2,1},{5,6},{6,5},{9,10},{10,9},{13,14},{14,13},{17,18},{18,... | collective-permute-start | bytes 258056 | tf_op jit(solution)/shard_map/ppermute | solution.py:544

commit v11 on v9

--- a/solution.py
+++ b/solution.py
@@ -220,6 +220,13 @@
         for q in range(2)
     ]
 
+    last = jnp.concatenate([spots, jnp.ones((8, TILE), f32)], axis=0).astype(jnp.bfloat16)
+    odd = jnp.bitwise_and(lax.axis_index("span"), 1)
+    ends = ((inner, (1 - odd) * (rows - 1)), (outer, odd * (rows - 1)))
+    for to, s in ends:
+        for j in range(total // 2):
+            to[j] = jnp.concatenate([g[2 * j, rows + s], g[2 * j + 1, rows + s]], axis=0).astype(jnp.bfloat16)
+        to[total // 2 + var_count * own_blocks] = last
     fetch.wait()
 
     def block(s, b, t):
@@ -266,17 +273,12 @@
             )
             o_s[v, s] = v_s[v, s] + carry * columns[1][cut] - jnp.where(layer_all == 0, pushed[v : v + 1], 0.0)
 
-    last = jnp.concatenate([spots, jnp.ones((8, TILE), f32)], axis=0).astype(jnp.bfloat16)
-    odd = jnp.bitwise_and(lax.axis_index("span"), 1)
-    for to, s in ((inner, (1 - odd) * (rows - 1)), (outer, odd * (rows - 1))):
-        for j in range(total // 2):
-            to[j] = jnp.concatenate([g[2 * j, rows + s], g[2 * j + 1, rows + s]], axis=0).astype(jnp.bfloat16)
+    for to, s in ends:
         for v in range(var_count):
             for n, ref in enumerate((a_r, a_s, o_r, o_s)):
                 held[v, n * layers : (n + 1) * layers, :] = ref[v, s]
             for i in range(own_blocks):
                 to[total // 2 + v * own_blocks + i] = held[v, :, i * TILE : (i + 1) * TILE].astype(jnp.bfloat16)
-        to[total // 2 + var_count * own_blocks] = last
 
 
 def corner_of(tile, row, rows):

time: 24.2 us -> 24.1 us (level)
  no operation moved by 1% of the time
where the time goes in v11:
time: 24.1 us; the launch traced here: 24 us
  waiting for transfers between devices  13.5 us (56%)
  Pallas kernels  5.4 us (22%)
  starting transfers between devices  4.26 us (18%)
  between operations  0.75 us (3%)
    ppermute x3, waiting for transfers between devices, per_device(): other = lax.ppermute(mine, 'circ', [(i, i ^ hop) for i in range(members)])  9.53 us
    ppermute x1, waiting for transfers between devices, per_device(): outer = lax.ppermute(outer, 'span', far)  3.3 us
    ppermute x1, starting transfers between devices, per_device(): outer = lax.ppermute(outer, 'span', far)  2.38 us
    pallas_call x1, Pallas kernels, per_device(): pl.pallas_call(first_kernel, out_shape=(field, field, jax.ShapeDtypeStruc...  1.64 us
    ppermute x1, starting transfers between devices, per_device(): inner = lax.ppermute(inner, 'span', near)  1.56 us
    pallas_call x1, Pallas kernels, per_device(): pl.pallas_call(functools.partial(fourth_kernel, bands), out_shape=(field,...  1.01 us
    pallas_call x1, Pallas kernels, per_device(): pl.pallas_call(functools.partial(second_kernel, masks), out_shape=(field,...  0.98 us
    pallas_call x1, Pallas kernels, per_device(): pl.pallas_call(table_kernel, out_shape=(jax.ShapeDtypeStruct((rows, sprea...  0.94 us
  transfers between devices with their start and end apart: 5, of which 5 were waited for; matrix products, arithmetic and copies ran while one was open for 0% of the time, Pallas kernels for 7%

profile of v11, /device:TPU:28, one launch (start us, length us, event | category | flops | bytes accessed | tf_op | source)
XLA Modules:
  0.0 24.0 jit_solution(10737916315450781362)
XLA Ops:
  0.6 1.6 %local_part.1 = (f32[6,2,4,256]{3,2,1,0:T(4,128)S(1)}, f32[6,2,4,256]{3,2,1,0:T(4,128)S(1)}, bf16[2,64,128]{2,1,0:T(8,128)(2,1)S(1)}, f32[6,2,4,256]{3,2,1,0:T(4...) custom-call(f32[6,2,4,256]{3,2,1,0:T(4,128)} %refs_0_.1, ...), custom_call_target="tpu_custom_call" | custom-call | tf_op jit(solution)/shard_map/local_part/pallas_call | solution.py:484
  2.3 0.1 collective-permute-start
  2.4 0.9 %weight_tables.1 = (f32[2,15,4,128]{3,2,1,0:T(4,128)S(1)}, f32[2,4,8,128]{3,2,1,0:T(8,128)S(1)}) custom-call(f32[2,16,4,128]{3,2,1,0:T(4,128)S(1)} %get-tuple-element.32.weights, s32[2,4,16]{2,1,0:T(4,128)S(1)} %get-tuple-element.33.margin.margin_in, s32[2,16]{1,0:T(2,128)S(1)} %get-tuple-element.34.count), custom_call_target="tpu_custom_call" | custom-call | tf_op jit(solution)/shard_map/weight_tables/pallas_call | solution.py:498
  3.3 4.2 %collective-permute-done = bf16[2,64,128]{2,1,0:T(8,128)(2,1)S(1)} collective-permute-done((bf16[2,64,128]{2,1,0:T(8,128)(2,1)S(1)}, bf16[2,64,128]{2,1,0:T(8,128)(2,1)S(1)}, u32[]{:S(2)}, u32[]{:S(2)}) %collective-permute-start) | collective-permute-done | bytes 32800 | tf_op jit(solution)/shard_map/ppermute | solution.py:514
  7.5 0.1 collective-permute-start.1
  7.6 4.1 %collective-permute-done.1 = bf16[4,64,128]{2,1,0:T(8,128)(2,1)S(1)} collective-permute-done((bf16[4,64,128]{2,1,0:T(8,128)(2,1)S(1)}, bf16[4,64,128]{2,1,0:T(8,128)(2,1)S(1)}, u32[]{:S(2)}, u32[]{:S(2)}) %collective-permute-start.1) | collective-permute-done | bytes 65568 | tf_op jit(solution)/shard_map/ppermute | solution.py:514
  11.7 0.2 collective-permute-start.2
  11.9 1.2 %collective-permute-done.2.other = bf16[8,64,128]{2,1,0:T(8,128)(2,1)S(1)} collective-permute-done((bf16[8,64,128]{2,1,0:T(8,128)(2,1)S(1)}, bf16[8,64,128]{2,1,0:T(8,128)(2,1)S(1)}, u32[]{:S(2)}, u32[]{:S(2)}) %collective-permute-start.2) | collective-permute-done | bytes 131104 | tf_op jit(solution)/shard_map/ppermute | solution.py:514
  13.1 0.0 copy-start
  13.1 0.0 copy-start.1
  13.1 0.0 copy-start.2
  13.1 0.0 copy-start.3
  13.1 0.0 copy-start.4
  13.1 0.0 copy-start.5
  13.2 1.0 %interface_part.1 = (f32[6,2,4,256]{3,2,1,0:T(4,128)S(1)}, f32[6,2,4,256]{3,2,1,0:T(4,128)S(1)}, f32[2,8,256]{2,1,0:T(8,128)S(1)}, f32[2,8,256]{2,1,0:T(8,128)S(...) custom-call(bf16[8,64,128]{2,1,0:T(8,128)(2,1)S(1)} %constant_dynami, ...), custom_call_target="tpu_custom_call" | custom-call | tf_op jit(solution)/shard_map/interface_part/pallas_call | solution.py:526
  14.2 1.6 %collective-permute-start.4 = (bf16[21,16,128]{2,1,0:T(8,128)(2,1)S(1)}, bf16[21,16,128]{2,1,0:T(8,128)(2,1)S(1)}, u32[]{:S(2)}, u32[]{:S(2)}) collective-permute-start(bf16[21,16,128]{2,1,0:T(8,128)(2,1)S(1)} %get-tuple-element.45), channel_id=1, source_target_pairs={{0,1},{1,0},{2,3},{3,2},{4,5},{5,4},{6,7},{7,6},{8,9},{9,8},{10,11... | collective-permute-start | bytes 258056 | tf_op jit(solution)/shard_map/ppermute | solution.py:543
  15.7 2.4 %collective-permute-start.3 = (bf16[21,16,128]{2,1,0:T(8,128)(2,1)S(1)}, bf16[21,16,128]{2,1,0:T(8,128)(2,1)S(1)}, u32[]{:S(2)}, u32[]{:S(2)}) collective-permute-start(bf16[21,16,128]{2,1,0:T(8,128)(2,1)S(1)} %get-tuple-element.44), channel_id=1, source_target_pairs={{1,2},{2,1},{5,6},{6,5},{9,10},{10,9},{13,14},{14,13},{17,18},{18,... | collective-permute-start | bytes 258056 | tf_op jit(solution)/shard_map/ppermute | solution.py:544
  18.1 0.7 %collective-permute-done.4.inner = bf16[21,16,128]{2,1,0:T(8,128)(2,1)S(1)} collective-permute-done((bf16[21,16,128]{2,1,0:T(8,128)(2,1)S(1)}, bf16[21,16,128]{2,1,0:T(8,128)(2,1)S(1)}, u32[]{:S(2)}, u32[]{:S(2)}) %collective-permute-start.4) | collective-permute-done | bytes 86048 | tf_op jit(solution)/shard_map/ppermute | solution.py:543
  18.8 0.0 copy-done
  18.8 0.0 copy-done.1
  18.8 0.0 copy-done.2
  18.8 0.0 copy-done.3
  18.8 0.0 copy-done.4
  18.8 0.0 copy-done.5
  18.8 0.8 %near_part.1 = (f32[6,2,4,256]{3,2,1,0:T(4,128)S(1)}, f32[6,2,4,256]{3,2,1,0:T(4,128)S(1)}, f32[8,128]{1,0:T(8,128)S(1)}, f32[2,11,8,128]{3,2,1,0:T(8,128)S(1)}) custom-call(bf16[21,16,128]{2,1,0:T(8,128)(2,1)S(1)} %collective-permute-done.4.inner, f32[6,2,4,256]{3,2,1,0:T(4,128)S(1)} %get-tuple-element.46.o_r, f32[6,2,4,256]{3,2,1,0:T(4,128)S(1)} %get-tuple-element.47.o_s, ...), custom_call_target="tpu_custom_call" | custom-call | tf_op jit(solution)/shard_map/near_part/pallas_call | solution.py:549
  19.7 3.3 %collective-permute-done.3.outer = bf16[21,16,128]{2,1,0:T(8,128)(2,1)S(1)} collective-permute-done((bf16[21,16,128]{2,1,0:T(8,128)(2,1)S(1)}, bf16[21,16,128]{2,1,0:T(8,128)(2,1)S(1)}, u32[]{:S(2)}, u32[]{:S(2)}) %collective-permute-start.3) | collective-permute-done | bytes 86048 | tf_op jit(solution)/shard_map/ppermute | solution.py:544
  23.0 1.0 %final_part.1 = (f32[6,2,4,256]{3,2,1,0:T(4,128)}, f32[6,2,4,256]{3,2,1,0:T(4,128)}) custom-call(bf16[21,16,128]{2,1,0:T(8,128)(2,1)S(1)} %collective-permute-done.3.outer, f32[6,2,4,256]{3,2,1,0:T(4,128)S(1)} %get-tuple-element.56.part_r, f32[6,2,4,256]{3,2,1,0:T(4,128)S(1)} %get-tuple-element.57.part_s, f32[2,11,8,128]{3,2,1,0:T(8,128)S(1)} %get-tuple-element.50.q, ...), custom_call_target="tpu_custom_call" | custom-call | tf_op jit(solution)/shard_map/final_part/pallas_call | solution.py:561
  (3 shorter events, 0.0 us)
Async XLA Ops:
  2.3 5.2 %collective-permute-start = (bf16[2,64,128]{2,1,0:T(8,128)(2,1)S(1)}, bf16[2,64,128]{2,1,0:T(8,128)(2,1)S(1)}, u32[]{:S(2)}, u32[]{:S(2)}) collective-permute-start(bf16[2,64,128]{2,1,0:T(8,128)(2,1)S(1)} %get-tuple-element.31), channel_id=1, source_target_pairs={{0,20},{4,16},{8,28},{12,24},{16,4},{20,0},{24,12},{28,8},{1,21},{... | collective-permute-start | bytes 98312 | tf_op jit(solution)/shard_map/ppermute | solution.py:514
  7.5 4.2 %collective-permute-start.1 = (bf16[4,64,128]{2,1,0:T(8,128)(2,1)S(1)}, bf16[4,64,128]{2,1,0:T(8,128)(2,1)S(1)}, u32[]{:S(2)}, u32[]{:S(2)}) collective-permute-start(bf16[4,64,128]{2,1,0:T(8,128)(2,1)S(1)} %pad_maximum_fusion), channel_id=1, source_target_pairs={{0,12},{4,8},{8,4},{12,0},{16,28},{20,24},{24,20},{28,16},{1,13},{... | collective-permute-start | bytes 196616 | tf_op jit(solution)/shard_map/ppermute | solution.py:514
  11.7 1.4 %collective-permute-start.2 = (bf16[8,64,128]{2,1,0:T(8,128)(2,1)S(1)}, bf16[8,64,128]{2,1,0:T(8,128)(2,1)S(1)}, u32[]{:S(2)}, u32[]{:S(2)}) collective-permute-start(bf16[8,64,128]{2,1,0:T(8,128)(2,1)S(1)} %constant_dynamic-update-slice_fusion.mine), channel_id=1, source_target_pairs={{0,4},{4,0},{8,12},{12,8},{16,20},{20,16},{24,28},{28,24},{1,5},{5... | collective-permute-start | bytes 393224 | tf_op jit(solution)/shard_map/ppermute | solution.py:514
  13.1 5.7 %copy-start = (bf16[6,6,2,4,256]{4,3,2,1,0:T(4,128)(2,1)S(1)}, bf16[6,6,2,4,256]{4,3,2,1,0:T(4,128)(2,1)}, u32[]{:S(2)}) copy-start(bf16[6,6,2,4,256]{4,3,2,1,0:T(4,128)(2,1)} %jo_r.3) | copy-start | bytes 442372
  13.1 5.7 %copy-start.1 = (bf16[6,6,2,4,256]{4,3,2,1,0:T(4,128)(2,1)S(1)}, bf16[6,6,2,4,256]{4,3,2,1,0:T(4,128)(2,1)}, u32[]{:S(2)}) copy-start(bf16[6,6,2,4,256]{4,3,2,1,0:T(4,128)(2,1)} %jo_s.3) | copy-start | bytes 442372
  13.1 5.7 %copy-start.2 = (f32[6,2,4,256]{3,2,1,0:T(4,128)S(1)}, f32[6,2,4,256]{3,2,1,0:T(4,128)}, u32[]{:S(2)}) copy-start(f32[6,2,4,256]{3,2,1,0:T(4,128)} %jd_r.3) | copy-start | bytes 147460
  13.1 5.7 %copy-start.3 = (f32[6,2,4,256]{3,2,1,0:T(4,128)S(1)}, f32[6,2,4,256]{3,2,1,0:T(4,128)}, u32[]{:S(2)}) copy-start(f32[6,2,4,256]{3,2,1,0:T(4,128)} %jd_s.3) | copy-start | bytes 147460
  13.1 5.7 %copy-start.4 = (f32[6,2,4,256]{3,2,1,0:T(4,128)S(1)}, f32[6,2,4,256]{3,2,1,0:T(4,128)}, u32[]{:S(2)}) copy-start(f32[6,2,4,256]{3,2,1,0:T(4,128)} %src_r.1) | copy-start | bytes 147460
  13.1 5.7 %copy-start.5 = (f32[6,2,4,256]{3,2,1,0:T(4,128)S(1)}, f32[6,2,4,256]{3,2,1,0:T(4,128)}, u32[]{:S(2)}) copy-start(f32[6,2,4,256]{3,2,1,0:T(4,128)} %src_s.1) | copy-start | bytes 147460
  14.2 4.6 %collective-permute-start.4 = (bf16[21,16,128]{2,1,0:T(8,128)(2,1)S(1)}, bf16[21,16,128]{2,1,0:T(8,128)(2,1)S(1)}, u32[]{:S(2)}, u32[]{:S(2)}) collective-permute-start(bf16[21,16,128]{2,1,0:T(8,128)(2,1)S(1)} %get-tuple-element.45), channel_id=1, source_target_pairs={{0,1},{1,0},{2,3},{3,2},{4,5},{5,4},{6,7},{7,6},{8,9},{9,8},{10,11... | collective-permute-start | bytes 258056 | tf_op jit(solution)/shard_map/ppermute | solution.py:543
  15.7 7.3 %collective-permute-start.3 = (bf16[21,16,128]{2,1,0:T(8,128)(2,1)S(1)}, bf16[21,16,128]{2,1,0:T(8,128)(2,1)S(1)}, u32[]{:S(2)}, u32[]{:S(2)}) collective-permute-start(bf16[21,16,128]{2,1,0:T(8,128)(2,1)S(1)} %get-tuple-element.44), channel_id=1, source_target_pairs={{1,2},{2,1},{5,6},{6,5},{9,10},{10,9},{13,14},{14,13},{17,18},{18,... | collective-permute-start | bytes 258056 | tf_op jit(solution)/shard_map/ppermute | solution.py:544
